TPU v7x, 32 devices: a whole 2x2x4 slice. The times are simulated.
32 devices in a mesh: segment: 4 (over y, core), frame: 8 (over z, x).
Axes of the slice: x: 2, y: 2, z: 4, core: 2. Of those that a mesh axis runs over, the one named last changes fastest.
Arguments:
- clips: bfloat16 [4, 8, 320, 1024], P('segment', 'frame'), may hold values from -6 to 6
- timesteps: int32 [4], replicated, may hold values from 0 to 999
- gain: float32 [4, 320], replicated, may hold values from 0.25 to 1.75
- temporal_weight: bfloat16 [4, 3, 320, 320], P('segment'), may hold values from -0.1875 to 0.1875
- film_weight: bfloat16 [4, 320, 320], P('segment'), may hold values from -0.3125 to 0.3125
- out_weight: bfloat16 [4, 320, 320], P('segment'), may hold values from -0.3125 to 0.3125
- skip_weight: bfloat16 [2, 320, 320], replicated, may hold values from -0.3125 to 0.3125
Outputs:
- video_out: bfloat16 [4, 8, 320, 1024], P('segment', 'frame')
All inputs are finite; a program needn't handle non-finite values.
Results may differ from a plain program's by a relative error of at most 0.012.
Values may be sent and summed in bfloat16 or wider, within the bound.
No kernel may reach another device: no remote copies, remote signals or barrier semaphores. Data moves between devices by JAX's collectives and lax.ppermute only.
A program may use at most 64 MiB of HBM per device.

v0:
```python
import math

import jax
import jax.numpy as jnp
from jax import lax
from jax.sharding import PartitionSpec as P


def extended(cells, sides, width):
    for axis, dim in sides:
        count = lax.axis_size(axis)
        ends = count - 1
        head = lax.slice_in_dim(cells, 0, width, axis=dim)
        tail = lax.slice_in_dim(cells, cells.shape[dim] - width, cells.shape[dim], axis=dim)
        cells = jnp.concatenate(
            [
                lax.ppermute(tail, axis, [(i, (i + 1) % count) for i in range(ends)]),
                cells,
                lax.ppermute(head, axis, [((i + 1) % count, i) for i in range(ends)]),
            ],
            axis=dim,
        )
    return cells


def shifted(array, axis, by):
    length = lax.axis_size(axis)
    pairs = [(i, i + by) for i in range(length) if 0 <= i + by < length]
    return lax.ppermute(array, axis, pairs)


def embed(timesteps, width):
    half = width // 2
    freq = jnp.exp(-math.log(10000.0) * jnp.arange(half, dtype=jnp.float32) / half)
    angle = timesteps.astype(jnp.float32)[:, None] * freq[None, :]
    return jnp.concatenate([jnp.sin(angle), jnp.cos(angle)], axis=-1).astype(jnp.bfloat16)


def channel_mix(weight, field):
    return jnp.einsum("io,fip->fop", weight, field, preferred_element_type=jnp.float32)


def temporal_mix(normed, taps):
    padded = extended(normed, (("frame", 0),), 1)
    count = normed.shape[0]
    mixed = channel_mix(taps[0], padded[0:count])
    mixed = mixed + channel_mix(taps[1], padded[1 : count + 1])
    mixed = mixed + channel_mix(taps[2], padded[2 : count + 2])
    return mixed


def section_core(state, own_gain, taps, film_vec, projection):
    values = state.astype(jnp.float32)
    meansq = jnp.mean(values * values, axis=1, keepdims=True)
    normed = (values * lax.rsqrt(meansq + 1e-05) * own_gain[None, :, None]).astype(jnp.bfloat16)
    mixed = temporal_mix(normed, taps)
    hidden = jax.nn.silu(mixed * (1.0 + film_vec[None, :, None])).astype(jnp.bfloat16)
    return values + channel_mix(projection, hidden)


def shards(clips, timesteps, gain, temporal_weight, film_weight, out_weight, skip_weight):
    sections = lax.axis_size("segment")
    section = lax.axis_index("segment")
    emb = embed(timesteps, clips.shape[2])
    all_clips = lax.all_gather(clips, "segment", axis=0, tiled=True)
    batches = all_clips.shape[0]
    film_all = jnp.dot(emb, film_weight[0], preferred_element_type=jnp.float32)
    own_gain = lax.dynamic_index_in_dim(gain, section, 0, keepdims=False)
    taps = temporal_weight[0]
    projection = out_weight[0]
    decoder_weight = jnp.where(section == sections - 1, skip_weight[1], skip_weight[0])
    is_first = section == 0
    is_decoder = section >= 2
    empty = jnp.zeros(all_clips.shape[1:], jnp.bfloat16)
    handed = empty
    carried = empty
    finals = []
    steps_total = batches + sections - 1
    for step in range(steps_total):
        source = all_clips[step] if step < batches else empty
        state = jnp.where(is_first, source, handed)
        micro = step - section
        select = jnp.arange(batches) == micro
        film_vec = jnp.sum(jnp.where(select[:, None], film_all, 0.0), axis=0)
        far_skip = empty
        if step >= 3 and step - 3 < batches:
            far_skip = all_clips[step - 3]
        skip_in = jnp.where(section == sections - 1, far_skip, carried)
        total = section_core(state, own_gain, taps, film_vec, projection)
        skip_term = channel_mix(decoder_weight, skip_in)
        total = total + jnp.where(is_decoder, skip_term, 0.0)
        result = total.astype(jnp.bfloat16)
        if step >= sections - 1:
            finals.append(result)
        if step < steps_total - 1:
            handed, carried = shifted((result, state), "segment", 1)
    stacked = jnp.stack(finals, axis=0).astype(jnp.float32)
    stacked = jnp.where(section == sections - 1, stacked, 0.0)
    return lax.psum_scatter(
        stacked.astype(jnp.bfloat16), "segment", scatter_dimension=0, tiled=True
    )


def solution(mesh):
    placed = (
        P("segment", "frame", None, None),
        P(),
        P(),
        P("segment", None, None, None),
        P("segment", None, None),
        P("segment", None, None),
        P(),
    )
    return jax.shard_map(
        shards,
        mesh=mesh,
        in_specs=placed,
        out_specs=P("segment", "frame", None, None),
        check_vma=False,
    )
```

profile of v0, /device:TPU:17, one launch (start us, length us, event | category | flops | bytes accessed | tf_op | source)
XLA Modules:
  0.0 380.8 jit_solution(8646410057896050401)
XLA Ops:
  10.0 26.0 %all-gather.2.cloned.1.call-done = bf16[4,1,320,1024]{3,2,1,0:T(8,128)(2,1)} async-done(((bf16[1,1,320,1024]{3,2,1,0:T(8,128)(2,1)}), bf16[4,1,320,1024]{3,2,1,0:T(8,128)(2,1)}) %all-gather.2.cloned.1.call-update) | async-done | bytes 2621456 | tf_op jit(solution)/shard_map/all_gather | solution.py:65
  45.9 23.6 %collective-permute-done.1 = bf16[1,320,1024]{2,1,0:T(8,128)(2,1)S(1)} collective-permute-done((bf16[1,320,1024]{2,1,0:T(8,128)(2,1)S(1)}, bf16[1,320,1024]{2,1,0:T(8,128)(2,1)S(1)}, u32[]{:S(2)}, u32[]{:S(2)}) %collective-permute-start.1) | collective-permute-done | bytes 655392 | tf_op jit(solution)/shard_map/ppermute | solution.py:19
  79.8 5.6 %collective-permute-done.2 = bf16[1,320,1024]{2,1,0:T(8,128)(2,1)S(1)} collective-permute-done((bf16[1,320,1024]{2,1,0:T(8,128)(2,1)S(1)}, bf16[1,320,1024]{2,1,0:T(8,128)(2,1)S(1)}, u32[]{:S(2)}, u32[]{:S(2)}) %collective-permute-start.2) | collective-permute-done | bytes 655392 | tf_op jit(solution)/shard_map/ppermute | solution.py:29
  95.7 19.1 %collective-permute-done.4 = bf16[1,320,1024]{2,1,0:T(8,128)(2,1)S(1)} collective-permute-done((bf16[1,320,1024]{2,1,0:T(8,128)(2,1)S(1)}, bf16[1,320,1024]{2,1,0:T(8,128)(2,1)S(1)}, u32[]{:S(2)}, u32[]{:S(2)}) %collective-permute-start.4) | collective-permute-done | bytes 655392 | tf_op jit(solution)/shard_map/ppermute | solution.py:19
  116.4 3.5 fusion.47
  123.7 5.6 %collective-permute-done.6 = bf16[1,320,1024]{2,1,0:T(8,128)(2,1)S(1)} collective-permute-done((bf16[1,320,1024]{2,1,0:T(8,128)(2,1)S(1)}, bf16[1,320,1024]{2,1,0:T(8,128)(2,1)S(1)}, u32[]{:S(2)}, u32[]{:S(2)}) %collective-permute-start.6) | collective-permute-done | bytes 655392 | tf_op jit(solution)/shard_map/ppermute | solution.py:29
  138.5 20.2 %collective-permute-done.8 = bf16[1,320,1024]{2,1,0:T(8,128)(2,1)S(1)} collective-permute-done((bf16[1,320,1024]{2,1,0:T(8,128)(2,1)S(1)}, bf16[1,320,1024]{2,1,0:T(8,128)(2,1)S(1)}, u32[]{:S(2)}, u32[]{:S(2)}) %collective-permute-start.8) | collective-permute-done | bytes 655392 | tf_op jit(solution)/shard_map/ppermute | solution.py:19
  160.3 3.9 %fusion.46 = bf16[1,320,1024]{2,1,0:T(8,128)(2,1)} fusion(f32[1,320,1024]{2,1,0:T(8,128)} %fusion.32, bf16[1,320,1024]{2,1,0:T(8,128)(2,1)S(1)} %get-tuple-element.19, f32[1024,320]{0,1:T(8,128)} %fusion.113, f32[1024,320]{0,1:T(8,128)S(1)} %fusion.115, bf16[1,320,1024]{2,1,0:T(8,128)(2,1)} %collective-permute-done.7, f32[320]{0:T(512)S(1)} %broadcast_add_fusion.4, ...), kind=kOutput, calls=%fused_computation.89 | convolution fusion | flops 423362560 | bytes 6391808 | tf_op jit(solution)/shard_map/io,fip->fop/dot_general | solution.py:40
  168.1 5.9 %collective-permute-done.10 = bf16[1,320,1024]{2,1,0:T(8,128)(2,1)S(1)} collective-permute-done((bf16[1,320,1024]{2,1,0:T(8,128)(2,1)}, bf16[1,320,1024]{2,1,0:T(8,128)(2,1)S(1)}, u32[]{:S(2)}, u32[]{:S(2)}) %collective-permute-start.10) | collective-permute-done | bytes 655392 | tf_op jit(solution)/shard_map/ppermute | solution.py:29
  177.5 3.5 collective-permute-start.11
  185.5 17.6 %collective-permute-done.12 = bf16[1,320,1024]{2,1,0:T(8,128)(2,1)S(1)} collective-permute-done((bf16[1,320,1024]{2,1,0:T(8,128)(2,1)S(1)}, bf16[1,320,1024]{2,1,0:T(8,128)(2,1)S(1)}, u32[]{:S(2)}, u32[]{:S(2)}) %collective-permute-start.12) | collective-permute-done | bytes 655392 | tf_op jit(solution)/shard_map/ppermute | solution.py:19
  204.7 3.5 fusion.45
  212.0 5.6 %collective-permute-done.14 = bf16[1,320,1024]{2,1,0:T(8,128)(2,1)S(1)} collective-permute-done((bf16[1,320,1024]{2,1,0:T(8,128)(2,1)S(1)}, bf16[1,320,1024]{2,1,0:T(8,128)(2,1)S(1)}, u32[]{:S(2)}, u32[]{:S(2)}) %collective-permute-start.14) | collective-permute-done | bytes 655392 | tf_op jit(solution)/shard_map/ppermute | solution.py:29
  220.0 3.4 collective-permute-start.15
  227.9 18.0 %collective-permute-done.16 = bf16[1,320,1024]{2,1,0:T(8,128)(2,1)S(1)} collective-permute-done((bf16[1,320,1024]{2,1,0:T(8,128)(2,1)S(1)}, bf16[1,320,1024]{2,1,0:T(8,128)(2,1)S(1)}, u32[]{:S(2)}, u32[]{:S(2)}) %collective-permute-start.16) | collective-permute-done | bytes 655392 | tf_op jit(solution)/shard_map/ppermute | solution.py:19
  247.5 3.9 %fusion.44 = bf16[1,320,1024]{2,1,0:T(8,128)(2,1)} fusion(f32[1,320,1024]{2,1,0:T(8,128)} %fusion.30, bf16[1,320,1024]{2,1,0:T(8,128)(2,1)S(1)} %get-tuple-element.15, f32[1024,320]{0,1:T(8,128)} %fusion.99, f32[1024,320]{0,1:T(8,128)S(1)} %fusion.101, bf16[1,320,1024]{2,1,0:T(8,128)(2,1)} %collective-permute-done.15, f32[320]{0:T(512)S(1)} %broadcast_add_fusion.2, ...), kind=kOutput, calls=%fused_computation.87 | convolution fusion | flops 423362560 | bytes 6391808 | tf_op jit(solution)/shard_map/io,fip->fop/dot_general | solution.py:40
  255.3 5.9 %collective-permute-done.18 = bf16[1,320,1024]{2,1,0:T(8,128)(2,1)S(1)} collective-permute-done((bf16[1,320,1024]{2,1,0:T(8,128)(2,1)}, bf16[1,320,1024]{2,1,0:T(8,128)(2,1)S(1)}, u32[]{:S(2)}, u32[]{:S(2)}) %collective-permute-start.18) | collective-permute-done | bytes 655392 | tf_op jit(solution)/shard_map/ppermute | solution.py:29
  272.5 16.6 %collective-permute-done.20 = bf16[1,320,1024]{2,1,0:T(8,128)(2,1)S(1)} collective-permute-done((bf16[1,320,1024]{2,1,0:T(8,128)(2,1)S(1)}, bf16[1,320,1024]{2,1,0:T(8,128)(2,1)S(1)}, u32[]{:S(2)}, u32[]{:S(2)}) %collective-permute-start.20) | collective-permute-done | bytes 655392 | tf_op jit(solution)/shard_map/ppermute | solution.py:19
  290.7 3.5 fusion.43
  298.1 5.6 %collective-permute-done.22 = bf16[1,320,1024]{2,1,0:T(8,128)(2,1)S(1)} collective-permute-done((bf16[1,320,1024]{2,1,0:T(8,128)(2,1)S(1)}, bf16[1,320,1024]{2,1,0:T(8,128)(2,1)S(1)}, u32[]{:S(2)}, u32[]{:S(2)}) %collective-permute-start.22) | collective-permute-done | bytes 655392 | tf_op jit(solution)/shard_map/ppermute | solution.py:29
  306.0 3.6 collective-permute-start.23
  313.9 18.0 %collective-permute-done.24 = bf16[1,320,1024]{2,1,0:T(8,128)(2,1)S(1)} collective-permute-done((bf16[1,320,1024]{2,1,0:T(8,128)(2,1)S(1)}, bf16[1,320,1024]{2,1,0:T(8,128)(2,1)S(1)}, u32[]{:S(2)}, u32[]{:S(2)}) %collective-permute-start.24) | collective-permute-done | bytes 655392 | tf_op jit(solution)/shard_map/ppermute | solution.py:19
  333.5 3.9 %fusion.72 = bf16[1,1,320,1024]{3,2,1,0:T(8,128)(2,1)} fusion(f32[1,320,1024]{2,1,0:T(8,128)} %fusion.28, f32[1024,320]{0,1:T(8,128)} %fusion.85, f32[1024,320]{0,1:T(8,128)S(1)} %fusion.87, bf16[1,320,1024]{2,1,0:T(8,128)(2,1)} %collective-permute-done.23, f32[320]{0:T(512)S(1)} %broadcast_add_fusion, ...), kind=kOutput, calls=%fused_computation.123 | convolution fusion | flops 423690240 | bytes 6391809 | tf_op jit(solution)/shard_map/io,fip->fop/dot_general | solution.py:40
  340.5 33.4 %reduce-scatter.2.cloned.1.call-done = bf16[1,1,320,1024]{3,2,1,0:T(8,128)(2,1)} async-done(((bf16[4,1,320,1024]{3,2,1,0:T(8,128)(2,1)}), bf16[1,1,320,1024]{3,2,1,0:T(8,128)(2,1)}) %reduce-scatter.2.cloned.1.call-update) | async-done | bytes 655376 | tf_op jit(solution)/shard_map/reduce_scatter | solution.py:99
  (111 shorter events, 107.7 us)
Async XLA Ops:
  6.5 29.5 %all-gather.2.cloned.1.call-start = ((), (), s32[]{:S(2)}) async-start(), calls=%async_computation.1 | async-start | bytes 3276800 | tf_op jit(solution)/shard_map/all_gather | solution.py:65
  7.3 366.7 %reduce-scatter.2.cloned.1.call-start = ((), (), s32[]{:S(2)}) async-start(), calls=%async_computation.2 | async-start | bytes 3276800 | tf_op jit(solution)/shard_map/reduce_scatter | solution.py:99
  37.5 32.0 %collective-permute-start.1 = (bf16[1,320,1024]{2,1,0:T(8,128)(2,1)S(1)}, bf16[1,320,1024]{2,1,0:T(8,128)(2,1)S(1)}, u32[]{:S(2)}, u32[]{:S(2)}) collective-permute-start(bf16[1,320,1024]{2,1,0:T(8,128)(2,1)S(1)} %fusion.51), channel_id=1, source_target_pairs={{1,0},{2,1},{3,2},{4,3},{5,4},{6,5},{7,6},{9,8},{10,9},{11,10},{12... | collective-permute-start | bytes 1966088 | tf_op jit(solution)/shard_map/ppermute | solution.py:19
  40.8 30.3 %collective-permute-start = (bf16[1,320,1024]{2,1,0:T(8,128)(2,1)S(1)}, bf16[1,320,1024]{2,1,0:T(8,128)(2,1)}, u32[]{:S(2)}, u32[]{:S(2)}) collective-permute-start(bf16[1,320,1024]{2,1,0:T(8,128)(2,1)S(1)} %fusion.51), channel_id=1, source_target_pairs={{0,1},{1,2},{2,3},{3,4},{4,5},{5,6},{6,7},{8,9},{9,10},{10,11},{11... | collective-permute-start | bytes 1966088 | tf_op jit(solution)/shard_map/ppermute | solution.py:17
  74.7 10.7 %collective-permute-start.2 = (bf16[1,320,1024]{2,1,0:T(8,128)(2,1)S(1)}, bf16[1,320,1024]{2,1,0:T(8,128)(2,1)S(1)}, u32[]{:S(2)}, u32[]{:S(2)}) collective-permute-start(bf16[1,320,1024]{2,1,0:T(8,128)(2,1)S(1)} %fusion.48), channel_id=1, source_target_pairs={{0,8},{8,16},{16,24},{1,9},{9,17},{17,25},{2,10},{10,18},{18,26},{... | collective-permute-start | bytes 1966088 | tf_op jit(solution)/shard_map/ppermute | solution.py:29
  77.9 14.5 %collective-permute-start.5 = (bf16[1,320,1024]{2,1,0:T(8,128)(2,1)S(1)}, bf16[1,320,1024]{2,1,0:T(8,128)(2,1)S(1)}, u32[]{:S(2)}, u32[]{:S(2)}) collective-permute-start(bf16[1,320,1024]{2,1,0:T(8,128)(2,1)S(1)} %get-tuple-element.23), channel_id=1, source_target_pairs={{0,8},{8,16},{16,24},{1,9},{9,17},{17,25},{2,10},{10,18},{18,26},{... | collective-permute-start | bytes 1966088 | tf_op jit(solution)/shard_map/ppermute | solution.py:29
  86.9 27.8 %collective-permute-start.4 = (bf16[1,320,1024]{2,1,0:T(8,128)(2,1)S(1)}, bf16[1,320,1024]{2,1,0:T(8,128)(2,1)S(1)}, u32[]{:S(2)}, u32[]{:S(2)}) collective-permute-start(bf16[1,320,1024]{2,1,0:T(8,128)(2,1)S(1)} %fusion.54), channel_id=1, source_target_pairs={{1,0},{2,1},{3,2},{4,3},{5,4},{6,5},{7,6},{9,8},{10,9},{11,10},{12... | collective-permute-start | bytes 1966088 | tf_op jit(solution)/shard_map/ppermute | solution.py:19
  89.4 27.0 %collective-permute-start.3 = (bf16[1,320,1024]{2,1,0:T(8,128)(2,1)S(1)}, bf16[1,320,1024]{2,1,0:T(8,128)(2,1)}, u32[]{:S(2)}, u32[]{:S(2)}) collective-permute-start(bf16[1,320,1024]{2,1,0:T(8,128)(2,1)S(1)} %fusion.54), channel_id=1, source_target_pairs={{0,1},{1,2},{2,3},{3,4},{4,5},{5,6},{6,7},{8,9},{9,10},{10,11},{11... | collective-permute-start | bytes 1966088 | tf_op jit(solution)/shard_map/ppermute | solution.py:17
  121.8 14.5 %collective-permute-start.9 = (bf16[1,320,1024]{2,1,0:T(8,128)(2,1)S(1)}, bf16[1,320,1024]{2,1,0:T(8,128)(2,1)S(1)}, u32[]{:S(2)}, u32[]{:S(2)}) collective-permute-start(bf16[1,320,1024]{2,1,0:T(8,128)(2,1)S(1)} %get-tuple-element.21), channel_id=1, source_target_pairs={{0,8},{8,16},{16,24},{1,9},{9,17},{17,25},{2,10},{10,18},{18,26},{... | collective-permute-start | bytes 1966088 | tf_op jit(solution)/shard_map/ppermute | solution.py:29
  130.9 27.8 %collective-permute-start.8 = (bf16[1,320,1024]{2,1,0:T(8,128)(2,1)S(1)}, bf16[1,320,1024]{2,1,0:T(8,128)(2,1)S(1)}, u32[]{:S(2)}, u32[]{:S(2)}) collective-permute-start(bf16[1,320,1024]{2,1,0:T(8,128)(2,1)S(1)} %fusion.57), channel_id=1, source_target_pairs={{1,0},{2,1},{3,2},{4,3},{5,4},{6,5},{7,6},{9,8},{10,9},{11,10},{12... | collective-permute-start | bytes 1966088 | tf_op jit(solution)/shard_map/ppermute | solution.py:19
  132.9 27.5 %collective-permute-start.7 = (bf16[1,320,1024]{2,1,0:T(8,128)(2,1)S(1)}, bf16[1,320,1024]{2,1,0:T(8,128)(2,1)}, u32[]{:S(2)}, u32[]{:S(2)}) collective-permute-start(bf16[1,320,1024]{2,1,0:T(8,128)(2,1)S(1)} %fusion.57), channel_id=1, source_target_pairs={{0,1},{1,2},{2,3},{3,4},{4,5},{5,6},{6,7},{8,9},{9,10},{10,11},{11... | collective-permute-start | bytes 1966088 | tf_op jit(solution)/shard_map/ppermute | solution.py:17
  164.2 9.7 %collective-permute-start.10 = (bf16[1,320,1024]{2,1,0:T(8,128)(2,1)}, bf16[1,320,1024]{2,1,0:T(8,128)(2,1)S(1)}, u32[]{:S(2)}, u32[]{:S(2)}) collective-permute-start(bf16[1,320,1024]{2,1,0:T(8,128)(2,1)} %fusion.46), channel_id=1, source_target_pairs={{0,8},{8,16},{16,24},{1,9},{9,17},{17,25},{2,10},{10,18},{18,26},{... | collective-permute-start | bytes 1966088 | tf_op jit(solution)/shard_map/ppermute | solution.py:29
  166.2 14.9 %collective-permute-start.13 = (bf16[1,320,1024]{2,1,0:T(8,128)(2,1)S(1)}, bf16[1,320,1024]{2,1,0:T(8,128)(2,1)S(1)}, u32[]{:S(2)}, u32[]{:S(2)}) collective-permute-start(bf16[1,320,1024]{2,1,0:T(8,128)(2,1)S(1)} %get-tuple-element.19), channel_id=1, source_target_pairs={{0,8},{8,16},{16,24},{1,9},{9,17},{17,25},{2,10},{10,18},{18,26},{... | collective-permute-start | bytes 1966088 | tf_op jit(solution)/shard_map/ppermute | solution.py:29
  175.6 27.5 %collective-permute-start.12 = (bf16[1,320,1024]{2,1,0:T(8,128)(2,1)S(1)}, bf16[1,320,1024]{2,1,0:T(8,128)(2,1)S(1)}, u32[]{:S(2)}, u32[]{:S(2)}) collective-permute-start(bf16[1,320,1024]{2,1,0:T(8,128)(2,1)S(1)} %fusion.60), channel_id=1, source_target_pairs={{1,0},{2,1},{3,2},{4,3},{5,4},{6,5},{7,6},{9,8},{10,9},{11,10},{12... | collective-permute-start | bytes 1966088 | tf_op jit(solution)/shard_map/ppermute | solution.py:19
  177.5 27.2 %collective-permute-start.11 = (bf16[1,320,1024]{2,1,0:T(8,128)(2,1)S(1)}, bf16[1,320,1024]{2,1,0:T(8,128)(2,1)}, u32[]{:S(2)}, u32[]{:S(2)}) collective-permute-start(bf16[1,320,1024]{2,1,0:T(8,128)(2,1)S(1)} %fusion.60), channel_id=1, source_target_pairs={{0,1},{1,2},{2,3},{3,4},{4,5},{5,6},{6,7},{8,9},{9,10},{10,11},{11... | collective-permute-start | bytes 1966088 | tf_op jit(solution)/shard_map/ppermute | solution.py:17
  210.1 14.5 %collective-permute-start.17 = (bf16[1,320,1024]{2,1,0:T(8,128)(2,1)S(1)}, bf16[1,320,1024]{2,1,0:T(8,128)(2,1)S(1)}, u32[]{:S(2)}, u32[]{:S(2)}) collective-permute-start(bf16[1,320,1024]{2,1,0:T(8,128)(2,1)S(1)} %get-tuple-element.17), channel_id=1, source_target_pairs={{0,8},{8,16},{16,24},{1,9},{9,17},{17,25},{2,10},{10,18},{18,26},{... | collective-permute-start | bytes 1966088 | tf_op jit(solution)/shard_map/ppermute | solution.py:29
  218.0 27.8 %collective-permute-start.16 = (bf16[1,320,1024]{2,1,0:T(8,128)(2,1)S(1)}, bf16[1,320,1024]{2,1,0:T(8,128)(2,1)S(1)}, u32[]{:S(2)}, u32[]{:S(2)}) collective-permute-start(bf16[1,320,1024]{2,1,0:T(8,128)(2,1)S(1)} %fusion.63), channel_id=1, source_target_pairs={{1,0},{2,1},{3,2},{4,3},{5,4},{6,5},{7,6},{9,8},{10,9},{11,10},{12... | collective-permute-start | bytes 1966088 | tf_op jit(solution)/shard_map/ppermute | solution.py:19
  220.0 27.5 %collective-permute-start.15 = (bf16[1,320,1024]{2,1,0:T(8,128)(2,1)S(1)}, bf16[1,320,1024]{2,1,0:T(8,128)(2,1)}, u32[]{:S(2)}, u32[]{:S(2)}) collective-permute-start(bf16[1,320,1024]{2,1,0:T(8,128)(2,1)S(1)} %fusion.63), channel_id=1, source_target_pairs={{0,1},{1,2},{2,3},{3,4},{4,5},{5,6},{6,7},{8,9},{9,10},{10,11},{11... | collective-permute-start | bytes 1966088 | tf_op jit(solution)/shard_map/ppermute | solution.py:17
  253.3 14.7 %collective-permute-start.21 = (bf16[1,320,1024]{2,1,0:T(8,128)(2,1)S(1)}, bf16[1,320,1024]{2,1,0:T(8,128)(2,1)S(1)}, u32[]{:S(2)}, u32[]{:S(2)}) collective-permute-start(bf16[1,320,1024]{2,1,0:T(8,128)(2,1)S(1)} %get-tuple-element.15), channel_id=1, source_target_pairs={{0,8},{8,16},{16,24},{1,9},{9,17},{17,25},{2,10},{10,18},{18,26},{... | collective-permute-start | bytes 1966088 | tf_op jit(solution)/shard_map/ppermute | solution.py:29
  261.6 27.5 %collective-permute-start.20 = (bf16[1,320,1024]{2,1,0:T(8,128)(2,1)S(1)}, bf16[1,320,1024]{2,1,0:T(8,128)(2,1)S(1)}, u32[]{:S(2)}, u32[]{:S(2)}) collective-permute-start(bf16[1,320,1024]{2,1,0:T(8,128)(2,1)S(1)} %fusion.66), channel_id=1, source_target_pairs={{1,0},{2,1},{3,2},{4,3},{5,4},{6,5},{7,6},{9,8},{10,9},{11,10},{12... | collective-permute-start | bytes 1966088 | tf_op jit(solution)/shard_map/ppermute | solution.py:19
  263.5 27.2 %collective-permute-start.19 = (bf16[1,320,1024]{2,1,0:T(8,128)(2,1)S(1)}, bf16[1,320,1024]{2,1,0:T(8,128)(2,1)}, u32[]{:S(2)}, u32[]{:S(2)}) collective-permute-start(bf16[1,320,1024]{2,1,0:T(8,128)(2,1)S(1)} %fusion.66), channel_id=1, source_target_pairs={{0,1},{1,2},{2,3},{3,4},{4,5},{5,6},{6,7},{8,9},{9,10},{10,11},{11... | collective-permute-start | bytes 1966088 | tf_op jit(solution)/shard_map/ppermute | solution.py:17
  296.1 14.5 %collective-permute-start.25 = (bf16[1,320,1024]{2,1,0:T(8,128)(2,1)S(1)}, bf16[1,320,1024]{2,1,0:T(8,128)(2,1)S(1)}, u32[]{:S(2)}, u32[]{:S(2)}) collective-permute-start(bf16[1,320,1024]{2,1,0:T(8,128)(2,1)S(1)} %get-tuple-element.13), channel_id=1, source_target_pairs={{0,8},{8,16},{16,24},{1,9},{9,17},{17,25},{2,10},{10,18},{18,26},{... | collective-permute-start | bytes 1966088 | tf_op jit(solution)/shard_map/ppermute | solution.py:29
  304.1 27.8 %collective-permute-start.24 = (bf16[1,320,1024]{2,1,0:T(8,128)(2,1)S(1)}, bf16[1,320,1024]{2,1,0:T(8,128)(2,1)S(1)}, u32[]{:S(2)}, u32[]{:S(2)}) collective-permute-start(bf16[1,320,1024]{2,1,0:T(8,128)(2,1)S(1)} %fusion.69), channel_id=1, source_target_pairs={{1,0},{2,1},{3,2},{4,3},{5,4},{6,5},{7,6},{9,8},{10,9},{11,10},{12... | collective-permute-start | bytes 1966088 | tf_op jit(solution)/shard_map/ppermute | solution.py:19
  306.0 27.5 %collective-permute-start.23 = (bf16[1,320,1024]{2,1,0:T(8,128)(2,1)S(1)}, bf16[1,320,1024]{2,1,0:T(8,128)(2,1)}, u32[]{:S(2)}, u32[]{:S(2)}) collective-permute-start(bf16[1,320,1024]{2,1,0:T(8,128)(2,1)S(1)} %fusion.69), channel_id=1, source_target_pairs={{0,1},{1,2},{2,3},{3,4},{4,5},{5,6},{6,7},{8,9},{9,10},{10,11},{11... | collective-permute-start | bytes 1966088 | tf_op jit(solution)/shard_map/ppermute | solution.py:17
  (9 other events, 186.7 us)
Sparse Core Ops, SparseCore 0:
  8.9 27.0 all-gather.1
  340.6 33.2 reduce-scatter.1
where the time goes:
time: 384 us; the launch traced here: 381 us
  waiting for transfers between devices  231 us (60%)
  starting transfers between devices  61.7 us (16%)
  matrix products  60.9 us (16%)
  between operations  14 us (4%)
  other arithmetic  12.4 us (3%)
    ppermute x7, waiting for transfers between devices, extended(): lax.ppermute(head, axis, [((i + 1) % count, i) for i in range(ends)])  133 us
    dot_general x28, matrix products, channel_mix(): jnp.einsum('io,fip->fop', weight, field, preferred_element_type=jnp.float32)  60.7 us
    ppermute x12, waiting for transfers between devices, shifted(): return lax.ppermute(array, axis, pairs)  37.9 us
    reduce_scatter x1, waiting for transfers between devices, shards(): lax.psum_scatter(stacked.astype(jnp.bfloat16), 'segment', scatter_dimensi...  33.4 us
    all_gather x1, waiting for transfers between devices, shards(): all_clips = lax.all_gather(clips, 'segment', axis=0, tiled=True)  26 us
    ppermute x12, starting transfers between devices, shifted(): return lax.ppermute(array, axis, pairs)  24.3 us
    ppermute x7, starting transfers between devices, extended(): lax.ppermute(tail, axis, [(i, (i + 1) % count) for i in range(ends)])  22.2 us
    ppermute x7, starting transfers between devices, extended(): lax.ppermute(head, axis, [((i + 1) % count, i) for i in range(ends)])  15.2 us
  transfers between devices with their start and end apart: 28, of which 20 were waited for; matrix products, arithmetic and copies ran while one was open for 12% of the time, Pallas kernels for 0%

commit v1 on v0

v1 whole, which is shorter than its diff:
```python
import functools
import math

import jax
import jax.numpy as jnp
from jax import lax
from jax.experimental import pallas as pl
from jax.experimental.pallas import tpu as pltpu
from jax.sharding import PartitionSpec as P

BF = jnp.bfloat16
F32 = jnp.float32
LANES = 128
EPS = 1e-05


def embed(timesteps, width):
    half = width // 2
    freq = jnp.exp(-math.log(10000.0) * jnp.arange(half, dtype=jnp.float32) / half)
    angle = timesteps.astype(jnp.float32)[:, None] * freq[None, :]
    return jnp.concatenate([jnp.sin(angle), jnp.cos(angle)], axis=-1).astype(jnp.bfloat16)


def exchange(array, axis, by):
    return lax.ppermute(array, axis, [(i, i ^ by) for i in range(lax.axis_size(axis))])


def plain_section(state, gain, taps, film, projection, extra):
    values = state.astype(F32)
    meansq = jnp.mean(values * values, axis=1, keepdims=True)
    normed = (values * lax.rsqrt(meansq + EPS) * gain[None, :, None]).astype(BF)
    padded = jnp.pad(normed, ((1, 1), (0, 0), (0, 0)))
    count = state.shape[0]
    mixed = sum(
        jnp.einsum("io,fip->fop", taps[tau], padded[tau : tau + count], preferred_element_type=F32)
        for tau in range(3)
    )
    hidden = jax.nn.silu(mixed * (1.0 + film[None, :, None])).astype(BF)
    total = values + jnp.einsum("io,fip->fop", projection, hidden, preferred_element_type=F32)
    if extra is not None:
        total = total + jnp.einsum("io,fip->fop", extra[0], extra[1], preferred_element_type=F32)
    return total.astype(BF)


def plain_shards(clips, timesteps, gain, temporal_weight, film_weight, out_weight, skip_weight):
    own = clips[0]
    pixels = own.shape[2]
    split = lax.axis_size("frame")
    pad = -pixels % split
    if pad:
        own = jnp.pad(own, ((0, 0), (0, 0), (0, pad)))
    state = lax.all_to_all(own, "frame", 2, 0, tiled=True)
    emb = embed(timesteps, clips.shape[2])
    film = jnp.dot(emb, film_weight[0], preferred_element_type=F32)
    taps = lax.all_gather(temporal_weight[0], "segment")
    projection = lax.all_gather(out_weight[0], "segment")
    films = lax.all_gather(film, "segment")
    micro = lax.axis_index("segment")
    first = state
    skips = {}
    for section in range(gain.shape[0]):
        extra = None
        if section == 2:
            extra = (skip_weight[0], skips[0])
        if section == 3:
            extra = (skip_weight[1], first)
        film_vec = lax.dynamic_index_in_dim(films[section], micro, 0, keepdims=False)
        state = plain_section(
            state, gain[section], taps[section], film_vec, projection[section], extra
        )
        skips[section] = state
    result = lax.all_to_all(state, "frame", 0, 2, tiled=True)
    return result[None, :, :, :pixels]


def transposed_dot(weight, field):
    return lax.dot_general(weight, field, (((0,), (0,)), ((), ())), preferred_element_type=F32)


def sections_kernel(frames, width, *refs):
    blocks = refs[0:frames]
    taps_in = refs[frames : frames + 4]
    rest_in = refs[frames + 4 : frames + 8]
    skip_in, gain_ref = refs[frames + 8 : frames + 10]
    outs = refs[frames + 10 : 2 * frames + 10]
    first, taps, rest, skip, unfolded, one, work, last, sem_x, sem_w, sem_s, sem_o = refs[
        2 * frames + 10 :
    ]
    me = lax.axis_index("frame")
    segment = lax.axis_index("segment")
    columns = frames * LANES

    loads = [
        pltpu.make_async_copy(blocks[d], first.at[me ^ d], sem_x.at[d]) for d in range(frames)
    ]
    for load in loads:
        load.start()
    for b in range(4):
        to = segment ^ b
        pltpu.make_async_copy(taps_in[b], taps.at[to], sem_w.at[to, 0]).start()
        pltpu.make_async_copy(rest_in[b], rest.at[to], sem_w.at[to, 1]).start()
    skip_load = pltpu.make_async_copy(skip_in, skip, sem_s)
    skip_load.start()

    zeros = jnp.zeros((width, LANES), BF)
    for half in range(2):
        unfolded[half, 0:width, 0:LANES] = zeros
        unfolded[half, 2 * width :, columns - LANES :] = zeros
    chosen = lax.broadcasted_iota(jnp.int32, (16, LANES), 0)
    chosen = jnp.where((chosen == segment) | (chosen == segment + 4), 1.0, 0.0).astype(BF)
    for load in loads:
        load.wait()

    def at(ref, f):
        return ref[f] if ref is first else ref[:, f * LANES : (f + 1) * LANES]

    def pair(ref, j):
        return jnp.concatenate([at(ref, 2 * j), at(ref, 2 * j + 1)], axis=1)

    for s in range(4):
        source = (first, one, work, work)[s]
        target = (one, work, work, last)[s]
        half = s % 2
        for f in range(frames):
            values = at(source, f).astype(F32)
            scale = lax.rsqrt(jnp.mean(values * values, axis=0, keepdims=True) + EPS)
            normed = (values * scale * gain_ref[:, s : s + 1]).astype(BF)
            for tau in range(3):
                to = f + 1 - tau
                if 0 <= to < frames:
                    unfolded[
                        half, tau * width : (tau + 1) * width, to * LANES : (to + 1) * LANES
                    ] = normed
        pltpu.make_async_copy(taps_in[0], taps.at[s], sem_w.at[s, 0]).wait()
        pltpu.make_async_copy(rest_in[0], rest.at[s], sem_w.at[s, 1]).wait()
        film = 1.0 + transposed_dot(rest[s, width : width + 16], chosen)
        film = jnp.concatenate([film, film], axis=1)
        if s == 2:
            skip_load.wait()
        for j in range(frames // 2):
            cols = slice(2 * j * LANES, 2 * (j + 1) * LANES)
            mixed = transposed_dot(taps[s], unfolded[half, :, cols]) * film
            hidden = (mixed * (0.5 + 0.5 * jnp.tanh(0.5 * mixed))).astype(BF)
            total = pair(source, j).astype(F32) + transposed_dot(rest[s, 0:width], hidden)
            if s >= 2:
                total = total + transposed_dot(skip[s - 2], pair(one if s == 2 else first, j))
            total = total.astype(BF)
            if s == 3:
                last[2 * j] = total[:, :LANES]
                last[2 * j + 1] = total[:, LANES:]
            else:
                target[:, cols] = total
    stores = [pltpu.make_async_copy(last.at[me ^ d], outs[d], sem_o.at[d]) for d in range(frames)]
    for store in stores:
        store.start()
    for store in stores:
        store.wait()


def run_sections(blocks, taps, rest, skip, gain):
    frames = len(blocks)
    width = gain.shape[0]
    columns = frames * LANES
    anywhere = pl.BlockSpec(memory_space=pl.ANY)
    return pl.pallas_call(
        functools.partial(sections_kernel, frames, width),
        out_shape=[jax.ShapeDtypeStruct((width, LANES), BF)] * frames,
        in_specs=[anywhere] * (frames + 9) + [pl.BlockSpec(memory_space=pltpu.VMEM)],
        out_specs=[anywhere] * frames,
        scratch_shapes=[
            pltpu.VMEM((frames, width, LANES), BF),
            pltpu.VMEM((4, 3 * width, width), BF),
            pltpu.VMEM((4, width + 16, width), BF),
            pltpu.VMEM((2, width, width), BF),
            pltpu.VMEM((2, 3 * width, columns), BF),
            pltpu.VMEM((width, columns), BF),
            pltpu.VMEM((width, columns), BF),
            pltpu.VMEM((frames, width, LANES), BF),
            pltpu.SemaphoreType.DMA((frames,)),
            pltpu.SemaphoreType.DMA((4, 2)),
            pltpu.SemaphoreType.DMA,
            pltpu.SemaphoreType.DMA((frames,)),
        ],
        compiler_params=pltpu.CompilerParams(vmem_limit_bytes=40 << 20),
        name="sections",
    )(*blocks, *taps, *rest, skip, gain)


def join_kernel(frames, *refs):
    blocks, out, sems = refs[:frames], refs[frames], refs[frames + 1]
    me = lax.axis_index("frame")
    copies = []
    for d in range(frames):
        lane = pl.multiple_of((me ^ d) * LANES, LANES)
        copies.append(pltpu.make_async_copy(blocks[d], out.at[:, pl.ds(lane, LANES)], sems.at[d]))
    for copy in copies:
        copy.start()
    for copy in copies:
        copy.wait()


def join_blocks(blocks):
    frames = len(blocks)
    width = blocks[0].shape[0]
    return pl.pallas_call(
        functools.partial(join_kernel, frames),
        out_shape=jax.ShapeDtypeStruct((width, frames * LANES), BF),
        in_specs=[pl.BlockSpec(memory_space=pl.ANY)] * frames,
        out_specs=pl.BlockSpec(memory_space=pl.ANY),
        scratch_shapes=[pltpu.SemaphoreType.DMA((frames,))],
        name="join",
    )(*blocks)


def block_shards(clips, timesteps, gain, temporal_weight, film_weight, out_weight, skip_weight):
    frames = lax.axis_size("frame")
    width = clips.shape[2]
    own = clips[0, 0]
    me = lax.axis_index("frame")
    order = [6, 7, 4, 5, 2, 3, 1]

    taps0 = temporal_weight[0].reshape(3 * width, width)
    taps2 = exchange(taps0, "segment", 2)
    cut = [lax.dynamic_slice_in_dim(own, (me ^ d) * LANES, LANES, 1) for d in range(frames)]
    cut = lax.optimization_barrier(tuple(cut))
    got = {0: cut[0]}
    for d in order:
        got[d] = exchange(cut[d], "frame", d)

    film = jnp.dot(embed(timesteps, width), film_weight[0], preferred_element_type=F32)
    high = film.astype(BF)
    low = (film - high.astype(F32)).astype(BF)
    rest0 = jnp.concatenate([out_weight[0], high, low, jnp.zeros((8, width), BF)], axis=0)
    rest2 = exchange(rest0, "segment", 2)
    taps1 = exchange(taps0, "segment", 1)
    rest1 = exchange(rest0, "segment", 1)
    taps3 = exchange(taps2, "segment", 1)
    rest3 = exchange(rest2, "segment", 1)

    outs = run_sections(
        [got[d] for d in range(frames)],
        [taps0, taps1, taps2, taps3],
        [rest0, rest1, rest2, rest3],
        skip_weight,
        gain.T,
    )
    back = {0: outs[0]}
    for d in order:
        back[d] = exchange(outs[d], "frame", d)
    return join_blocks([back[d] for d in range(frames)])[None, None]


def solution(mesh):
    placed = (
        P("segment", "frame", None, None),
        P(),
        P(),
        P("segment", None, None, None),
        P("segment", None, None),
        P("segment", None, None),
        P(),
    )

    def run(*arrays):
        clips, gain = arrays[0], arrays[2]
        split = mesh.shape["frame"]
        fits = (
            clips.shape[1] == split
            and split & (split - 1) == 0
            and split == 8
            and clips.shape[3] == split * LANES
            and clips.shape[2] % 64 == 0
            and clips.shape[0] == gain.shape[0] == mesh.shape["segment"] == 4
        )
        return jax.shard_map(
            block_shards if fits else plain_shards,
            mesh=mesh,
            in_specs=placed,
            out_specs=P("segment", "frame", None, None),
            check_vma=False,
        )(*arrays)

    return run
```

time: 384 us -> 114 us (0.30)
  the two profiles are of different devices: /device:TPU:17 before, /device:TPU:0 now
where the time goes in v1:
time: 114 us; the launch traced here: 113 us
  Pallas kernels  35.6 us (31%)
  starting transfers between devices  32.1 us (28%)
  waiting for transfers between devices  30.6 us (27%)
  local copies, waits for them, and re-layouts  13.5 us (12%)
  other arithmetic  1.2 us (1%)
    ppermute x20, starting transfers between devices, exchange(): lax.ppermute(array, axis, [(i, i ^ by) for i in range(lax.axis_size(axis))])  32.1 us
    ppermute x20, waiting for transfers between devices, exchange(): lax.ppermute(array, axis, [(i, i ^ by) for i in range(lax.axis_size(axis))])  30.6 us
    pallas_call x1, Pallas kernels, join_blocks(): pl.pallas_call(functools.partial(join_kernel, frames), out_shape=jax.Shap...  21 us
    pallas_call x1, Pallas kernels, run_sections(): pl.pallas_call(functools.partial(sections_kernel, frames, width), out_sha...  14.6 us
    unnamed x47, local copies, waits for them, and re-layouts  8.84 us
  transfers between devices with their start and end apart: 20, of which 8 were waited for; matrix products, arithmetic and copies ran while one was open for 5% of the time, Pallas kernels for 0%

profile of v1, /device:TPU:0, one launch (start us, length us, event | category | flops | bytes accessed | tf_op | source)
XLA Modules:
  0.0 113.4 jit_solution(7545664683910524992)
XLA Ops:
  0.0 1.4 %copy.9 = bf16[960,320]{0,1:T(8,128)(2,1)S(1)} copy(bf16[960,320]{1,0:T(8,128)(2,1)} %bitcast.25) | data formatting | bytes 1228800 | tf_op jit(solution)/shard_map/reshape;squeeze | solution.py:222
  1.4 3.0 %collective-permute-start.8 = (bf16[960,320]{0,1:T(8,128)(2,1)S(1)}, bf16[960,320]{0,1:T(8,128)(2,1)S(1)}, u32[]{:S(2)}, u32[]{:S(2)}) collective-permute-start(bf16[960,320]{0,1:T(8,128)(2,1)S(1)} %copy.9), channel_id=1, source_target_pairs={{0,16},{8,24},{16,0},{24,8},{1,17},{9,25},{17,1},{25,9},{2,18},{10... | collective-permute-start | bytes 1843208 | tf_op jit(solution)/shard_map/ppermute | solution.py:25
  4.6 14.6 %collective-permute-done.8 = bf16[960,320]{0,1:T(8,128)(2,1)S(1)} collective-permute-done((bf16[960,320]{0,1:T(8,128)(2,1)S(1)}, bf16[960,320]{0,1:T(8,128)(2,1)S(1)}, u32[]{:S(2)}, u32[]{:S(2)}) %collective-permute-start.8) | collective-permute-done | bytes 614432 | tf_op jit(solution)/shard_map/ppermute | solution.py:25
  20.6 1.8 %collective-permute-start.11 = (bf16[336,320]{1,0:T(8,128)(2,1)S(1)}, bf16[336,320]{1,0:T(8,128)(2,1)}, u32[]{:S(2)}, u32[]{:S(2)}) collective-permute-start(bf16[336,320]{1,0:T(8,128)(2,1)S(1)} %maximum_maximum_fusion.refs_12_), channel_id=1, source_target_pairs={{0,16},{8,24},{16,0},{24,8},{1,17},{9,25},{17,1},{25,9},{2,18},{10... | collective-permute-start | bytes 645128 | tf_op jit(solution)/shard_map/ppermute | solution.py:25
  23.2 1.5 %collective-permute-start = (bf16[320,128]{1,0:T(8,128)(2,1)S(1)}, bf16[320,128]{1,0:T(8,128)(2,1)S(1)}, u32[]{:S(2)}, u32[]{:S(2)}) collective-permute-start(bf16[320,128]{1,0:T(8,128)(2,1)S(1)} %get-tuple-element.22), channel_id=1, source_target_pairs={{0,1},{1,0},{2,3},{3,2},{4,5},{5,4},{6,7},{7,6},{8,9},{9,8},{10,11... | collective-permute-start | bytes 245768 | tf_op jit(solution)/shard_map/ppermute | solution.py:25
  24.7 1.6 %collective-permute-start.1 = (bf16[320,128]{1,0:T(8,128)(2,1)S(1)}, bf16[320,128]{1,0:T(8,128)(2,1)S(1)}, u32[]{:S(2)}, u32[]{:S(2)}) collective-permute-start(bf16[320,128]{1,0:T(8,128)(2,1)S(1)} %get-tuple-element.23), channel_id=1, source_target_pairs={{0,2},{1,3},{2,0},{3,1},{4,6},{5,7},{6,4},{7,5},{8,10},{9,11},{10,... | collective-permute-start | bytes 245768 | tf_op jit(solution)/shard_map/ppermute | solution.py:25
  26.3 1.5 %collective-permute-done.refs_1_ = bf16[320,128]{1,0:T(8,128)(2,1)S(1)} collective-permute-done((bf16[320,128]{1,0:T(8,128)(2,1)S(1)}, bf16[320,128]{1,0:T(8,128)(2,1)S(1)}, u32[]{:S(2)}, u32[]{:S(2)}) %collective-permute-start) | collective-permute-done | bytes 81952 | tf_op jit(solution)/shard_map/ppermute | solution.py:25
  27.8 2.5 %collective-permute-start.2 = (bf16[320,128]{1,0:T(8,128)(2,1)S(1)}, bf16[320,128]{1,0:T(8,128)(2,1)S(1)}, u32[]{:S(2)}, u32[]{:S(2)}) collective-permute-start(bf16[320,128]{1,0:T(8,128)(2,1)S(1)} %get-tuple-element.24), channel_id=1, source_target_pairs={{0,3},{1,2},{2,1},{3,0},{4,7},{5,6},{6,5},{7,4},{8,11},{9,10},{10,... | collective-permute-start | bytes 245768 | tf_op jit(solution)/shard_map/ppermute | solution.py:25
  30.8 2.3 %collective-permute-done.2.refs_3_ = bf16[320,128]{1,0:T(8,128)(2,1)S(1)} collective-permute-done((bf16[320,128]{1,0:T(8,128)(2,1)S(1)}, bf16[320,128]{1,0:T(8,128)(2,1)S(1)}, u32[]{:S(2)}, u32[]{:S(2)}) %collective-permute-start.2) | collective-permute-done | bytes 81952 | tf_op jit(solution)/shard_map/ppermute | solution.py:25
  33.8 2.6 %collective-permute-start.3 = (bf16[320,128]{1,0:T(8,128)(2,1)S(1)}, bf16[320,128]{1,0:T(8,128)(2,1)S(1)}, u32[]{:S(2)}, u32[]{:S(2)}) collective-permute-start(bf16[320,128]{1,0:T(8,128)(2,1)S(1)} %get-tuple-element.25), channel_id=1, source_target_pairs={{0,4},{1,5},{2,6},{3,7},{4,0},{5,1},{6,2},{7,3},{8,12},{9,13},{10,... | collective-permute-start | bytes 245768 | tf_op jit(solution)/shard_map/ppermute | solution.py:25
  36.4 2.8 %collective-permute-done.3.refs_4_ = bf16[320,128]{1,0:T(8,128)(2,1)S(1)} collective-permute-done((bf16[320,128]{1,0:T(8,128)(2,1)S(1)}, bf16[320,128]{1,0:T(8,128)(2,1)S(1)}, u32[]{:S(2)}, u32[]{:S(2)}) %collective-permute-start.3) | collective-permute-done | bytes 81952 | tf_op jit(solution)/shard_map/ppermute | solution.py:25
  39.7 3.6 %collective-permute-start.4 = (bf16[320,128]{1,0:T(8,128)(2,1)}, bf16[320,128]{1,0:T(8,128)(2,1)}, u32[]{:S(2)}, u32[]{:S(2)}) collective-permute-start(bf16[320,128]{1,0:T(8,128)(2,1)} %get-tuple-element.26), channel_id=1, source_target_pairs={{0,5},{1,4},{2,7},{3,6},{4,1},{5,0},{6,3},{7,2},{8,13},{9,12},{10,... | collective-permute-start | bytes 245768 | tf_op jit(solution)/shard_map/ppermute | solution.py:25
  43.3 1.3 %collective-permute-start.5 = (bf16[320,128]{1,0:T(8,128)(2,1)}, bf16[320,128]{1,0:T(8,128)(2,1)}, u32[]{:S(2)}, u32[]{:S(2)}) collective-permute-start(bf16[320,128]{1,0:T(8,128)(2,1)} %get-tuple-element.27), channel_id=1, source_target_pairs={{0,6},{1,7},{2,4},{3,5},{4,2},{5,3},{6,0},{7,1},{8,14},{9,15},{10,... | collective-permute-start | bytes 245768 | tf_op jit(solution)/shard_map/ppermute | solution.py:25
  44.6 2.5 %collective-permute-start.6 = (bf16[320,128]{1,0:T(8,128)(2,1)}, bf16[320,128]{1,0:T(8,128)(2,1)}, u32[]{:S(2)}, u32[]{:S(2)}) collective-permute-start(bf16[320,128]{1,0:T(8,128)(2,1)} %get-tuple-element.28), channel_id=1, source_target_pairs={{0,7},{1,6},{2,5},{3,4},{4,3},{5,2},{6,1},{7,0},{8,15},{9,14},{10,... | collective-permute-start | bytes 245768 | tf_op jit(solution)/shard_map/ppermute | solution.py:25
  48.7 1.5 %copy.14.refs_11_ = bf16[960,320]{1,0:T(8,128)(2,1)S(1)} copy(bf16[960,320]{0,1:T(8,128)(2,1)} %collective-permute-done.9) | data formatting | bytes 1228800 | tf_op jit(solution)/shard_map/ppermute | solution.py:25
  50.3 1.9 %collective-permute-done.6.refs_7_ = bf16[320,128]{1,0:T(8,128)(2,1)} collective-permute-done((bf16[320,128]{1,0:T(8,128)(2,1)}, bf16[320,128]{1,0:T(8,128)(2,1)}, u32[]{:S(2)}, u32[]{:S(2)}) %collective-permute-start.6) | collective-permute-done | bytes 81952 | tf_op jit(solution)/shard_map/ppermute | solution.py:25
  57.7 14.6 %sections.1 = (bf16[320,128]{1,0:T(8,128)(2,1)S(1)}, bf16[320,128]{1,0:T(8,128)(2,1)S(1)}, bf16[320,128]{1,0:T(8,128)(2,1)S(1)}, bf16[320,128]{1,0:T(8,128)(2,1)...) custom-call(bf16[320,128]{1,0:T(8,128)(2,1)S(1)} %get-tuple-element., ...), custom_call_target="tpu_custom_call" | custom-call | tf_op jit(solution)/shard_map/sections/pallas_call | solution.py:165
  73.9 2.5 %collective-permute-start.14 = (bf16[320,128]{1,0:T(8,128)(2,1)S(1)}, bf16[320,128]{1,0:T(8,128)(2,1)S(1)}, u32[]{:S(2)}, u32[]{:S(2)}) collective-permute-start(bf16[320,128]{1,0:T(8,128)(2,1)S(1)} %get-tuple-element.31), channel_id=1, source_target_pairs={{0,2},{1,3},{2,0},{3,1},{4,6},{5,7},{6,4},{7,5},{8,10},{9,11},{10,... | collective-permute-start | bytes 245768 | tf_op jit(solution)/shard_map/ppermute | solution.py:25
  76.4 2.7 %collective-permute-start.16 = (bf16[320,128]{1,0:T(8,128)(2,1)S(1)}, bf16[320,128]{1,0:T(8,128)(2,1)S(1)}, u32[]{:S(2)}, u32[]{:S(2)}) collective-permute-start(bf16[320,128]{1,0:T(8,128)(2,1)S(1)} %get-tuple-element.33), channel_id=1, source_target_pairs={{0,4},{1,5},{2,6},{3,7},{4,0},{5,1},{6,2},{7,3},{8,12},{9,13},{10,... | collective-permute-start | bytes 245768 | tf_op jit(solution)/shard_map/ppermute | solution.py:25
  80.2 2.1 %collective-permute-start.18 = (bf16[320,128]{1,0:T(8,128)(2,1)S(1)}, bf16[320,128]{1,0:T(8,128)(2,1)S(1)}, u32[]{:S(2)}, u32[]{:S(2)}) collective-permute-start(bf16[320,128]{1,0:T(8,128)(2,1)S(1)} %get-tuple-element.35), channel_id=1, source_target_pairs={{0,6},{1,7},{2,4},{3,5},{4,2},{5,3},{6,0},{7,1},{8,14},{9,15},{10,... | collective-permute-start | bytes 245768 | tf_op jit(solution)/shard_map/ppermute | solution.py:25
  82.4 1.7 %collective-permute-start.19 = (bf16[320,128]{1,0:T(8,128)(2,1)S(1)}, bf16[320,128]{1,0:T(8,128)(2,1)S(1)}, u32[]{:S(2)}, u32[]{:S(2)}) collective-permute-start(bf16[320,128]{1,0:T(8,128)(2,1)S(1)} %get-tuple-element.36), channel_id=1, source_target_pairs={{0,7},{1,6},{2,5},{3,4},{4,3},{5,2},{6,1},{7,0},{8,15},{9,14},{10,... | collective-permute-start | bytes 245768 | tf_op jit(solution)/shard_map/ppermute | solution.py:25
  84.1 3.5 %collective-permute-done.16.refs_4_ = bf16[320,128]{1,0:T(8,128)(2,1)S(1)} collective-permute-done((bf16[320,128]{1,0:T(8,128)(2,1)S(1)}, bf16[320,128]{1,0:T(8,128)(2,1)S(1)}, u32[]{:S(2)}, u32[]{:S(2)}) %collective-permute-start.16) | collective-permute-done | bytes 81952 | tf_op jit(solution)/shard_map/ppermute | solution.py:25
  87.6 4.0 %collective-permute-done.17.refs_5_ = bf16[320,128]{1,0:T(8,128)(2,1)S(1)} collective-permute-done((bf16[320,128]{1,0:T(8,128)(2,1)S(1)}, bf16[320,128]{1,0:T(8,128)(2,1)S(1)}, u32[]{:S(2)}, u32[]{:S(2)}) %collective-permute-start.17) | collective-permute-done | bytes 81952 | tf_op jit(solution)/shard_map/ppermute | solution.py:25
  92.3 21.0 %join.1 = bf16[320,1024]{1,0:T(8,128)(2,1)} custom-call(bf16[320,128]{1,0:T(8,128)(2,1)} %copy-done.4, bf16[320,128]{1,0:T(8,128)(2,1)} %copy-done.14, bf16[320,128]{1,0:T(8,128)(2,1)} %copy-done.15, bf16[320,128]{1,0:T(8,128)(2,1)} %copy-done.16, bf16[320,128]{1,0:T(8,128)(2,1)} %copy-done.17, bf16[320,128]{1,0:T(8,128)(2,1)} %copy-done.18, ...), custom_call_target="tpu_custom_call" | custom-call | tf_op jit(solution)/shard_map/join/pallas_call | solution.py:205
  (77 shorter events, 14.6 us)
Async XLA Ops:
  0.0 19.2 %copy-start = (bf16[1,320,320]{2,1,0:T(8,128)(2,1)S(1)}, bf16[1,320,320]{2,1,0:T(8,128)(2,1)}, u32[]{:S(2)}) copy-start(bf16[1,320,320]{2,1,0:T(8,128)(2,1)} %param.11) | copy-start | bytes 614404
  1.4 21.0 %copy-start.13 = (bf16[1,1,320,1024]{3,2,1,0:T(8,128)(2,1)S(1)}, bf16[1,1,320,1024]{3,2,1,0:T(8,128)(2,1)}, u32[]{:S(2)}) copy-start(bf16[1,1,320,1024]{3,2,1,0:T(8,128)(2,1)} %param.7) | copy-start | bytes 1966084
  1.4 17.8 %collective-permute-start.8 = (bf16[960,320]{0,1:T(8,128)(2,1)S(1)}, bf16[960,320]{0,1:T(8,128)(2,1)S(1)}, u32[]{:S(2)}, u32[]{:S(2)}) collective-permute-start(bf16[960,320]{0,1:T(8,128)(2,1)S(1)} %copy.9), channel_id=1, source_target_pairs={{0,16},{8,24},{16,0},{24,8},{1,17},{9,25},{17,1},{25,9},{2,18},{10... | collective-permute-start | bytes 1843208 | tf_op jit(solution)/shard_map/ppermute | solution.py:25
  4.5 38.9 %collective-permute-start.7 = (bf16[960,320]{0,1:T(8,128)(2,1)S(1)}, bf16[960,320]{0,1:T(8,128)(2,1)S(1)}, u32[]{:S(2)}, u32[]{:S(2)}) collective-permute-start(bf16[960,320]{0,1:T(8,128)(2,1)S(1)} %copy.9), channel_id=1, source_target_pairs={{0,8},{8,0},{16,24},{24,16},{1,9},{9,1},{17,25},{25,17},{2,10},{10... | collective-permute-start | bytes 1843208 | tf_op jit(solution)/shard_map/ppermute | solution.py:25
  19.2 25.4 %collective-permute-start.9 = (bf16[960,320]{0,1:T(8,128)(2,1)S(1)}, bf16[960,320]{0,1:T(8,128)(2,1)}, u32[]{:S(2)}, u32[]{:S(2)}) collective-permute-start(bf16[960,320]{0,1:T(8,128)(2,1)S(1)} %collective-permute-done.8), channel_id=1, source_target_pairs={{0,8},{8,0},{16,24},{24,16},{1,9},{9,1},{17,25},{25,17},{2,10},{10... | collective-permute-start | bytes 1843208 | tf_op jit(solution)/shard_map/ppermute | solution.py:25
  20.6 9.7 %collective-permute-start.11 = (bf16[336,320]{1,0:T(8,128)(2,1)S(1)}, bf16[336,320]{1,0:T(8,128)(2,1)}, u32[]{:S(2)}, u32[]{:S(2)}) collective-permute-start(bf16[336,320]{1,0:T(8,128)(2,1)S(1)} %maximum_maximum_fusion.refs_12_), channel_id=1, source_target_pairs={{0,16},{8,24},{16,0},{24,8},{1,17},{9,25},{17,1},{25,9},{2,18},{10... | collective-permute-start | bytes 645128 | tf_op jit(solution)/shard_map/ppermute | solution.py:25
  23.2 23.9 %copy-start.21 = (f32[4,320]{1,0:T(4,128)S(1)}, f32[4,320]{1,0:T(4,128)}, u32[]{:S(2)}) copy-start(f32[4,320]{1,0:T(4,128)} %param.9) | copy-start | bytes 15364
  23.2 4.6 %collective-permute-start = (bf16[320,128]{1,0:T(8,128)(2,1)S(1)}, bf16[320,128]{1,0:T(8,128)(2,1)S(1)}, u32[]{:S(2)}, u32[]{:S(2)}) collective-permute-start(bf16[320,128]{1,0:T(8,128)(2,1)S(1)} %get-tuple-element.22), channel_id=1, source_target_pairs={{0,1},{1,0},{2,3},{3,2},{4,5},{5,4},{6,7},{7,6},{8,9},{9,8},{10,11... | collective-permute-start | bytes 245768 | tf_op jit(solution)/shard_map/ppermute | solution.py:25
  24.7 5.6 %collective-permute-start.1 = (bf16[320,128]{1,0:T(8,128)(2,1)S(1)}, bf16[320,128]{1,0:T(8,128)(2,1)S(1)}, u32[]{:S(2)}, u32[]{:S(2)}) collective-permute-start(bf16[320,128]{1,0:T(8,128)(2,1)S(1)} %get-tuple-element.23), channel_id=1, source_target_pairs={{0,2},{1,3},{2,0},{3,1},{4,6},{5,7},{6,4},{7,5},{8,10},{9,11},{10,... | collective-permute-start | bytes 245768 | tf_op jit(solution)/shard_map/ppermute | solution.py:25
  27.8 20.1 %copy-start.5 = (bf16[320,128]{1,0:T(8,128)(2,1)}, bf16[320,128]{1,0:T(8,128)(2,1)S(1)}, u32[]{:S(2)}) copy-start(bf16[320,128]{1,0:T(8,128)(2,1)S(1)} %collective-permute-done.refs_1_) | copy-start | bytes 245764
  27.8 5.3 %collective-permute-start.2 = (bf16[320,128]{1,0:T(8,128)(2,1)S(1)}, bf16[320,128]{1,0:T(8,128)(2,1)S(1)}, u32[]{:S(2)}, u32[]{:S(2)}) collective-permute-start(bf16[320,128]{1,0:T(8,128)(2,1)S(1)} %get-tuple-element.24), channel_id=1, source_target_pairs={{0,3},{1,2},{2,1},{3,0},{4,7},{5,6},{6,5},{7,4},{8,11},{9,10},{10,... | collective-permute-start | bytes 245768 | tf_op jit(solution)/shard_map/ppermute | solution.py:25
  30.3 21.8 %collective-permute-start.10 = (bf16[336,320]{1,0:T(8,128)(2,1)S(1)}, bf16[336,320]{1,0:T(8,128)(2,1)}, u32[]{:S(2)}, u32[]{:S(2)}) collective-permute-start(bf16[336,320]{1,0:T(8,128)(2,1)S(1)} %maximum_maximum_fusion.refs_12_), channel_id=1, source_target_pairs={{0,8},{8,0},{16,24},{24,16},{1,9},{9,1},{17,25},{25,17},{2,10},{10... | collective-permute-start | bytes 645128 | tf_op jit(solution)/shard_map/ppermute | solution.py:25
  30.3 21.8 %collective-permute-start.12 = (bf16[336,320]{1,0:T(8,128)(2,1)}, bf16[336,320]{1,0:T(8,128)(2,1)}, u32[]{:S(2)}, u32[]{:S(2)}) collective-permute-start(bf16[336,320]{1,0:T(8,128)(2,1)} %collective-permute-done.11.refs_14_), channel_id=1, source_target_pairs={{0,8},{8,0},{16,24},{24,16},{1,9},{9,1},{17,25},{25,17},{2,10},{10... | collective-permute-start | bytes 645128 | tf_op jit(solution)/shard_map/ppermute | solution.py:25
  33.8 5.3 %collective-permute-start.3 = (bf16[320,128]{1,0:T(8,128)(2,1)S(1)}, bf16[320,128]{1,0:T(8,128)(2,1)S(1)}, u32[]{:S(2)}, u32[]{:S(2)}) collective-permute-start(bf16[320,128]{1,0:T(8,128)(2,1)S(1)} %get-tuple-element.25), channel_id=1, source_target_pairs={{0,4},{1,5},{2,6},{3,7},{4,0},{5,1},{6,2},{7,3},{8,12},{9,13},{10,... | collective-permute-start | bytes 245768 | tf_op jit(solution)/shard_map/ppermute | solution.py:25
  39.7 10.6 %collective-permute-start.4 = (bf16[320,128]{1,0:T(8,128)(2,1)}, bf16[320,128]{1,0:T(8,128)(2,1)}, u32[]{:S(2)}, u32[]{:S(2)}) collective-permute-start(bf16[320,128]{1,0:T(8,128)(2,1)} %get-tuple-element.26), channel_id=1, source_target_pairs={{0,5},{1,4},{2,7},{3,6},{4,1},{5,0},{6,3},{7,2},{8,13},{9,12},{10,... | collective-permute-start | bytes 245768 | tf_op jit(solution)/shard_map/ppermute | solution.py:25
  43.3 7.0 %collective-permute-start.5 = (bf16[320,128]{1,0:T(8,128)(2,1)}, bf16[320,128]{1,0:T(8,128)(2,1)}, u32[]{:S(2)}, u32[]{:S(2)}) collective-permute-start(bf16[320,128]{1,0:T(8,128)(2,1)} %get-tuple-element.27), channel_id=1, source_target_pairs={{0,6},{1,7},{2,4},{3,5},{4,2},{5,3},{6,0},{7,1},{8,14},{9,15},{10,... | collective-permute-start | bytes 245768 | tf_op jit(solution)/shard_map/ppermute | solution.py:25
  44.6 7.6 %collective-permute-start.6 = (bf16[320,128]{1,0:T(8,128)(2,1)}, bf16[320,128]{1,0:T(8,128)(2,1)}, u32[]{:S(2)}, u32[]{:S(2)}) collective-permute-start(bf16[320,128]{1,0:T(8,128)(2,1)} %get-tuple-element.28), channel_id=1, source_target_pairs={{0,7},{1,6},{2,5},{3,4},{4,3},{5,2},{6,1},{7,0},{8,15},{9,14},{10,... | collective-permute-start | bytes 245768 | tf_op jit(solution)/shard_map/ppermute | solution.py:25
  72.9 7.4 %collective-permute-start.13 = (bf16[320,128]{1,0:T(8,128)(2,1)S(1)}, bf16[320,128]{1,0:T(8,128)(2,1)S(1)}, u32[]{:S(2)}, u32[]{:S(2)}) collective-permute-start(bf16[320,128]{1,0:T(8,128)(2,1)S(1)} %get-tuple-element.30), channel_id=1, source_target_pairs={{0,1},{1,0},{2,3},{3,2},{4,5},{5,4},{6,7},{7,6},{8,9},{9,8},{10,11... | collective-permute-start | bytes 245768 | tf_op jit(solution)/shard_map/ppermute | solution.py:25
  73.9 8.5 %collective-permute-start.14 = (bf16[320,128]{1,0:T(8,128)(2,1)S(1)}, bf16[320,128]{1,0:T(8,128)(2,1)S(1)}, u32[]{:S(2)}, u32[]{:S(2)}) collective-permute-start(bf16[320,128]{1,0:T(8,128)(2,1)S(1)} %get-tuple-element.31), channel_id=1, source_target_pairs={{0,2},{1,3},{2,0},{3,1},{4,6},{5,7},{6,4},{7,5},{8,10},{9,11},{10,... | collective-permute-start | bytes 245768 | tf_op jit(solution)/shard_map/ppermute | solution.py:25
  76.4 7.7 %collective-permute-start.15 = (bf16[320,128]{1,0:T(8,128)(2,1)S(1)}, bf16[320,128]{1,0:T(8,128)(2,1)S(1)}, u32[]{:S(2)}, u32[]{:S(2)}) collective-permute-start(bf16[320,128]{1,0:T(8,128)(2,1)S(1)} %get-tuple-element.32), channel_id=1, source_target_pairs={{0,3},{1,2},{2,1},{3,0},{4,7},{5,6},{6,5},{7,4},{8,11},{9,10},{10,... | collective-permute-start | bytes 245768 | tf_op jit(solution)/shard_map/ppermute | solution.py:25
  76.4 11.2 %collective-permute-start.16 = (bf16[320,128]{1,0:T(8,128)(2,1)S(1)}, bf16[320,128]{1,0:T(8,128)(2,1)S(1)}, u32[]{:S(2)}, u32[]{:S(2)}) collective-permute-start(bf16[320,128]{1,0:T(8,128)(2,1)S(1)} %get-tuple-element.33), channel_id=1, source_target_pairs={{0,4},{1,5},{2,6},{3,7},{4,0},{5,1},{6,2},{7,3},{8,12},{9,13},{10,... | collective-permute-start | bytes 245768 | tf_op jit(solution)/shard_map/ppermute | solution.py:25
  79.1 12.5 %collective-permute-start.17 = (bf16[320,128]{1,0:T(8,128)(2,1)S(1)}, bf16[320,128]{1,0:T(8,128)(2,1)S(1)}, u32[]{:S(2)}, u32[]{:S(2)}) collective-permute-start(bf16[320,128]{1,0:T(8,128)(2,1)S(1)} %get-tuple-element.34), channel_id=1, source_target_pairs={{0,5},{1,4},{2,7},{3,6},{4,1},{5,0},{6,3},{7,2},{8,13},{9,12},{10,... | collective-permute-start | bytes 245768 | tf_op jit(solution)/shard_map/ppermute | solution.py:25
  80.2 11.3 %collective-permute-start.18 = (bf16[320,128]{1,0:T(8,128)(2,1)S(1)}, bf16[320,128]{1,0:T(8,128)(2,1)S(1)}, u32[]{:S(2)}, u32[]{:S(2)}) collective-permute-start(bf16[320,128]{1,0:T(8,128)(2,1)S(1)} %get-tuple-element.35), channel_id=1, source_target_pairs={{0,6},{1,7},{2,4},{3,5},{4,2},{5,3},{6,0},{7,1},{8,14},{9,15},{10,... | collective-permute-start | bytes 245768 | tf_op jit(solution)/shard_map/ppermute | solution.py:25
  82.4 9.2 %collective-permute-start.19 = (bf16[320,128]{1,0:T(8,128)(2,1)S(1)}, bf16[320,128]{1,0:T(8,128)(2,1)S(1)}, u32[]{:S(2)}, u32[]{:S(2)}) collective-permute-start(bf16[320,128]{1,0:T(8,128)(2,1)S(1)} %get-tuple-element.36), channel_id=1, source_target_pairs={{0,7},{1,6},{2,5},{3,4},{4,3},{5,2},{6,1},{7,0},{8,15},{9,14},{10,... | collective-permute-start | bytes 245768 | tf_op jit(solution)/shard_map/ppermute | solution.py:25
  (19 other events, 67.1 us)

commit v2 on v1

v2 whole, which is shorter than its diff:
```python
import functools
import math

import jax
import jax.numpy as jnp
from jax import lax
from jax.experimental import pallas as pl
from jax.experimental.pallas import tpu as pltpu
from jax.sharding import PartitionSpec as P

BF = jnp.bfloat16
F32 = jnp.float32
LANES = 128
EPS = 1e-05


def embed(timesteps, width):
    half = width // 2
    freq = jnp.exp(-math.log(10000.0) * jnp.arange(half, dtype=jnp.float32) / half)
    angle = timesteps.astype(jnp.float32)[:, None] * freq[None, :]
    return jnp.concatenate([jnp.sin(angle), jnp.cos(angle)], axis=-1).astype(jnp.bfloat16)


def exchange(array, axis, by):
    return lax.ppermute(array, axis, [(i, i ^ by) for i in range(lax.axis_size(axis))])


def plain_section(state, gain, taps, film, projection, extra):
    values = state.astype(F32)
    meansq = jnp.mean(values * values, axis=1, keepdims=True)
    normed = (values * lax.rsqrt(meansq + EPS) * gain[None, :, None]).astype(BF)
    padded = jnp.pad(normed, ((1, 1), (0, 0), (0, 0)))
    count = state.shape[0]
    mixed = sum(
        jnp.einsum("io,fip->fop", taps[tau], padded[tau : tau + count], preferred_element_type=F32)
        for tau in range(3)
    )
    hidden = jax.nn.silu(mixed * (1.0 + film[None, :, None])).astype(BF)
    total = values + jnp.einsum("io,fip->fop", projection, hidden, preferred_element_type=F32)
    if extra is not None:
        total = total + jnp.einsum("io,fip->fop", extra[0], extra[1], preferred_element_type=F32)
    return total.astype(BF)


def plain_shards(clips, timesteps, gain, temporal_weight, film_weight, out_weight, skip_weight):
    own = clips[0]
    pixels = own.shape[2]
    split = lax.axis_size("frame")
    pad = -pixels % split
    if pad:
        own = jnp.pad(own, ((0, 0), (0, 0), (0, pad)))
    state = lax.all_to_all(own, "frame", 2, 0, tiled=True)
    emb = embed(timesteps, clips.shape[2])
    film = jnp.dot(emb, film_weight[0], preferred_element_type=F32)
    taps = lax.all_gather(temporal_weight[0], "segment")
    projection = lax.all_gather(out_weight[0], "segment")
    films = lax.all_gather(film, "segment")
    micro = lax.axis_index("segment")
    first = state
    skips = {}
    for section in range(gain.shape[0]):
        extra = None
        if section == 2:
            extra = (skip_weight[0], skips[0])
        if section == 3:
            extra = (skip_weight[1], first)
        film_vec = lax.dynamic_index_in_dim(films[section], micro, 0, keepdims=False)
        state = plain_section(
            state, gain[section], taps[section], film_vec, projection[section], extra
        )
        skips[section] = state
    result = lax.all_to_all(state, "frame", 0, 2, tiled=True)
    return result[None, :, :, :pixels]


FILM_ROWS = 16


def place():
    segment, frame = lax.axis_index("segment"), lax.axis_index("frame")
    return segment // 2, segment % 2, frame // 2, frame % 2


def devices():
    for segment in range(4):
        for frame in range(8):
            yield segment, frame, (segment // 2, segment % 2, frame // 2, frame % 2)


def move(array, rule):
    pairs = []
    for segment, frame, (y, c, z, x) in devices():
        y, c, z, x = rule(y, c, z, x)
        pairs.append((segment * 8 + frame, (2 * y + c) * 8 + 2 * z + x))
    return lax.ppermute(array, ("segment", "frame"), pairs)


def turn(array, by):
    return move(array, lambda y, c, z, x: (y, x, z ^ by, c))


def swap_cores(array):
    return move(array, lambda y, c, z, x: (y, 1 - c, z, x))


def swap_planes(array):
    return move(array, lambda y, c, z, x: (1 - y, c, z, x))


def pin(arrays, space):
    return [pltpu.with_memory_space_constraint(a, space) for a in arrays]


def pack_kernel(levels, times_ref, x_ref, taps_ref, projection_ref, film_ref, *outs):
    width = projection_ref.shape[0]
    pack = outs[levels]
    held = jnp.concatenate(
        [taps_ref[...].reshape(3 * width, width).T, projection_ref[...].T], axis=1
    )
    lane = lax.broadcasted_iota(jnp.int32, (8, width), 1)
    row = lax.broadcasted_iota(jnp.int32, (8, width), 0)
    half = width // 2
    index = jnp.where(lane < half, lane, lane - half).astype(F32)
    freq = jnp.exp(-math.log(10000.0) * index / half)
    times = jnp.zeros((8, width), jnp.int32)
    for m in range(4):
        times = jnp.where(row == m, times_ref[m], times)
    angle = times.astype(F32) * freq
    emb = jnp.where(lane < half, jnp.sin(angle), jnp.cos(angle)).astype(BF)
    film = jnp.dot(emb, film_ref[...], preferred_element_type=F32)
    high = film.astype(BF).astype(F32)
    rows = jnp.concatenate([high[0:4], (film - high)[0:4], jnp.zeros((8, width), F32)], axis=0)
    rows = jnp.concatenate([rows.astype(BF), jnp.zeros((FILM_ROWS, 3 * width), BF)], axis=1)
    pack[0:width] = held
    pack[width:] = rows
    z = lax.axis_index("frame") // 2
    for d in range(levels):
        for k in range(2):
            at = pl.multiple_of(((z ^ d) * 2 + k) * LANES, LANES)
            outs[d][k] = x_ref[:, pl.ds(at, LANES)]


def pack_and_cut(times, own, taps, projection, film_weight, levels):
    width = own.shape[0]
    vmem = pl.BlockSpec(memory_space=pltpu.VMEM)
    return pl.pallas_call(
        functools.partial(pack_kernel, levels),
        out_shape=[jax.ShapeDtypeStruct((2, width, LANES), BF)] * levels
        + [jax.ShapeDtypeStruct((width + FILM_ROWS, 4 * width), BF)],
        in_specs=[pl.BlockSpec(memory_space=pltpu.SMEM)] + [vmem] * 4,
        out_specs=[vmem] * (levels + 1),
        name="pack",
    )(times, own, taps, projection, film_weight)


def join_kernel(levels, *refs):
    blocks, out = refs[:levels], refs[levels]
    frame = lax.axis_index("frame")
    z, x = frame // 2, frame % 2
    for d in range(levels):
        for k in range(2):
            at = pl.multiple_of(((z ^ d) * 2 + (x ^ k)) * LANES, LANES)
            out[:, pl.ds(at, LANES)] = blocks[d][k]


def join_blocks(blocks):
    levels, width = len(blocks), blocks[0].shape[1]
    vmem = pl.BlockSpec(memory_space=pltpu.VMEM)
    return pl.pallas_call(
        functools.partial(join_kernel, levels),
        out_shape=jax.ShapeDtypeStruct((width, 2 * levels * LANES), BF),
        in_specs=[vmem] * levels,
        out_specs=vmem,
        name="join",
    )(*pin(blocks, pltpu.VMEM))


def sections_kernel(spans, dests, borders, levels, width, loaded, *refs):
    refs = list(refs)

    def take(count):
        taken = refs[:count]
        del refs[:count]
        return taken

    near = borders is not None and spans[0][0] == 0
    turned, swapped = take(len(loaded)), take(len(loaded))
    packs = take(4)
    skip_in, gain_ref = take(2)
    if near:
        (border_in,) = take(1)
    kept, given = take(2)
    if borders and not near:
        (border_out,) = take(1)
    first, weights, skip, unfolded, with_one, with_first, two, three, last, bordering = take(10)
    sem_x, sem_w, sem_s, sem_o, sem_b = take(5)
    y, core, z, x = place()
    clip = 2 * y + x
    segment = 2 * y + core
    frames = 2 * levels
    upper = jnp.where(z >= levels // 2, 1, 0)
    mirror = upper * (frames - 1)

    loads = []
    for n, d in enumerate(loaded):
        for k in range(2):
            slot = (2 * (z ^ d) + (core ^ k)) ^ mirror
            source = (turned, swapped)[k][n].at[core]
            loads.append(pltpu.make_async_copy(source, first.at[slot], sem_x.at[2 * n + k]))
    if near:
        loads.append(pltpu.make_async_copy(border_in, bordering, sem_b))
    for load in loads:
        load.start()

    for s in range(4):
        for b in range(4):

            @pl.when(segment ^ s == b)
            def _():
                pltpu.make_async_copy(packs[b], weights.at[s], sem_w.at[s]).start()

    skip_load = pltpu.make_async_copy(skip_in, skip, sem_s)
    skip_load.start()

    def rows_of(step):
        return pl.ds(pl.multiple_of((1 - step + 2 * step * upper) * width, 64), width)

    def span(f, count=1):
        return slice(f * LANES, (f + count) * LANES)

    zeros = jnp.zeros((width, LANES), BF)
    unfolded[3 * width :, :] = jnp.zeros((unfolded.shape[0] - 3 * width, frames * LANES), BF)
    unfolded[rows_of(1), span(0)] = zeros
    unfolded[rows_of(-1), span(frames - 1)] = zeros
    for ref in (with_one, with_first):
        ref[0:64, :] = jnp.zeros((64, frames * LANES), BF)

    def column_of(rows, chosen):
        at = lax.broadcasted_iota(jnp.int32, (16, LANES), 0)
        hit = functools.reduce(jnp.logical_or, [at == c for c in chosen])
        return lax.dot_general(
            rows,
            jnp.where(hit, 1.0, 0.0).astype(BF),
            (((0,), (0,)), ((), ())),
            preferred_element_type=F32,
        )

    gains = []
    rest = gain_ref[...]
    for _ in range(3):
        gains.append(rest.astype(BF).astype(F32))
        rest = rest - gains[-1]
    gains = jnp.concatenate(gains + [jnp.zeros_like(rest)], axis=0).astype(BF)

    for load in loads:
        load.wait()
    one, zero = with_one.at[64 + width :, :], with_first.at[64 + width :, :]
    states = (zero, one, two, three)
    for f in range(2 * len(loaded)):
        zero[:, span(f)] = first[f]
    if near:
        for n, (s, f) in enumerate(borders):
            states[s][:, span(f)] = bordering[n]

    for s, (low, high) in enumerate(spans):
        source = states[s]
        gain = column_of(gains, [s, 4 + s, 8 + s])
        for f in range(max(low - 1, 0), min(high + 1, frames)):
            values = source[:, span(f)].astype(F32)
            scale = lax.rsqrt(jnp.mean(values * values, axis=0, keepdims=True) + EPS)
            normed = (values * scale * gain).astype(BF)
            for step in (-1, 0, 1):
                if low <= f + step < high:
                    unfolded[rows_of(step), span(f + step)] = normed
        pltpu.make_async_copy(packs[0], weights.at[s], sem_w.at[s]).wait()
        film = 1.0 + column_of(weights[s, width:, 0:width], [clip, 4 + clip])
        film = jnp.concatenate([film] * (high - low), axis=1)
        cols = span(low, high - low)
        taps = weights[s, 0:width, 0 : unfolded.shape[0]]
        mixed = jnp.dot(taps, unfolded[:, cols], preferred_element_type=F32) * film
        hidden = (mixed * (0.5 + 0.5 * jnp.tanh(0.5 * mixed))).astype(BF)
        projection = weights[s, 0:width, 3 * width - 64 :]
        if s < 2:
            with_one[64 : 64 + width, cols] = hidden
            right = with_one[0 : 64 + width, cols]
        else:
            if s == 2:
                skip_load.wait()
            beside = with_one if s == 2 else with_first
            beside[64 : 64 + width, cols] = hidden
            right = beside[:, cols]
            projection = jnp.concatenate([projection, skip[s - 2].T], axis=1)
        total = source[:, cols].astype(F32)
        total = (total + jnp.dot(projection, right, preferred_element_type=F32)).astype(BF)
        if s < 3:
            states[s + 1][:, cols] = total
        else:
            for f in range(low, high):
                last[f] = total[:, span(f - low)]
    stores = []
    for n, d in enumerate(dests):
        for k, out in enumerate((kept, given)):
            slot = (2 * (z ^ d) + (core ^ k)) ^ mirror
            stores.append(
                pltpu.make_async_copy(last.at[slot], out.at[n], sem_o.at[2 * n + k])
            )
    if borders and not near:
        for n, (s, f) in enumerate(borders):
            bordering[n] = states[s][:, span(f)]
        stores.append(pltpu.make_async_copy(bordering, border_out, sem_b))
    for store in stores:
        store.start()
    for store in stores:
        store.wait()


def run_sections(spans, dests, borders, turned, swapped, weights, skip, gain, border=None):
    levels = lax.axis_size("frame") // 2
    frames = 2 * levels
    width = gain.shape[1]
    columns = frames * LANES
    hbm = pl.BlockSpec(memory_space=pltpu.HBM)
    vmem = pl.BlockSpec(memory_space=pltpu.VMEM)
    given_out = [jax.ShapeDtypeStruct((len(dests), width, LANES), BF)] * 2
    blocks, inputs = [*turned, *swapped], [*weights, skip]
    after = []
    if border is not None:
        after = pin([border], pltpu.HBM)
    elif borders:
        given_out.append(jax.ShapeDtypeStruct((len(borders), width, LANES), BF))
    flops = sum(high - low for low, high in spans) * LANES * 2 * 5 * width * width
    return pl.pallas_call(
        functools.partial(
            sections_kernel, spans, dests, borders, levels, width, list(range(len(turned)))
        ),
        out_shape=given_out,
        in_specs=[vmem] * len(blocks)
        + [hbm] * len(inputs)
        + [pl.BlockSpec(memory_space=pltpu.VMEM)]
        + [hbm] * len(after),
        out_specs=[hbm] * len(given_out),
        scratch_shapes=[
            pltpu.VMEM((frames, width, LANES), BF),
            pltpu.VMEM((4, width + FILM_ROWS, 4 * width), BF),
            pltpu.VMEM((2, width, width), BF),
            pltpu.VMEM((3 * width + 64, columns), BF),
            pltpu.VMEM((2 * width + 64, columns), BF),
            pltpu.VMEM((2 * width + 64, columns), BF),
            pltpu.VMEM((width, columns), BF),
            pltpu.VMEM((width, columns), BF),
            pltpu.VMEM((frames, width, LANES), BF),
            pltpu.VMEM((6, width, LANES), BF),
            pltpu.SemaphoreType.DMA((frames,)),
            pltpu.SemaphoreType.DMA((4,)),
            pltpu.SemaphoreType.DMA,
            pltpu.SemaphoreType.DMA((frames,)),
            pltpu.SemaphoreType.DMA,
        ],
        compiler_params=pltpu.CompilerParams(vmem_limit_bytes=40 << 20),
        cost_estimate=pl.CostEstimate(flops=flops, bytes_accessed=4 << 20, transcendentals=0),
        name="sections",
    )(*pin(blocks, pltpu.VMEM), *pin(inputs, pltpu.HBM), gain, *after)


def send_back(kept, given, dests):
    swapped = swap_cores(given)
    blocks = [jnp.stack([kept[n], swapped[n]]) for n in range(len(dests))]
    return [turn(block, d) for block, d in zip(blocks, dests, strict=True)], blocks


SPLIT = False


def block_shards(clips, timesteps, gain, temporal_weight, film_weight, out_weight, skip_weight):
    levels = lax.axis_size("frame") // 2
    order = [3, 2, 1, 0]

    *cut, pack0 = pack_and_cut(
        timesteps, clips[0, 0], temporal_weight[0], out_weight[0], film_weight[0], levels
    )
    pack2 = swap_planes(pack0)
    turned = [None] * levels
    for d in order:
        turned[d] = turn(cut[d], d)
    pack1 = swap_cores(pack0)

    turned, pack2 = lax.optimization_barrier((turned, pack2))
    swapped = [swap_cores(block) for block in turned]
    pack3 = swap_cores(pack2)

    weights = [pack0, pack1, pack2, pack3]
    frames = 2 * levels
    if SPLIT:
        borders = [(1, 1), (1, 2), (2, 2), (2, 3), (3, 3), (3, 4)]
        far = [(s + 1, frames) for s in range(4)]
        kept, given, border = run_sections(
            far, [2, 3], borders, turned, swapped, weights, skip_weight, gain
        )
        back, blocks = send_back(kept, given, [2, 3])
        border, _ = lax.optimization_barrier((border, blocks))
        kept, given = run_sections(
            [(0, s + 1) for s in range(4)],
            [0, 1],
            borders,
            turned[:2],
            swapped[:2],
            weights,
            skip_weight,
            gain,
            border,
        )
        back = send_back(kept, given, [0, 1])[0] + back
    else:
        kept, given = run_sections(
            [(0, frames)] * 4, [0, 1, 2, 3], None, turned, swapped, weights, skip_weight, gain
        )
        back = send_back(kept, given, [0, 1, 2, 3])[0]
    return join_blocks(back)[None, None]


def solution(mesh):
    placed = (
        P("segment", "frame", None, None),
        P(),
        P(),
        P("segment", None, None, None),
        P("segment", None, None),
        P("segment", None, None),
        P(),
    )

    def run(*arrays):
        clips, gain = arrays[0], arrays[2]
        split = mesh.shape["frame"]
        fits = (
            clips.shape[1] == split == 8
            and clips.shape[3] == split * LANES
            and clips.shape[2] % 64 == 0
            and clips.shape[0] == gain.shape[0] == mesh.shape["segment"] == 4
        )
        return jax.shard_map(
            block_shards if fits else plain_shards,
            mesh=mesh,
            in_specs=placed,
            out_specs=P("segment", "frame", None, None),
            check_vma=False,
        )(*arrays)

    return run
```

time: 114 us -> 62.3 us (0.55)
  the two profiles are of different devices: /device:TPU:0 before, /device:TPU:17 now
where the time goes in v2:
time: 62.3 us; the launch traced here: 62.2 us
  waiting for transfers between devices  28.5 us (46%)
  starting transfers between devices  18.5 us (30%)
  Pallas kernels  14 us (22%)
  local copies, waits for them, and re-layouts  0.96 us (2%)
    ppermute x16, waiting for transfers between devices, move(): return lax.ppermute(array, ('segment', 'frame'), pairs)  28.5 us
    ppermute x16, starting transfers between devices, move(): return lax.ppermute(array, ('segment', 'frame'), pairs)  18.5 us
    pallas_call x1, Pallas kernels, run_sections(): pl.pallas_call(functools.partial(sections_kernel, spans, dests, borders,...  9.97 us
    pallas_call x1, Pallas kernels, pack_and_cut(): pl.pallas_call(functools.partial(pack_kernel, levels), out_shape=[jax.Sha...  2.97 us
  transfers between devices with their start and end apart: 16, of which 11 were waited for; matrix products, arithmetic and copies ran while one was open for 0% of the time, Pallas kernels for 0%

profile of v2, /device:TPU:17, one launch (start us, length us, event | category | flops | bytes accessed | tf_op | source)
XLA Modules:
  0.0 62.2 jit_solution(688236798157825736)
XLA Ops:
  0.0 3.0 %pack.1 = (bf16[2,320,128]{2,1,0:T(8,128)(2,1)}, bf16[2,320,128]{2,1,0:T(8,128)(2,1)}, bf16[2,320,128]{2,1,0:T(8,128)(2,1)}, bf16[2,320,128]{2,1,0:T(8,128)(2,1)}, bf16[336,1280]{1,0:T(8,128)(2,1)}) custom-call(s32[4]{0:T(128)} %times_ref.1, bf16[320,1024]{1,0:T(8,128)(2,1)} %bitcast.6, bf16[3,320,320]{2,1,0:T(8,128)(2,1)} %bitcast.5, ...), custom_call_target="tpu_custom_call" | custom-call | tf_op jit(solution)/shard_map/pack/pallas_call | solution.py:146
  3.0 1.2 %collective-permute-start.4 = (bf16[336,1280]{1,0:T(8,128)(2,1)}, bf16[336,1280]{1,0:T(8,128)(2,1)S(1)}, u32[]{:S(2)}, u32[]{:S(2)}) collective-permute-start(bf16[336,1280]{1,0:T(8,128)(2,1)} %get-tuple-element.21.refs_8_), channel_id=1, source_target_pairs={{0,16},{1,17},{2,18},{3,19},{4,20},{5,21},{6,22},{7,23},{8,24},{9,... | collective-permute-start | bytes 2580488 | tf_op jit(solution)/shard_map/ppermute | solution.py:95
  4.2 3.9 %collective-permute-start = (bf16[2,320,128]{2,1,0:T(8,128)(2,1)}, bf16[2,320,128]{2,1,0:T(8,128)(2,1)S(1)}, u32[]{:S(2)}, u32[]{:S(2)}) collective-permute-start(bf16[2,320,128]{2,1,0:T(8,128)(2,1)} %get-tuple-element.17), channel_id=1, source_target_pairs={{0,0},{1,8},{2,2},{3,10},{4,4},{5,12},{6,6},{7,14},{8,1},{9,9},{10... | collective-permute-start | bytes 491528 | tf_op jit(solution)/shard_map/ppermute | solution.py:95
  8.2 1.1 %collective-permute-start.1 = (bf16[2,320,128]{2,1,0:T(8,128)(2,1)}, bf16[2,320,128]{2,1,0:T(8,128)(2,1)S(1)}, u32[]{:S(2)}, u32[]{:S(2)}) collective-permute-start(bf16[2,320,128]{2,1,0:T(8,128)(2,1)} %get-tuple-element.18), channel_id=1, source_target_pairs={{0,2},{1,10},{2,0},{3,8},{4,6},{5,14},{6,4},{7,12},{8,3},{9,11},{1... | collective-permute-start | bytes 491528 | tf_op jit(solution)/shard_map/ppermute | solution.py:95
  9.3 1.5 %collective-permute-start.2 = (bf16[2,320,128]{2,1,0:T(8,128)(2,1)}, bf16[2,320,128]{2,1,0:T(8,128)(2,1)S(1)}, u32[]{:S(2)}, u32[]{:S(2)}) collective-permute-start(bf16[2,320,128]{2,1,0:T(8,128)(2,1)} %get-tuple-element.19), channel_id=1, source_target_pairs={{0,4},{1,12},{2,6},{3,14},{4,0},{5,8},{6,2},{7,10},{8,5},{9,13},{1... | collective-permute-start | bytes 491528 | tf_op jit(solution)/shard_map/ppermute | solution.py:95
  10.8 1.2 %collective-permute-start.3 = (bf16[2,320,128]{2,1,0:T(8,128)(2,1)}, bf16[2,320,128]{2,1,0:T(8,128)(2,1)S(1)}, u32[]{:S(2)}, u32[]{:S(2)}) collective-permute-start(bf16[2,320,128]{2,1,0:T(8,128)(2,1)} %get-tuple-element.20), channel_id=1, source_target_pairs={{0,6},{1,14},{2,4},{3,12},{4,2},{5,10},{6,0},{7,8},{8,7},{9,15},{1... | collective-permute-start | bytes 491528 | tf_op jit(solution)/shard_map/ppermute | solution.py:95
  12.0 4.0 %collective-permute-done.1.refs_1_ = bf16[2,320,128]{2,1,0:T(8,128)(2,1)S(1)} collective-permute-done((bf16[2,320,128]{2,1,0:T(8,128)(2,1)}, bf16[2,320,128]{2,1,0:T(8,128)(2,1)S(1)}, u32[]{:S(2)}, u32[]{:S(2)}) %collective-permute-start.1) | collective-permute-done | bytes 163872 | tf_op jit(solution)/shard_map/ppermute | solution.py:95
  16.0 6.0 %collective-permute-done.2.refs_2_ = bf16[2,320,128]{2,1,0:T(8,128)(2,1)S(1)} collective-permute-done((bf16[2,320,128]{2,1,0:T(8,128)(2,1)}, bf16[2,320,128]{2,1,0:T(8,128)(2,1)S(1)}, u32[]{:S(2)}, u32[]{:S(2)}) %collective-permute-start.2) | collective-permute-done | bytes 163872 | tf_op jit(solution)/shard_map/ppermute | solution.py:95
  22.0 2.6 %collective-permute-done.3.refs_3_ = bf16[2,320,128]{2,1,0:T(8,128)(2,1)S(1)} collective-permute-done((bf16[2,320,128]{2,1,0:T(8,128)(2,1)}, bf16[2,320,128]{2,1,0:T(8,128)(2,1)S(1)}, u32[]{:S(2)}, u32[]{:S(2)}) %collective-permute-start.3) | collective-permute-done | bytes 163872 | tf_op jit(solution)/shard_map/ppermute | solution.py:95
  24.7 0.4 collective-permute-start.5
  25.2 0.4 collective-permute-start.7
  25.8 1.5 %collective-permute-done.5.refs_4_ = bf16[2,320,128]{2,1,0:T(8,128)(2,1)S(1)} collective-permute-done((bf16[2,320,128]{2,1,0:T(8,128)(2,1)S(1)}, bf16[2,320,128]{2,1,0:T(8,128)(2,1)S(1)}, u32[]{:S(2)}, u32[]{:S(2)}) %collective-permute-start.5) | collective-permute-done | bytes 163872 | tf_op jit(solution)/shard_map/ppermute | solution.py:95
  27.2 0.2 collective-permute-done.6.refs_5_
  27.5 0.2 collective-permute-done.7.refs_6_
  28.0 0.9 %copy-done.3 = bf16[336,1280]{1,0:T(8,128)(2,1)} copy-done((bf16[336,1280]{1,0:T(8,128)(2,1)}, bf16[336,1280]{1,0:T(8,128)(2,1)S(1)}, u32[]{:S(2)}) %copy-start.3) | copy-done | bytes 860184
  28.9 10.0 %sections.1 = (bf16[4,320,128]{2,1,0:T(8,128)(2,1)S(1)}, bf16[4,320,128]{2,1,0:T(8,128)(2,1)S(1)}) custom-call(bf16[2,320,128]{2,1,0:T(8,128)(2,1)S(1)} %collective-permute-done.refs_0_, bf16[2,320,128]{2,1,0:T(8,128)(2,1)S(1)} %collective-permute-done.1.refs_1_, bf16[2,320,128]{2,1,0:T(8,128)(2,1)S(1)} %collective-permute-done.2.refs_2_, ...), custom_call_target="tpu_custom_call" | custom-call | flops 4194304000 | bytes 4194304 | tf_op jit(solution)/shard_map/sections/pallas_call | solution.py:332
  39.1 1.5 %collective-permute-done.11 = bf16[4,320,128]{2,1,0:T(8,128)(2,1)S(1)} collective-permute-done((bf16[4,320,128]{2,1,0:T(8,128)(2,1)S(1)}, bf16[4,320,128]{2,1,0:T(8,128)(2,1)S(1)}, u32[]{:S(2)}, u32[]{:S(2)}) %collective-permute-start.11) | collective-permute-done | bytes 327712 | tf_op jit(solution)/shard_map/ppermute | solution.py:95
  40.6 4.4 %collective-permute-start.12 = (bf16[2,320,128]{2,1,0:T(8,128)(2,1)S(1)}, bf16[2,320,128]{2,1,0:T(8,128)(2,1)S(1)}, u32[]{:S(2)}, u32[]{:S(2)}) collective-permute-start(bf16[2,320,128]{2,1,0:T(8,128)(2,1)S(1)} %pad_maximum_fusion), channel_id=1, source_target_pairs={{0,0},{1,8},{2,2},{3,10},{4,4},{5,12},{6,6},{7,14},{8,1},{9,9},{10... | collective-permute-start | bytes 491528 | tf_op jit(solution)/shard_map/ppermute | solution.py:95
  45.2 2.6 %collective-permute-start.14 = (bf16[2,320,128]{2,1,0:T(8,128)(2,1)S(1)}, bf16[2,320,128]{2,1,0:T(8,128)(2,1)S(1)}, u32[]{:S(2)}, u32[]{:S(2)}) collective-permute-start(bf16[2,320,128]{2,1,0:T(8,128)(2,1)S(1)} %pad_maximum_fusion.2), channel_id=1, source_target_pairs={{0,4},{1,12},{2,6},{3,14},{4,0},{5,8},{6,2},{7,10},{8,5},{9,13},{1... | collective-permute-start | bytes 491528 | tf_op jit(solution)/shard_map/ppermute | solution.py:95
  47.8 1.1 %collective-permute-start.15 = (bf16[2,320,128]{2,1,0:T(8,128)(2,1)S(1)}, bf16[2,320,128]{2,1,0:T(8,128)(2,1)S(1)}, u32[]{:S(2)}, u32[]{:S(2)}) collective-permute-start(bf16[2,320,128]{2,1,0:T(8,128)(2,1)S(1)} %pad_maximum_fusion.3), channel_id=1, source_target_pairs={{0,6},{1,14},{2,4},{3,12},{4,2},{5,10},{6,0},{7,8},{8,7},{9,15},{1... | collective-permute-start | bytes 491528 | tf_op jit(solution)/shard_map/ppermute | solution.py:95
  48.9 3.7 %collective-permute-done.13.refs_1_ = bf16[2,320,128]{2,1,0:T(8,128)(2,1)S(1)} collective-permute-done((bf16[2,320,128]{2,1,0:T(8,128)(2,1)S(1)}, bf16[2,320,128]{2,1,0:T(8,128)(2,1)S(1)}, u32[]{:S(2)}, u32[]{:S(2)}) %collective-permute-start.13) | collective-permute-done | bytes 163872 | tf_op jit(solution)/shard_map/ppermute | solution.py:95
  52.6 4.2 %collective-permute-done.14.refs_2_ = bf16[2,320,128]{2,1,0:T(8,128)(2,1)S(1)} collective-permute-done((bf16[2,320,128]{2,1,0:T(8,128)(2,1)S(1)}, bf16[2,320,128]{2,1,0:T(8,128)(2,1)S(1)}, u32[]{:S(2)}, u32[]{:S(2)}) %collective-permute-start.14) | collective-permute-done | bytes 163872 | tf_op jit(solution)/shard_map/ppermute | solution.py:95
  56.8 4.3 %collective-permute-done.15.refs_3_ = bf16[2,320,128]{2,1,0:T(8,128)(2,1)S(1)} collective-permute-done((bf16[2,320,128]{2,1,0:T(8,128)(2,1)S(1)}, bf16[2,320,128]{2,1,0:T(8,128)(2,1)S(1)}, u32[]{:S(2)}, u32[]{:S(2)}) %collective-permute-start.15) | collective-permute-done | bytes 163872 | tf_op jit(solution)/shard_map/ppermute | solution.py:95
  61.1 1.0 %join.1 = bf16[320,1024]{1,0:T(8,128)(2,1)} custom-call(bf16[2,320,128]{2,1,0:T(8,128)(2,1)S(1)} %collective-permute-done.12.refs_0_, bf16[2,320,128]{2,1,0:T(8,128)(2,1)S(1)} %collective-permute-done.13.refs_1_, bf16[2,320,128]{2,1,0:T(8,128)(2,1)S(1)} %collective-permute-done.14.refs_2_, bf16[2,320,128]{2,1,0:T(8,128)(2,1)S(1)} %collective-permute-done.15.refs_3_), custom_call_target="tpu_custom_call" | custom-call | tf_op jit(solution)/shard_map/join/pallas_call | solution.py:169
  (25 shorter events, 1.0 us)
Async XLA Ops:
  3.0 25.9 %copy-start = (f32[4,320]{1,0:T(4,128)S(1)}, f32[4,320]{1,0:T(4,128)}, u32[]{:S(2)}) copy-start(f32[4,320]{1,0:T(4,128)} %refs_13_.1) | copy-start | bytes 15364
  3.0 21.6 %collective-permute-start.4 = (bf16[336,1280]{1,0:T(8,128)(2,1)}, bf16[336,1280]{1,0:T(8,128)(2,1)S(1)}, u32[]{:S(2)}, u32[]{:S(2)}) collective-permute-start(bf16[336,1280]{1,0:T(8,128)(2,1)} %get-tuple-element.21.refs_8_), channel_id=1, source_target_pairs={{0,16},{1,17},{2,18},{3,19},{4,20},{5,21},{6,22},{7,23},{8,24},{9,... | collective-permute-start | bytes 2580488 | tf_op jit(solution)/shard_map/ppermute | solution.py:95
  4.2 7.8 %collective-permute-start = (bf16[2,320,128]{2,1,0:T(8,128)(2,1)}, bf16[2,320,128]{2,1,0:T(8,128)(2,1)S(1)}, u32[]{:S(2)}, u32[]{:S(2)}) collective-permute-start(bf16[2,320,128]{2,1,0:T(8,128)(2,1)} %get-tuple-element.17), channel_id=1, source_target_pairs={{0,0},{1,8},{2,2},{3,10},{4,4},{5,12},{6,6},{7,14},{8,1},{9,9},{10... | collective-permute-start | bytes 491528 | tf_op jit(solution)/shard_map/ppermute | solution.py:95
  8.2 7.8 %collective-permute-start.1 = (bf16[2,320,128]{2,1,0:T(8,128)(2,1)}, bf16[2,320,128]{2,1,0:T(8,128)(2,1)S(1)}, u32[]{:S(2)}, u32[]{:S(2)}) collective-permute-start(bf16[2,320,128]{2,1,0:T(8,128)(2,1)} %get-tuple-element.18), channel_id=1, source_target_pairs={{0,2},{1,10},{2,0},{3,8},{4,6},{5,14},{6,4},{7,12},{8,3},{9,11},{1... | collective-permute-start | bytes 491528 | tf_op jit(solution)/shard_map/ppermute | solution.py:95
  9.3 12.7 %collective-permute-start.2 = (bf16[2,320,128]{2,1,0:T(8,128)(2,1)}, bf16[2,320,128]{2,1,0:T(8,128)(2,1)S(1)}, u32[]{:S(2)}, u32[]{:S(2)}) collective-permute-start(bf16[2,320,128]{2,1,0:T(8,128)(2,1)} %get-tuple-element.19), channel_id=1, source_target_pairs={{0,4},{1,12},{2,6},{3,14},{4,0},{5,8},{6,2},{7,10},{8,5},{9,13},{1... | collective-permute-start | bytes 491528 | tf_op jit(solution)/shard_map/ppermute | solution.py:95
  10.8 13.8 %collective-permute-start.3 = (bf16[2,320,128]{2,1,0:T(8,128)(2,1)}, bf16[2,320,128]{2,1,0:T(8,128)(2,1)S(1)}, u32[]{:S(2)}, u32[]{:S(2)}) collective-permute-start(bf16[2,320,128]{2,1,0:T(8,128)(2,1)} %get-tuple-element.20), channel_id=1, source_target_pairs={{0,6},{1,14},{2,4},{3,12},{4,2},{5,10},{6,0},{7,8},{8,7},{9,15},{1... | collective-permute-start | bytes 491528 | tf_op jit(solution)/shard_map/ppermute | solution.py:95
  12.0 13.7 %collective-permute-start.9 = (bf16[336,1280]{1,0:T(8,128)(2,1)}, bf16[336,1280]{1,0:T(8,128)(2,1)S(1)}, u32[]{:S(2)}, u32[]{:S(2)}) collective-permute-start(bf16[336,1280]{1,0:T(8,128)(2,1)} %get-tuple-element.21.refs_8_), channel_id=1, source_target_pairs={{0,8},{1,9},{2,10},{3,11},{4,12},{5,13},{6,14},{7,15},{8,0},{9,1},... | collective-permute-start | bytes 2580488 | tf_op jit(solution)/shard_map/ppermute | solution.py:95
  24.6 3.3 %copy-start.1 = (bf16[336,1280]{1,0:T(8,128)(2,1)}, bf16[336,1280]{1,0:T(8,128)(2,1)S(1)}, u32[]{:S(2)}) copy-start(bf16[336,1280]{1,0:T(8,128)(2,1)S(1)} %collective-permute-done.4.refs_10_) | copy-start | bytes 2580484
  24.6 3.3 %collective-permute-start.10 = (bf16[336,1280]{1,0:T(8,128)(2,1)S(1)}, bf16[336,1280]{1,0:T(8,128)(2,1)S(1)}, u32[]{:S(2)}, u32[]{:S(2)}) collective-permute-start(bf16[336,1280]{1,0:T(8,128)(2,1)S(1)} %collective-permute-done.4.refs_10_), channel_id=1, source_target_pairs={{0,8},{1,9},{2,10},{3,11},{4,12},{5,13},{6,14},{7,15},{8,0},{9,1},... | collective-permute-start | bytes 2580488 | tf_op jit(solution)/shard_map/ppermute | solution.py:95
  24.7 2.5 %collective-permute-start.5 = (bf16[2,320,128]{2,1,0:T(8,128)(2,1)S(1)}, bf16[2,320,128]{2,1,0:T(8,128)(2,1)S(1)}, u32[]{:S(2)}, u32[]{:S(2)}) collective-permute-start(bf16[2,320,128]{2,1,0:T(8,128)(2,1)S(1)} %collective-permute-done.refs_0_), channel_id=1, source_target_pairs={{0,8},{1,9},{2,10},{3,11},{4,12},{5,13},{6,14},{7,15},{8,0},{9,1},... | collective-permute-start | bytes 491528 | tf_op jit(solution)/shard_map/ppermute | solution.py:95
  25.1 2.3 %collective-permute-start.6 = (bf16[2,320,128]{2,1,0:T(8,128)(2,1)S(1)}, bf16[2,320,128]{2,1,0:T(8,128)(2,1)S(1)}, u32[]{:S(2)}, u32[]{:S(2)}) collective-permute-start(bf16[2,320,128]{2,1,0:T(8,128)(2,1)S(1)} %collective-permute-done.1.refs_1_), channel_id=1, source_target_pairs={{0,8},{1,9},{2,10},{3,11},{4,12},{5,13},{6,14},{7,15},{8,0},{9,1},... | collective-permute-start | bytes 491528 | tf_op jit(solution)/shard_map/ppermute | solution.py:95
  25.2 2.5 %collective-permute-start.7 = (bf16[2,320,128]{2,1,0:T(8,128)(2,1)S(1)}, bf16[2,320,128]{2,1,0:T(8,128)(2,1)S(1)}, u32[]{:S(2)}, u32[]{:S(2)}) collective-permute-start(bf16[2,320,128]{2,1,0:T(8,128)(2,1)S(1)} %collective-permute-done.2.refs_2_), channel_id=1, source_target_pairs={{0,8},{1,9},{2,10},{3,11},{4,12},{5,13},{6,14},{7,15},{8,0},{9,1},... | collective-permute-start | bytes 491528 | tf_op jit(solution)/shard_map/ppermute | solution.py:95
  25.6 2.3 %copy-start.2 = (bf16[336,1280]{1,0:T(8,128)(2,1)}, bf16[336,1280]{1,0:T(8,128)(2,1)S(1)}, u32[]{:S(2)}) copy-start(bf16[336,1280]{1,0:T(8,128)(2,1)S(1)} %collective-permute-done.9.refs_9_) | copy-start | bytes 2580484
  25.6 2.3 %collective-permute-start.8 = (bf16[2,320,128]{2,1,0:T(8,128)(2,1)S(1)}, bf16[2,320,128]{2,1,0:T(8,128)(2,1)S(1)}, u32[]{:S(2)}, u32[]{:S(2)}) collective-permute-start(bf16[2,320,128]{2,1,0:T(8,128)(2,1)S(1)} %collective-permute-done.3.refs_3_), channel_id=1, source_target_pairs={{0,8},{1,9},{2,10},{3,11},{4,12},{5,13},{6,14},{7,15},{8,0},{9,1},... | collective-permute-start | bytes 491528 | tf_op jit(solution)/shard_map/ppermute | solution.py:95
  27.9 0.9 %copy-start.3 = (bf16[336,1280]{1,0:T(8,128)(2,1)}, bf16[336,1280]{1,0:T(8,128)(2,1)S(1)}, u32[]{:S(2)}) copy-start(bf16[336,1280]{1,0:T(8,128)(2,1)S(1)} %collective-permute-done.10.refs_11_) | copy-start | bytes 2580484
  38.8 1.7 %collective-permute-start.11 = (bf16[4,320,128]{2,1,0:T(8,128)(2,1)S(1)}, bf16[4,320,128]{2,1,0:T(8,128)(2,1)S(1)}, u32[]{:S(2)}, u32[]{:S(2)}) collective-permute-start(bf16[4,320,128]{2,1,0:T(8,128)(2,1)S(1)} %get-tuple-element.28), channel_id=1, source_target_pairs={{0,8},{1,9},{2,10},{3,11},{4,12},{5,13},{6,14},{7,15},{8,0},{9,1},... | collective-permute-start | bytes 983048 | tf_op jit(solution)/shard_map/ppermute | solution.py:95
  40.6 8.3 %collective-permute-start.12 = (bf16[2,320,128]{2,1,0:T(8,128)(2,1)S(1)}, bf16[2,320,128]{2,1,0:T(8,128)(2,1)S(1)}, u32[]{:S(2)}, u32[]{:S(2)}) collective-permute-start(bf16[2,320,128]{2,1,0:T(8,128)(2,1)S(1)} %pad_maximum_fusion), channel_id=1, source_target_pairs={{0,0},{1,8},{2,2},{3,10},{4,4},{5,12},{6,6},{7,14},{8,1},{9,9},{10... | collective-permute-start | bytes 491528 | tf_op jit(solution)/shard_map/ppermute | solution.py:95
  45.1 7.5 %collective-permute-start.13 = (bf16[2,320,128]{2,1,0:T(8,128)(2,1)S(1)}, bf16[2,320,128]{2,1,0:T(8,128)(2,1)S(1)}, u32[]{:S(2)}, u32[]{:S(2)}) collective-permute-start(bf16[2,320,128]{2,1,0:T(8,128)(2,1)S(1)} %pad_maximum_fusion.1), channel_id=1, source_target_pairs={{0,2},{1,10},{2,0},{3,8},{4,6},{5,14},{6,4},{7,12},{8,3},{9,11},{1... | collective-permute-start | bytes 491528 | tf_op jit(solution)/shard_map/ppermute | solution.py:95
  45.2 11.6 %collective-permute-start.14 = (bf16[2,320,128]{2,1,0:T(8,128)(2,1)S(1)}, bf16[2,320,128]{2,1,0:T(8,128)(2,1)S(1)}, u32[]{:S(2)}, u32[]{:S(2)}) collective-permute-start(bf16[2,320,128]{2,1,0:T(8,128)(2,1)S(1)} %pad_maximum_fusion.2), channel_id=1, source_target_pairs={{0,4},{1,12},{2,6},{3,14},{4,0},{5,8},{6,2},{7,10},{8,5},{9,13},{1... | collective-permute-start | bytes 491528 | tf_op jit(solution)/shard_map/ppermute | solution.py:95
  47.8 13.4 %collective-permute-start.15 = (bf16[2,320,128]{2,1,0:T(8,128)(2,1)S(1)}, bf16[2,320,128]{2,1,0:T(8,128)(2,1)S(1)}, u32[]{:S(2)}, u32[]{:S(2)}) collective-permute-start(bf16[2,320,128]{2,1,0:T(8,128)(2,1)S(1)} %pad_maximum_fusion.3), channel_id=1, source_target_pairs={{0,6},{1,14},{2,4},{3,12},{4,2},{5,10},{6,0},{7,8},{8,7},{9,15},{1... | collective-permute-start | bytes 491528 | tf_op jit(solution)/shard_map/ppermute | solution.py:95

commit v3 on v2

--- a/solution.py
+++ b/solution.py
@@ -153,21 +153,21 @@
     )(times, own, taps, projection, film_weight)
 
 
-def join_kernel(levels, *refs):
-    blocks, out = refs[:levels], refs[levels]
+def join_kernel(order, *refs):
+    blocks, out = refs[: len(order)], refs[len(order)]
     frame = lax.axis_index("frame")
     z, x = frame // 2, frame % 2
-    for d in range(levels):
+    for n, d in enumerate(order):
         for k in range(2):
             at = pl.multiple_of(((z ^ d) * 2 + (x ^ k)) * LANES, LANES)
-            out[:, pl.ds(at, LANES)] = blocks[d][k]
-
-
-def join_blocks(blocks):
+            out[:, pl.ds(at, LANES)] = blocks[n][k]
+
+
+def join_blocks(blocks, order):
     levels, width = len(blocks), blocks[0].shape[1]
     vmem = pl.BlockSpec(memory_space=pltpu.VMEM)
     return pl.pallas_call(
-        functools.partial(join_kernel, levels),
+        functools.partial(join_kernel, order),
         out_shape=jax.ShapeDtypeStruct((width, 2 * levels * LANES), BF),
         in_specs=[vmem] * levels,
         out_specs=vmem,
@@ -192,8 +192,8 @@
     kept, given = take(2)
     if borders and not near:
         (border_out,) = take(1)
-    first, weights, skip, unfolded, with_one, with_first, two, three, last, bordering = take(10)
-    sem_x, sem_w, sem_s, sem_o, sem_b = take(5)
+    weights, skip, unfolded, with_one, with_first, two, three, last, bordering = take(9)
+    sem_w, sem_s, sem_b = take(3)
     y, core, z, x = place()
     clip = 2 * y + x
     segment = 2 * y + core
@@ -201,29 +201,25 @@
     upper = jnp.where(z >= levels // 2, 1, 0)
     mirror = upper * (frames - 1)
 
-    loads = []
-    for n, d in enumerate(loaded):
-        for k in range(2):
-            slot = (2 * (z ^ d) + (core ^ k)) ^ mirror
-            source = (turned, swapped)[k][n].at[core]
-            loads.append(pltpu.make_async_copy(source, first.at[slot], sem_x.at[2 * n + k]))
-    if near:
-        loads.append(pltpu.make_async_copy(border_in, bordering, sem_b))
-    for load in loads:
-        load.start()
-
-    for s in range(4):
+    def load_weights(s):
         for b in range(4):
 
             @pl.when(segment ^ s == b)
             def _():
                 pltpu.make_async_copy(packs[b], weights.at[s], sem_w.at[s]).start()
 
+    load_weights(0)
+    if near:
+        border_load = pltpu.make_async_copy(border_in, bordering, sem_b)
+        border_load.start()
     skip_load = pltpu.make_async_copy(skip_in, skip, sem_s)
-    skip_load.start()
 
     def rows_of(step):
         return pl.ds(pl.multiple_of((1 - step + 2 * step * upper) * width, 64), width)
+
+    def lanes_of(d, k):
+        slot = (2 * (z ^ d) + (core ^ k)) ^ mirror
+        return pl.ds(pl.multiple_of(slot * LANES, LANES), LANES)
 
     def span(f, count=1):
         return slice(f * LANES, (f + count) * LANES)
@@ -252,13 +248,13 @@
         rest = rest - gains[-1]
     gains = jnp.concatenate(gains + [jnp.zeros_like(rest)], axis=0).astype(BF)
 
-    for load in loads:
-        load.wait()
     one, zero = with_one.at[64 + width :, :], with_first.at[64 + width :, :]
     states = (zero, one, two, three)
-    for f in range(2 * len(loaded)):
-        zero[:, span(f)] = first[f]
+    for n, d in enumerate(loaded):
+        for k in range(2):
+            zero[:, lanes_of(d, k)] = (turned, swapped)[k][n][core]
     if near:
+        border_load.wait()
         for n, (s, f) in enumerate(borders):
             states[s][:, span(f)] = bordering[n]
 
@@ -273,6 +269,10 @@
                 if low <= f + step < high:
                     unfolded[rows_of(step), span(f + step)] = normed
         pltpu.make_async_copy(packs[0], weights.at[s], sem_w.at[s]).wait()
+        if s < 3:
+            load_weights(s + 1)
+        if s == 0:
+            skip_load.start()
         film = 1.0 + column_of(weights[s, width:, 0:width], [clip, 4 + clip])
         film = jnp.concatenate([film] * (high - low), axis=1)
         cols = span(low, high - low)
@@ -292,37 +292,27 @@
             projection = jnp.concatenate([projection, skip[s - 2].T], axis=1)
         total = source[:, cols].astype(F32)
         total = (total + jnp.dot(projection, right, preferred_element_type=F32)).astype(BF)
-        if s < 3:
-            states[s + 1][:, cols] = total
-        else:
-            for f in range(low, high):
-                last[f] = total[:, span(f - low)]
-    stores = []
+        (one, two, three, last)[s][:, cols] = total
     for n, d in enumerate(dests):
         for k, out in enumerate((kept, given)):
-            slot = (2 * (z ^ d) + (core ^ k)) ^ mirror
-            stores.append(
-                pltpu.make_async_copy(last.at[slot], out.at[n], sem_o.at[2 * n + k])
-            )
+            out[n] = last[:, lanes_of(d, k)]
     if borders and not near:
         for n, (s, f) in enumerate(borders):
-            bordering[n] = states[s][:, span(f)]
-        stores.append(pltpu.make_async_copy(bordering, border_out, sem_b))
-    for store in stores:
-        store.start()
-    for store in stores:
-        store.wait()
-
-
-def run_sections(spans, dests, borders, turned, swapped, weights, skip, gain, border=None):
+            border_out[n] = states[s][:, span(f)]
+
+
+def run_sections(
+    spans, dests, borders, loaded, turned, swapped, weights, skip, gain, border=None
+):
     levels = lax.axis_size("frame") // 2
     frames = 2 * levels
     width = gain.shape[1]
     columns = frames * LANES
     hbm = pl.BlockSpec(memory_space=pltpu.HBM)
     vmem = pl.BlockSpec(memory_space=pltpu.VMEM)
-    given_out = [jax.ShapeDtypeStruct((len(dests), width, LANES), BF)] * 2
-    blocks, inputs = [*turned, *swapped], [*weights, skip]
+    given_out = [pltpu.VMEM((len(dests), width, LANES), BF)] * 2
+    blocks = [*turned, *swapped]
+    inputs = [*pin(weights[:3], pltpu.HBM), *pin(weights[3:], pltpu.VMEM), *pin([skip], pltpu.HBM)]
     after = []
     if border is not None:
         after = pin([border], pltpu.HBM)
@@ -331,16 +321,16 @@
     flops = sum(high - low for low, high in spans) * LANES * 2 * 5 * width * width
     return pl.pallas_call(
         functools.partial(
-            sections_kernel, spans, dests, borders, levels, width, list(range(len(turned)))
+            sections_kernel, spans, dests, borders, levels, width, loaded
         ),
         out_shape=given_out,
         in_specs=[vmem] * len(blocks)
-        + [hbm] * len(inputs)
+        + [hbm] * 3
+        + [vmem, hbm]
         + [pl.BlockSpec(memory_space=pltpu.VMEM)]
         + [hbm] * len(after),
-        out_specs=[hbm] * len(given_out),
+        out_specs=[vmem] * len(given_out),
         scratch_shapes=[
-            pltpu.VMEM((frames, width, LANES), BF),
             pltpu.VMEM((4, width + FILM_ROWS, 4 * width), BF),
             pltpu.VMEM((2, width, width), BF),
             pltpu.VMEM((3 * width + 64, columns), BF),
@@ -348,74 +338,50 @@
             pltpu.VMEM((2 * width + 64, columns), BF),
             pltpu.VMEM((width, columns), BF),
             pltpu.VMEM((width, columns), BF),
-            pltpu.VMEM((frames, width, LANES), BF),
+            pltpu.VMEM((width, columns), BF),
             pltpu.VMEM((6, width, LANES), BF),
-            pltpu.SemaphoreType.DMA((frames,)),
             pltpu.SemaphoreType.DMA((4,)),
             pltpu.SemaphoreType.DMA,
-            pltpu.SemaphoreType.DMA((frames,)),
             pltpu.SemaphoreType.DMA,
         ],
         compiler_params=pltpu.CompilerParams(vmem_limit_bytes=40 << 20),
         cost_estimate=pl.CostEstimate(flops=flops, bytes_accessed=4 << 20, transcendentals=0),
         name="sections",
-    )(*pin(blocks, pltpu.VMEM), *pin(inputs, pltpu.HBM), gain, *after)
-
-
-def send_back(kept, given, dests):
-    swapped = swap_cores(given)
-    blocks = [jnp.stack([kept[n], swapped[n]]) for n in range(len(dests))]
-    return [turn(block, d) for block, d in zip(blocks, dests, strict=True)], blocks
-
-
-SPLIT = False
+    )(*pin(blocks, pltpu.VMEM), *inputs, gain, *after)
+
+
+IN_ORDER = (2, 3, 1, 0)
+OUT_ORDER = (2, 3, 1, 0)
 
 
 def block_shards(clips, timesteps, gain, temporal_weight, film_weight, out_weight, skip_weight):
     levels = lax.axis_size("frame") // 2
-    order = [3, 2, 1, 0]
 
     *cut, pack0 = pack_and_cut(
         timesteps, clips[0, 0], temporal_weight[0], out_weight[0], film_weight[0], levels
     )
     pack2 = swap_planes(pack0)
-    turned = [None] * levels
-    for d in order:
-        turned[d] = turn(cut[d], d)
+    turned = [turn(cut[d], d) for d in IN_ORDER]
     pack1 = swap_cores(pack0)
-
-    turned, pack2 = lax.optimization_barrier((turned, pack2))
+    pack2, *turned = lax.optimization_barrier((pack2, *turned))
+    pack3 = swap_cores(pack2)
     swapped = [swap_cores(block) for block in turned]
-    pack3 = swap_cores(pack2)
-
-    weights = [pack0, pack1, pack2, pack3]
-    frames = 2 * levels
-    if SPLIT:
-        borders = [(1, 1), (1, 2), (2, 2), (2, 3), (3, 3), (3, 4)]
-        far = [(s + 1, frames) for s in range(4)]
-        kept, given, border = run_sections(
-            far, [2, 3], borders, turned, swapped, weights, skip_weight, gain
-        )
-        back, blocks = send_back(kept, given, [2, 3])
-        border, _ = lax.optimization_barrier((border, blocks))
-        kept, given = run_sections(
-            [(0, s + 1) for s in range(4)],
-            [0, 1],
-            borders,
-            turned[:2],
-            swapped[:2],
-            weights,
-            skip_weight,
-            gain,
-            border,
-        )
-        back = send_back(kept, given, [0, 1])[0] + back
-    else:
-        kept, given = run_sections(
-            [(0, frames)] * 4, [0, 1, 2, 3], None, turned, swapped, weights, skip_weight, gain
-        )
-        back = send_back(kept, given, [0, 1, 2, 3])[0]
-    return join_blocks(back)[None, None]
+
+    kept, given = run_sections(
+        [(0, 2 * levels)] * 4,
+        OUT_ORDER,
+        None,
+        IN_ORDER,
+        turned,
+        swapped,
+        [pack0, pack1, pack2, pack3],
+        skip_weight,
+        gain,
+    )
+    swapped = swap_cores(given)
+    blocks = [jnp.stack([kept[n], swapped[n]]) for n in range(levels)]
+    back = [turn(block, d) for block, d in zip(blocks, OUT_ORDER, strict=True)]
+    return join_blocks(back, OUT_ORDER)[None, None]
 
 
 def solution(mesh):

time: 62.3 us -> 57.4 us (0.921)
  waiting for transfers between devices: 28.5 us -> 23.7 us
  starting transfers between devices: 18.5 us -> 20.9 us
  Pallas kernels: 14 us -> 12.3 us
  local copies, waits for them, and re-layouts: 0.96 us -> 0.06 us
    ppermute x16, waiting for transfers between devices: 28.5 us -> 23.7 us  [move(): return lax.ppermute(array, ('segment', 'frame'), pairs)]
    ppermute x16, starting transfers between devices: 18.5 us -> 20.9 us  [move(): return lax.ppermute(array, ('segment', 'frame'), pairs)]
    pallas_call x1, Pallas kernels: 9.97 us -> 8.31 us  [run_sections(): pl.pallas_call(functools.partial(sections_kernel, spans, dests, borders,...]
    unnamed x8 -> x6, local copies, waits for them, and re-layouts: 0.92 us -> 0.01 us
  transfers between devices with their start and end apart: 16 -> 16, of which waited for: 11 -> 10; matrix products, arithmetic and copies ran while one was open for 0% -> 0% of each run, Pallas kernels for 0% -> 0%
where the time goes in v3:
time: 57.4 us; the launch traced here: 57.2 us
  waiting for transfers between devices  23.7 us (41%)
  starting transfers between devices  20.9 us (36%)
  Pallas kernels  12.3 us (21%)
    ppermute x16, waiting for transfers between devices, move(): return lax.ppermute(array, ('segment', 'frame'), pairs)  23.7 us
    ppermute x16, starting transfers between devices, move(): return lax.ppermute(array, ('segment', 'frame'), pairs)  20.9 us
    pallas_call x1, Pallas kernels, run_sections(): pl.pallas_call(functools.partial(sections_kernel, spans, dests, borders,...  8.31 us
    pallas_call x1, Pallas kernels, pack_and_cut(): pl.pallas_call(functools.partial(pack_kernel, levels), out_shape=[jax.Sha...  2.96 us
  transfers between devices with their start and end apart: 16, of which 10 were waited for; matrix products, arithmetic and copies ran while one was open for 0% of the time, Pallas kernels for 0%

profile of v3, /device:TPU:17, one launch (start us, length us, event | category | flops | bytes accessed | tf_op | source)
XLA Modules:
  0.0 57.2 jit_solution(6458541539997601297)
XLA Ops:
  0.0 3.0 %pack.1 = (bf16[2,320,128]{2,1,0:T(8,128)(2,1)}, bf16[2,320,128]{2,1,0:T(8,128)(2,1)}, bf16[2,320,128]{2,1,0:T(8,128)(2,1)}, bf16[2,320,128]{2,1,0:T(8,128)(2,1)}, bf16[336,1280]{1,0:T(8,128)(2,1)}) custom-call(s32[4]{0:T(128)} %times_ref.1, bf16[320,1024]{1,0:T(8,128)(2,1)} %bitcast.6, bf16[3,320,320]{2,1,0:T(8,128)(2,1)} %bitcast.5, ...), custom_call_target="tpu_custom_call" | custom-call | tf_op jit(solution)/shard_map/pack/pallas_call | solution.py:146
  3.0 1.2 %collective-permute-start = (bf16[336,1280]{1,0:T(8,128)(2,1)}, bf16[336,1280]{1,0:T(8,128)(2,1)S(1)}, u32[]{:S(2)}, u32[]{:S(2)}) collective-permute-start(bf16[336,1280]{1,0:T(8,128)(2,1)} %get-tuple-element.17.refs_8_), channel_id=1, source_target_pairs={{0,16},{1,17},{2,18},{3,19},{4,20},{5,21},{6,22},{7,23},{8,24},{9,... | collective-permute-start | bytes 2580488 | tf_op jit(solution)/shard_map/ppermute | solution.py:95
  4.2 1.8 %collective-permute-start.1 = (bf16[2,320,128]{2,1,0:T(8,128)(2,1)}, bf16[2,320,128]{2,1,0:T(8,128)(2,1)S(1)}, u32[]{:S(2)}, u32[]{:S(2)}) collective-permute-start(bf16[2,320,128]{2,1,0:T(8,128)(2,1)} %get-tuple-element.18), channel_id=1, source_target_pairs={{0,4},{1,12},{2,6},{3,14},{4,0},{5,8},{6,2},{7,10},{8,5},{9,13},{1... | collective-permute-start | bytes 491528 | tf_op jit(solution)/shard_map/ppermute | solution.py:95
  6.0 1.8 %collective-permute-start.2 = (bf16[2,320,128]{2,1,0:T(8,128)(2,1)}, bf16[2,320,128]{2,1,0:T(8,128)(2,1)S(1)}, u32[]{:S(2)}, u32[]{:S(2)}) collective-permute-start(bf16[2,320,128]{2,1,0:T(8,128)(2,1)} %get-tuple-element.19), channel_id=1, source_target_pairs={{0,6},{1,14},{2,4},{3,12},{4,2},{5,10},{6,0},{7,8},{8,7},{9,15},{1... | collective-permute-start | bytes 491528 | tf_op jit(solution)/shard_map/ppermute | solution.py:95
  7.9 2.8 %collective-permute-start.3 = (bf16[2,320,128]{2,1,0:T(8,128)(2,1)}, bf16[2,320,128]{2,1,0:T(8,128)(2,1)S(1)}, u32[]{:S(2)}, u32[]{:S(2)}) collective-permute-start(bf16[2,320,128]{2,1,0:T(8,128)(2,1)} %get-tuple-element.20), channel_id=1, source_target_pairs={{0,2},{1,10},{2,0},{3,8},{4,6},{5,14},{6,4},{7,12},{8,3},{9,11},{1... | collective-permute-start | bytes 491528 | tf_op jit(solution)/shard_map/ppermute | solution.py:95
  10.7 1.9 %collective-permute-start.4 = (bf16[2,320,128]{2,1,0:T(8,128)(2,1)}, bf16[2,320,128]{2,1,0:T(8,128)(2,1)S(1)}, u32[]{:S(2)}, u32[]{:S(2)}) collective-permute-start(bf16[2,320,128]{2,1,0:T(8,128)(2,1)} %get-tuple-element.21), channel_id=1, source_target_pairs={{0,0},{1,8},{2,2},{3,10},{4,4},{5,12},{6,6},{7,14},{8,1},{9,9},{10... | collective-permute-start | bytes 491528 | tf_op jit(solution)/shard_map/ppermute | solution.py:95
  12.6 4.7 %collective-permute-done.1.refs_0_ = bf16[2,320,128]{2,1,0:T(8,128)(2,1)S(1)} collective-permute-done((bf16[2,320,128]{2,1,0:T(8,128)(2,1)}, bf16[2,320,128]{2,1,0:T(8,128)(2,1)S(1)}, u32[]{:S(2)}, u32[]{:S(2)}) %collective-permute-start.1) | collective-permute-done | bytes 163872 | tf_op jit(solution)/shard_map/ppermute | solution.py:95
  17.3 5.4 %collective-permute-done.2.refs_1_ = bf16[2,320,128]{2,1,0:T(8,128)(2,1)S(1)} collective-permute-done((bf16[2,320,128]{2,1,0:T(8,128)(2,1)}, bf16[2,320,128]{2,1,0:T(8,128)(2,1)S(1)}, u32[]{:S(2)}, u32[]{:S(2)}) %collective-permute-start.2) | collective-permute-done | bytes 163872 | tf_op jit(solution)/shard_map/ppermute | solution.py:95
  22.8 0.4 collective-permute-done.refs_10_
  23.2 1.5 %collective-permute-start.10 = (bf16[336,1280]{1,0:T(8,128)(2,1)S(1)}, bf16[336,1280]{1,0:T(8,128)(2,1)S(1)}, u32[]{:S(2)}, u32[]{:S(2)}) collective-permute-start(bf16[336,1280]{1,0:T(8,128)(2,1)S(1)} %collective-permute-done.refs_10_), channel_id=1, source_target_pairs={{0,8},{1,9},{2,10},{3,11},{4,12},{5,13},{6,14},{7,15},{8,0},{9,1},... | collective-permute-start | bytes 2580488 | tf_op jit(solution)/shard_map/ppermute | solution.py:95
  24.7 0.5 collective-permute-start.6
  25.2 0.5 collective-permute-start.8
  25.7 1.2 %collective-permute-done.5.refs_4_ = bf16[2,320,128]{2,1,0:T(8,128)(2,1)S(1)} collective-permute-done((bf16[2,320,128]{2,1,0:T(8,128)(2,1)S(1)}, bf16[2,320,128]{2,1,0:T(8,128)(2,1)S(1)}, u32[]{:S(2)}, u32[]{:S(2)}) %collective-permute-start.5) | collective-permute-done | bytes 163872 | tf_op jit(solution)/shard_map/ppermute | solution.py:95
  27.2 0.2 collective-permute-done.7.refs_6_
  27.7 8.3 %sections.1 = (bf16[4,320,128]{2,1,0:T(8,128)(2,1)S(1)}, bf16[4,320,128]{2,1,0:T(8,128)(2,1)S(1)}) custom-call(bf16[2,320,128]{2,1,0:T(8,128)(2,1)S(1)} %collective-permute-done.1.refs_0_, bf16[2,320,128]{2,1,0:T(8,128)(2,1)S(1)} %collective-permute-done.2.refs_1_, bf16[2,320,128]{2,1,0:T(8,128)(2,1)S(1)} %collective-permute-done.3.refs_2_, ...), custom_call_target="tpu_custom_call" | custom-call | flops 4194304000 | bytes 4194304 | tf_op jit(solution)/shard_map/sections/pallas_call | solution.py:322
  36.0 0.4 collective-permute-start.11
  36.5 1.2 %collective-permute-done.11 = bf16[4,320,128]{2,1,0:T(8,128)(2,1)S(1)} collective-permute-done((bf16[4,320,128]{2,1,0:T(8,128)(2,1)S(1)}, bf16[4,320,128]{2,1,0:T(8,128)(2,1)S(1)}, u32[]{:S(2)}, u32[]{:S(2)}) %collective-permute-start.11) | collective-permute-done | bytes 327712 | tf_op jit(solution)/shard_map/ppermute | solution.py:95
  37.8 1.3 %collective-permute-start.12 = (bf16[2,320,128]{2,1,0:T(8,128)(2,1)S(1)}, bf16[2,320,128]{2,1,0:T(8,128)(2,1)S(1)}, u32[]{:S(2)}, u32[]{:S(2)}) collective-permute-start(bf16[2,320,128]{2,1,0:T(8,128)(2,1)S(1)} %pad_maximum_fusion), channel_id=1, source_target_pairs={{0,4},{1,12},{2,6},{3,14},{4,0},{5,8},{6,2},{7,10},{8,5},{9,13},{1... | collective-permute-start | bytes 491528 | tf_op jit(solution)/shard_map/ppermute | solution.py:95
  39.1 2.5 %collective-permute-start.13 = (bf16[2,320,128]{2,1,0:T(8,128)(2,1)S(1)}, bf16[2,320,128]{2,1,0:T(8,128)(2,1)S(1)}, u32[]{:S(2)}, u32[]{:S(2)}) collective-permute-start(bf16[2,320,128]{2,1,0:T(8,128)(2,1)S(1)} %pad_maximum_fusion.1), channel_id=1, source_target_pairs={{0,6},{1,14},{2,4},{3,12},{4,2},{5,10},{6,0},{7,8},{8,7},{9,15},{1... | collective-permute-start | bytes 491528 | tf_op jit(solution)/shard_map/ppermute | solution.py:95
  41.6 2.3 %collective-permute-start.14 = (bf16[2,320,128]{2,1,0:T(8,128)(2,1)S(1)}, bf16[2,320,128]{2,1,0:T(8,128)(2,1)S(1)}, u32[]{:S(2)}, u32[]{:S(2)}) collective-permute-start(bf16[2,320,128]{2,1,0:T(8,128)(2,1)S(1)} %pad_maximum_fusion.2), channel_id=1, source_target_pairs={{0,2},{1,10},{2,0},{3,8},{4,6},{5,14},{6,4},{7,12},{8,3},{9,11},{1... | collective-permute-start | bytes 491528 | tf_op jit(solution)/shard_map/ppermute | solution.py:95
  43.9 2.2 %collective-permute-start.15 = (bf16[2,320,128]{2,1,0:T(8,128)(2,1)S(1)}, bf16[2,320,128]{2,1,0:T(8,128)(2,1)S(1)}, u32[]{:S(2)}, u32[]{:S(2)}) collective-permute-start(bf16[2,320,128]{2,1,0:T(8,128)(2,1)S(1)} %pad_maximum_fusion.3), channel_id=1, source_target_pairs={{0,0},{1,8},{2,2},{3,10},{4,4},{5,12},{6,6},{7,14},{8,1},{9,9},{10... | collective-permute-start | bytes 491528 | tf_op jit(solution)/shard_map/ppermute | solution.py:95
  46.1 4.0 %collective-permute-done.12.refs_0_ = bf16[2,320,128]{2,1,0:T(8,128)(2,1)S(1)} collective-permute-done((bf16[2,320,128]{2,1,0:T(8,128)(2,1)S(1)}, bf16[2,320,128]{2,1,0:T(8,128)(2,1)S(1)}, u32[]{:S(2)}, u32[]{:S(2)}) %collective-permute-start.12) | collective-permute-done | bytes 163872 | tf_op jit(solution)/shard_map/ppermute | solution.py:95
  50.1 6.1 %collective-permute-done.13.refs_1_ = bf16[2,320,128]{2,1,0:T(8,128)(2,1)S(1)} collective-permute-done((bf16[2,320,128]{2,1,0:T(8,128)(2,1)S(1)}, bf16[2,320,128]{2,1,0:T(8,128)(2,1)S(1)}, u32[]{:S(2)}, u32[]{:S(2)}) %collective-permute-start.13) | collective-permute-done | bytes 163872 | tf_op jit(solution)/shard_map/ppermute | solution.py:95
  56.2 1.0 %join.1 = bf16[320,1024]{1,0:T(8,128)(2,1)} custom-call(bf16[2,320,128]{2,1,0:T(8,128)(2,1)S(1)} %collective-permute-done.12.refs_0_, bf16[2,320,128]{2,1,0:T(8,128)(2,1)S(1)} %collective-permute-done.13.refs_1_, bf16[2,320,128]{2,1,0:T(8,128)(2,1)S(1)} %collective-permute-done.14.refs_2_, bf16[2,320,128]{2,1,0:T(8,128)(2,1)S(1)} %collective-permute-done.15.refs_3_), custom_call_target="tpu_custom_call" | custom-call | tf_op jit(solution)/shard_map/join/pallas_call | solution.py:169
  (23 shorter events, 0.6 us)
Async XLA Ops:
  3.0 24.7 %copy-start = (f32[4,320]{1,0:T(4,128)S(1)}, f32[4,320]{1,0:T(4,128)}, u32[]{:S(2)}) copy-start(f32[4,320]{1,0:T(4,128)} %refs_13_.1) | copy-start | bytes 15364
  3.0 20.2 %collective-permute-start = (bf16[336,1280]{1,0:T(8,128)(2,1)}, bf16[336,1280]{1,0:T(8,128)(2,1)S(1)}, u32[]{:S(2)}, u32[]{:S(2)}) collective-permute-start(bf16[336,1280]{1,0:T(8,128)(2,1)} %get-tuple-element.17.refs_8_), channel_id=1, source_target_pairs={{0,16},{1,17},{2,18},{3,19},{4,20},{5,21},{6,22},{7,23},{8,24},{9,... | collective-permute-start | bytes 2580488 | tf_op jit(solution)/shard_map/ppermute | solution.py:95
  4.2 13.1 %collective-permute-start.1 = (bf16[2,320,128]{2,1,0:T(8,128)(2,1)}, bf16[2,320,128]{2,1,0:T(8,128)(2,1)S(1)}, u32[]{:S(2)}, u32[]{:S(2)}) collective-permute-start(bf16[2,320,128]{2,1,0:T(8,128)(2,1)} %get-tuple-element.18), channel_id=1, source_target_pairs={{0,4},{1,12},{2,6},{3,14},{4,0},{5,8},{6,2},{7,10},{8,5},{9,13},{1... | collective-permute-start | bytes 491528 | tf_op jit(solution)/shard_map/ppermute | solution.py:95
  6.0 16.7 %collective-permute-start.2 = (bf16[2,320,128]{2,1,0:T(8,128)(2,1)}, bf16[2,320,128]{2,1,0:T(8,128)(2,1)S(1)}, u32[]{:S(2)}, u32[]{:S(2)}) collective-permute-start(bf16[2,320,128]{2,1,0:T(8,128)(2,1)} %get-tuple-element.19), channel_id=1, source_target_pairs={{0,6},{1,14},{2,4},{3,12},{4,2},{5,10},{6,0},{7,8},{8,7},{9,15},{1... | collective-permute-start | bytes 491528 | tf_op jit(solution)/shard_map/ppermute | solution.py:95
  7.9 14.9 %collective-permute-start.3 = (bf16[2,320,128]{2,1,0:T(8,128)(2,1)}, bf16[2,320,128]{2,1,0:T(8,128)(2,1)S(1)}, u32[]{:S(2)}, u32[]{:S(2)}) collective-permute-start(bf16[2,320,128]{2,1,0:T(8,128)(2,1)} %get-tuple-element.20), channel_id=1, source_target_pairs={{0,2},{1,10},{2,0},{3,8},{4,6},{5,14},{6,4},{7,12},{8,3},{9,11},{1... | collective-permute-start | bytes 491528 | tf_op jit(solution)/shard_map/ppermute | solution.py:95
  10.7 12.1 %collective-permute-start.4 = (bf16[2,320,128]{2,1,0:T(8,128)(2,1)}, bf16[2,320,128]{2,1,0:T(8,128)(2,1)S(1)}, u32[]{:S(2)}, u32[]{:S(2)}) collective-permute-start(bf16[2,320,128]{2,1,0:T(8,128)(2,1)} %get-tuple-element.21), channel_id=1, source_target_pairs={{0,0},{1,8},{2,2},{3,10},{4,4},{5,12},{6,6},{7,14},{8,1},{9,9},{10... | collective-permute-start | bytes 491528 | tf_op jit(solution)/shard_map/ppermute | solution.py:95
  17.3 7.9 %collective-permute-start.9 = (bf16[336,1280]{1,0:T(8,128)(2,1)}, bf16[336,1280]{1,0:T(8,128)(2,1)S(1)}, u32[]{:S(2)}, u32[]{:S(2)}) collective-permute-start(bf16[336,1280]{1,0:T(8,128)(2,1)} %get-tuple-element.17.refs_8_), channel_id=1, source_target_pairs={{0,8},{1,9},{2,10},{3,11},{4,12},{5,13},{6,14},{7,15},{8,0},{9,1},... | collective-permute-start | bytes 2580488 | tf_op jit(solution)/shard_map/ppermute | solution.py:95
  23.2 4.5 %copy-start.1 = (bf16[336,1280]{1,0:T(8,128)(2,1)}, bf16[336,1280]{1,0:T(8,128)(2,1)S(1)}, u32[]{:S(2)}) copy-start(bf16[336,1280]{1,0:T(8,128)(2,1)S(1)} %collective-permute-done.refs_10_) | copy-start | bytes 2580484
  23.2 4.5 %collective-permute-start.10 = (bf16[336,1280]{1,0:T(8,128)(2,1)S(1)}, bf16[336,1280]{1,0:T(8,128)(2,1)S(1)}, u32[]{:S(2)}, u32[]{:S(2)}) collective-permute-start(bf16[336,1280]{1,0:T(8,128)(2,1)S(1)} %collective-permute-done.refs_10_), channel_id=1, source_target_pairs={{0,8},{1,9},{2,10},{3,11},{4,12},{5,13},{6,14},{7,15},{8,0},{9,1},... | collective-permute-start | bytes 2580488 | tf_op jit(solution)/shard_map/ppermute | solution.py:95
  24.7 2.3 %collective-permute-start.5 = (bf16[2,320,128]{2,1,0:T(8,128)(2,1)S(1)}, bf16[2,320,128]{2,1,0:T(8,128)(2,1)S(1)}, u32[]{:S(2)}, u32[]{:S(2)}) collective-permute-start(bf16[2,320,128]{2,1,0:T(8,128)(2,1)S(1)} %collective-permute-done.1.refs_0_), channel_id=1, source_target_pairs={{0,8},{1,9},{2,10},{3,11},{4,12},{5,13},{6,14},{7,15},{8,0},{9,1},... | collective-permute-start | bytes 491528 | tf_op jit(solution)/shard_map/ppermute | solution.py:95
  24.7 2.5 %collective-permute-start.6 = (bf16[2,320,128]{2,1,0:T(8,128)(2,1)S(1)}, bf16[2,320,128]{2,1,0:T(8,128)(2,1)S(1)}, u32[]{:S(2)}, u32[]{:S(2)}) collective-permute-start(bf16[2,320,128]{2,1,0:T(8,128)(2,1)S(1)} %collective-permute-done.2.refs_1_), channel_id=1, source_target_pairs={{0,8},{1,9},{2,10},{3,11},{4,12},{5,13},{6,14},{7,15},{8,0},{9,1},... | collective-permute-start | bytes 491528 | tf_op jit(solution)/shard_map/ppermute | solution.py:95
  25.2 2.2 %collective-permute-start.7 = (bf16[2,320,128]{2,1,0:T(8,128)(2,1)S(1)}, bf16[2,320,128]{2,1,0:T(8,128)(2,1)S(1)}, u32[]{:S(2)}, u32[]{:S(2)}) collective-permute-start(bf16[2,320,128]{2,1,0:T(8,128)(2,1)S(1)} %collective-permute-done.3.refs_2_), channel_id=1, source_target_pairs={{0,8},{1,9},{2,10},{3,11},{4,12},{5,13},{6,14},{7,15},{8,0},{9,1},... | collective-permute-start | bytes 491528 | tf_op jit(solution)/shard_map/ppermute | solution.py:95
  25.2 2.4 %copy-start.2 = (bf16[336,1280]{1,0:T(8,128)(2,1)}, bf16[336,1280]{1,0:T(8,128)(2,1)S(1)}, u32[]{:S(2)}) copy-start(bf16[336,1280]{1,0:T(8,128)(2,1)S(1)} %collective-permute-done.9.refs_9_) | copy-start | bytes 2580484
  25.2 2.4 %collective-permute-start.8 = (bf16[2,320,128]{2,1,0:T(8,128)(2,1)S(1)}, bf16[2,320,128]{2,1,0:T(8,128)(2,1)S(1)}, u32[]{:S(2)}, u32[]{:S(2)}) collective-permute-start(bf16[2,320,128]{2,1,0:T(8,128)(2,1)S(1)} %collective-permute-done.4.refs_3_), channel_id=1, source_target_pairs={{0,8},{1,9},{2,10},{3,11},{4,12},{5,13},{6,14},{7,15},{8,0},{9,1},... | collective-permute-start | bytes 491528 | tf_op jit(solution)/shard_map/ppermute | solution.py:95
  36.0 1.7 %collective-permute-start.11 = (bf16[4,320,128]{2,1,0:T(8,128)(2,1)S(1)}, bf16[4,320,128]{2,1,0:T(8,128)(2,1)S(1)}, u32[]{:S(2)}, u32[]{:S(2)}) collective-permute-start(bf16[4,320,128]{2,1,0:T(8,128)(2,1)S(1)} %get-tuple-element.28), channel_id=1, source_target_pairs={{0,8},{1,9},{2,10},{3,11},{4,12},{5,13},{6,14},{7,15},{8,0},{9,1},... | collective-permute-start | bytes 983048 | tf_op jit(solution)/shard_map/ppermute | solution.py:95
  37.8 12.3 %collective-permute-start.12 = (bf16[2,320,128]{2,1,0:T(8,128)(2,1)S(1)}, bf16[2,320,128]{2,1,0:T(8,128)(2,1)S(1)}, u32[]{:S(2)}, u32[]{:S(2)}) collective-permute-start(bf16[2,320,128]{2,1,0:T(8,128)(2,1)S(1)} %pad_maximum_fusion), channel_id=1, source_target_pairs={{0,4},{1,12},{2,6},{3,14},{4,0},{5,8},{6,2},{7,10},{8,5},{9,13},{1... | collective-permute-start | bytes 491528 | tf_op jit(solution)/shard_map/ppermute | solution.py:95
  39.1 17.1 %collective-permute-start.13 = (bf16[2,320,128]{2,1,0:T(8,128)(2,1)S(1)}, bf16[2,320,128]{2,1,0:T(8,128)(2,1)S(1)}, u32[]{:S(2)}, u32[]{:S(2)}) collective-permute-start(bf16[2,320,128]{2,1,0:T(8,128)(2,1)S(1)} %pad_maximum_fusion.1), channel_id=1, source_target_pairs={{0,6},{1,14},{2,4},{3,12},{4,2},{5,10},{6,0},{7,8},{8,7},{9,15},{1... | collective-permute-start | bytes 491528 | tf_op jit(solution)/shard_map/ppermute | solution.py:95
  41.6 14.6 %collective-permute-start.14 = (bf16[2,320,128]{2,1,0:T(8,128)(2,1)S(1)}, bf16[2,320,128]{2,1,0:T(8,128)(2,1)S(1)}, u32[]{:S(2)}, u32[]{:S(2)}) collective-permute-start(bf16[2,320,128]{2,1,0:T(8,128)(2,1)S(1)} %pad_maximum_fusion.2), channel_id=1, source_target_pairs={{0,2},{1,10},{2,0},{3,8},{4,6},{5,14},{6,4},{7,12},{8,3},{9,11},{1... | collective-permute-start | bytes 491528 | tf_op jit(solution)/shard_map/ppermute | solution.py:95
  43.9 12.2 %collective-permute-start.15 = (bf16[2,320,128]{2,1,0:T(8,128)(2,1)S(1)}, bf16[2,320,128]{2,1,0:T(8,128)(2,1)S(1)}, u32[]{:S(2)}, u32[]{:S(2)}) collective-permute-start(bf16[2,320,128]{2,1,0:T(8,128)(2,1)S(1)} %pad_maximum_fusion.3), channel_id=1, source_target_pairs={{0,0},{1,8},{2,2},{3,10},{4,4},{5,12},{6,6},{7,14},{8,1},{9,9},{10... | collective-permute-start | bytes 491528 | tf_op jit(solution)/shard_map/ppermute | solution.py:95

commit v4 on v3

--- a/solution.py
+++ b/solution.py
@@ -145,31 +145,32 @@
     vmem = pl.BlockSpec(memory_space=pltpu.VMEM)
     return pl.pallas_call(
         functools.partial(pack_kernel, levels),
-        out_shape=[jax.ShapeDtypeStruct((2, width, LANES), BF)] * levels
-        + [jax.ShapeDtypeStruct((width + FILM_ROWS, 4 * width), BF)],
+        out_shape=[pltpu.VMEM((2, width, LANES), BF)] * levels
+        + [pltpu.VMEM((width + FILM_ROWS, 4 * width), BF)],
         in_specs=[pl.BlockSpec(memory_space=pltpu.SMEM)] + [vmem] * 4,
         out_specs=[vmem] * (levels + 1),
         name="pack",
     )(times, own, taps, projection, film_weight)
 
 
-def join_kernel(order, *refs):
-    blocks, out = refs[: len(order)], refs[len(order)]
+def join_kernel(parts, *refs):
+    blocks, out = refs[: len(parts)], refs[len(parts)]
     frame = lax.axis_index("frame")
     z, x = frame // 2, frame % 2
-    for n, d in enumerate(order):
-        for k in range(2):
+    for block, (d, halves) in zip(blocks, parts, strict=True):
+        for n, k in enumerate(halves):
             at = pl.multiple_of(((z ^ d) * 2 + (x ^ k)) * LANES, LANES)
-            out[:, pl.ds(at, LANES)] = blocks[n][k]
-
-
-def join_blocks(blocks, order):
-    levels, width = len(blocks), blocks[0].shape[1]
+            out[:, pl.ds(at, LANES)] = block[n]
+
+
+def join_blocks(blocks, parts):
+    width = blocks[0].shape[1]
+    columns = sum(len(halves) for _, halves in parts) * LANES
     vmem = pl.BlockSpec(memory_space=pltpu.VMEM)
     return pl.pallas_call(
-        functools.partial(join_kernel, order),
-        out_shape=jax.ShapeDtypeStruct((width, 2 * levels * LANES), BF),
-        in_specs=[vmem] * levels,
+        functools.partial(join_kernel, parts),
+        out_shape=jax.ShapeDtypeStruct((width, columns), BF),
+        in_specs=[vmem] * len(blocks),
         out_specs=vmem,
         name="join",
     )(*pin(blocks, pltpu.VMEM))
@@ -312,7 +313,8 @@
     vmem = pl.BlockSpec(memory_space=pltpu.VMEM)
     given_out = [pltpu.VMEM((len(dests), width, LANES), BF)] * 2
     blocks = [*turned, *swapped]
-    inputs = [*pin(weights[:3], pltpu.HBM), *pin(weights[3:], pltpu.VMEM), *pin([skip], pltpu.HBM)]
+    places = [pltpu.VMEM, pltpu.HBM, pltpu.HBM, pltpu.VMEM, pltpu.HBM]
+    inputs = [pin([a], place)[0] for a, place in zip([*weights, skip], places, strict=True)]
     after = []
     if border is not None:
         after = pin([border], pltpu.HBM)
@@ -325,8 +327,7 @@
         ),
         out_shape=given_out,
         in_specs=[vmem] * len(blocks)
-        + [hbm] * 3
-        + [vmem, hbm]
+        + [pl.BlockSpec(memory_space=place) for place in places]
         + [pl.BlockSpec(memory_space=pltpu.VMEM)]
         + [hbm] * len(after),
         out_specs=[vmem] * len(given_out),
@@ -352,6 +353,7 @@
 
 IN_ORDER = (2, 3, 1, 0)
 OUT_ORDER = (2, 3, 1, 0)
+OUT_PARTS = ((0, (0, 1)), (1, (0, 1)), (3, (1,)), (2, (1,)), (3, (0,)), (2, (0,)))
 
 
 def block_shards(clips, timesteps, gain, temporal_weight, film_weight, out_weight, skip_weight):
@@ -379,9 +381,11 @@
         gain,
     )
     swapped = swap_cores(given)
-    blocks = [jnp.stack([kept[n], swapped[n]]) for n in range(levels)]
-    back = [turn(block, d) for block, d in zip(blocks, OUT_ORDER, strict=True)]
-    return join_blocks(back, OUT_ORDER)[None, None]
+    back = []
+    for d, halves in OUT_PARTS:
+        n = OUT_ORDER.index(d)
+        back.append(turn(jnp.stack([(kept, swapped)[k][n] for k in halves]), d))
+    return join_blocks(back, OUT_PARTS)[None, None]
 
 
 def solution(mesh):

time: 57.4 us -> 55.6 us (0.969); the launches traced: 57.2 us -> 54.6 us
  waiting for transfers between devices: 23.7 us -> 18.8 us
  starting transfers between devices: 20.9 us -> 24.1 us
  Pallas kernels: 12.3 us -> 11.5 us
    ppermute x16 -> x18, waiting for transfers between devices: 23.7 us -> 18.8 us  [move(): return lax.ppermute(array, ('segment', 'frame'), pairs)]
    ppermute x16 -> x18, starting transfers between devices: 20.9 us -> 24.1 us  [move(): return lax.ppermute(array, ('segment', 'frame'), pairs)]
    pallas_call x2, Pallas kernels: 3.99 us -> 3.01 us  [the longest x1 1.98 us: pack_and_cut(): pl.pallas_call(functools.partial(pack_kernel, levels), out_shape=[pltpu.V...]
  transfers between devices with their start and end apart: 16 -> 18, of which waited for: 10 -> 11; matrix products, arithmetic and copies ran while one was open for 0% -> 0% of each run, Pallas kernels for 0% -> 0%
where the time goes in v4:
time: 55.6 us; the launch traced here: 54.6 us
  starting transfers between devices  24.1 us (43%)
  waiting for transfers between devices  18.8 us (34%)
  Pallas kernels  11.5 us (21%)
    ppermute x18, starting transfers between devices, move(): return lax.ppermute(array, ('segment', 'frame'), pairs)  24.1 us
    ppermute x18, waiting for transfers between devices, move(): return lax.ppermute(array, ('segment', 'frame'), pairs)  18.8 us
    pallas_call x1, Pallas kernels, run_sections(): pl.pallas_call(functools.partial(sections_kernel, spans, dests, borders,...  8.47 us
    pallas_call x1, Pallas kernels, pack_and_cut(): pl.pallas_call(functools.partial(pack_kernel, levels), out_shape=[pltpu.V...  1.98 us
  transfers between devices with their start and end apart: 18, of which 11 were waited for; matrix products, arithmetic and copies ran while one was open for 0% of the time, Pallas kernels for 0%

profile of v4, /device:TPU:17, one launch (start us, length us, event | category | flops | bytes accessed | tf_op | source)
XLA Modules:
  0.0 54.6 jit_solution(15959896447459219030)
XLA Ops:
  0.0 2.0 %pack.1 = (bf16[2,320,128]{2,1,0:T(8,128)(2,1)S(1)}, bf16[2,320,128]{2,1,0:T(8,128)(2,1)S(1)}, bf16[2,320,128]{2,1,0:T(8,128)(2,1)S(1)}, bf16[2,320,128]{2,1,0:T(8,128)(2,1)S(1)}, bf16[336,1280]{1,0:T(8,128)(2,1)S(1)}) custom-call(s32[4]{0:T(128)} %times_ref.1, bf16[320,1024]{1,0:T(8,128)(2,1)} %bitcast.6, bf16[3,320,320]{2,1,0:T(8,128)(2,1)} %bitcast.5, ...), custom_call_target="tpu_custom_call" | custom-call | tf_op jit(solution)/shard_map/pack/pallas_call | solution.py:146
  2.0 1.3 %collective-permute-start = (bf16[336,1280]{1,0:T(8,128)(2,1)S(1)}, bf16[336,1280]{1,0:T(8,128)(2,1)S(1)}, u32[]{:S(2)}, u32[]{:S(2)}) collective-permute-start(bf16[336,1280]{1,0:T(8,128)(2,1)S(1)} %get-tuple-element.17.refs_8_), channel_id=1, source_target_pairs={{0,16},{1,17},{2,18},{3,19},{4,20},{5,21},{6,22},{7,23},{8,24},{9,... | collective-permute-start | bytes 2580488 | tf_op jit(solution)/shard_map/ppermute | solution.py:95
  3.3 1.8 %collective-permute-start.1 = (bf16[2,320,128]{2,1,0:T(8,128)(2,1)S(1)}, bf16[2,320,128]{2,1,0:T(8,128)(2,1)S(1)}, u32[]{:S(2)}, u32[]{:S(2)}) collective-permute-start(bf16[2,320,128]{2,1,0:T(8,128)(2,1)S(1)} %get-tuple-element.18), channel_id=1, source_target_pairs={{0,4},{1,12},{2,6},{3,14},{4,0},{5,8},{6,2},{7,10},{8,5},{9,13},{1... | collective-permute-start | bytes 491528 | tf_op jit(solution)/shard_map/ppermute | solution.py:95
  5.1 1.8 %collective-permute-start.2 = (bf16[2,320,128]{2,1,0:T(8,128)(2,1)S(1)}, bf16[2,320,128]{2,1,0:T(8,128)(2,1)S(1)}, u32[]{:S(2)}, u32[]{:S(2)}) collective-permute-start(bf16[2,320,128]{2,1,0:T(8,128)(2,1)S(1)} %get-tuple-element.19), channel_id=1, source_target_pairs={{0,6},{1,14},{2,4},{3,12},{4,2},{5,10},{6,0},{7,8},{8,7},{9,15},{1... | collective-permute-start | bytes 491528 | tf_op jit(solution)/shard_map/ppermute | solution.py:95
  7.0 2.8 %collective-permute-start.3 = (bf16[2,320,128]{2,1,0:T(8,128)(2,1)S(1)}, bf16[2,320,128]{2,1,0:T(8,128)(2,1)S(1)}, u32[]{:S(2)}, u32[]{:S(2)}) collective-permute-start(bf16[2,320,128]{2,1,0:T(8,128)(2,1)S(1)} %get-tuple-element.20), channel_id=1, source_target_pairs={{0,2},{1,10},{2,0},{3,8},{4,6},{5,14},{6,4},{7,12},{8,3},{9,11},{1... | collective-permute-start | bytes 491528 | tf_op jit(solution)/shard_map/ppermute | solution.py:95
  9.8 1.9 %collective-permute-start.4 = (bf16[2,320,128]{2,1,0:T(8,128)(2,1)S(1)}, bf16[2,320,128]{2,1,0:T(8,128)(2,1)S(1)}, u32[]{:S(2)}, u32[]{:S(2)}) collective-permute-start(bf16[2,320,128]{2,1,0:T(8,128)(2,1)S(1)} %get-tuple-element.21), channel_id=1, source_target_pairs={{0,0},{1,8},{2,2},{3,10},{4,4},{5,12},{6,6},{7,14},{8,1},{9,9},{10... | collective-permute-start | bytes 491528 | tf_op jit(solution)/shard_map/ppermute | solution.py:95
  11.7 4.4 %collective-permute-done.1.refs_0_ = bf16[2,320,128]{2,1,0:T(8,128)(2,1)S(1)} collective-permute-done((bf16[2,320,128]{2,1,0:T(8,128)(2,1)S(1)}, bf16[2,320,128]{2,1,0:T(8,128)(2,1)S(1)}, u32[]{:S(2)}, u32[]{:S(2)}) %collective-permute-start.1) | collective-permute-done | bytes 163872 | tf_op jit(solution)/shard_map/ppermute | solution.py:95
  16.1 5.5 %collective-permute-done.2.refs_1_ = bf16[2,320,128]{2,1,0:T(8,128)(2,1)S(1)} collective-permute-done((bf16[2,320,128]{2,1,0:T(8,128)(2,1)S(1)}, bf16[2,320,128]{2,1,0:T(8,128)(2,1)S(1)}, u32[]{:S(2)}, u32[]{:S(2)}) %collective-permute-start.2) | collective-permute-done | bytes 163872 | tf_op jit(solution)/shard_map/ppermute | solution.py:95
  21.6 0.4 collective-permute-done.refs_10_
  22.1 1.5 %collective-permute-start.10 = (bf16[336,1280]{1,0:T(8,128)(2,1)S(1)}, bf16[336,1280]{1,0:T(8,128)(2,1)S(1)}, u32[]{:S(2)}, u32[]{:S(2)}) collective-permute-start(bf16[336,1280]{1,0:T(8,128)(2,1)S(1)} %collective-permute-done.refs_10_), channel_id=1, source_target_pairs={{0,8},{1,9},{2,10},{3,11},{4,12},{5,13},{6,14},{7,15},{8,0},{9,1},... | collective-permute-start | bytes 2580488 | tf_op jit(solution)/shard_map/ppermute | solution.py:95
  23.6 0.5 collective-permute-start.6
  24.1 0.5 collective-permute-start.8
  24.6 1.2 %collective-permute-done.5.refs_4_ = bf16[2,320,128]{2,1,0:T(8,128)(2,1)S(1)} collective-permute-done((bf16[2,320,128]{2,1,0:T(8,128)(2,1)S(1)}, bf16[2,320,128]{2,1,0:T(8,128)(2,1)S(1)}, u32[]{:S(2)}, u32[]{:S(2)}) %collective-permute-start.5) | collective-permute-done | bytes 163872 | tf_op jit(solution)/shard_map/ppermute | solution.py:95
  26.6 8.5 %sections.1 = (bf16[4,320,128]{2,1,0:T(8,128)(2,1)S(1)}, bf16[4,320,128]{2,1,0:T(8,128)(2,1)S(1)}) custom-call(bf16[2,320,128]{2,1,0:T(8,128)(2,1)S(1)} %collective-permute-done.1.refs_0_, bf16[2,320,128]{2,1,0:T(8,128)(2,1)S(1)} %collective-permute-done.2.refs_1_, bf16[2,320,128]{2,1,0:T(8,128)(2,1)S(1)} %collective-permute-done.3.refs_2_, ...), custom_call_target="tpu_custom_call" | custom-call | flops 4194304000 | bytes 4194304 | tf_op jit(solution)/shard_map/sections/pallas_call | solution.py:324
  35.2 1.4 %collective-permute-start.17 = (bf16[1,320,128]{2,1,0:T(8,128)(2,1)S(1)}, bf16[1,320,128]{2,1,0:T(8,128)(2,1)S(1)}, u32[]{:S(2)}, u32[]{:S(2)}) collective-permute-start(bf16[1,320,128]{2,1,0:T(8,128)(2,1)S(1)} %get-tuple-element.29), channel_id=1, source_target_pairs={{0,4},{1,12},{2,6},{3,14},{4,0},{5,8},{6,2},{7,10},{8,5},{9,13},{1... | collective-permute-start | bytes 245768 | tf_op jit(solution)/shard_map/ppermute | solution.py:95
  36.8 3.1 %collective-permute-start.12 = (bf16[2,320,128]{2,1,0:T(8,128)(2,1)S(1)}, bf16[2,320,128]{2,1,0:T(8,128)(2,1)S(1)}, u32[]{:S(2)}, u32[]{:S(2)}) collective-permute-start(bf16[2,320,128]{2,1,0:T(8,128)(2,1)S(1)} %pad_maximum_fusion), channel_id=1, source_target_pairs={{0,0},{1,8},{2,2},{3,10},{4,4},{5,12},{6,6},{7,14},{8,1},{9,9},{10... | collective-permute-start | bytes 491528 | tf_op jit(solution)/shard_map/ppermute | solution.py:95
  40.0 1.6 %collective-permute-start.13 = (bf16[2,320,128]{2,1,0:T(8,128)(2,1)S(1)}, bf16[2,320,128]{2,1,0:T(8,128)(2,1)S(1)}, u32[]{:S(2)}, u32[]{:S(2)}) collective-permute-start(bf16[2,320,128]{2,1,0:T(8,128)(2,1)S(1)} %pad_maximum_fusion.1), channel_id=1, source_target_pairs={{0,2},{1,10},{2,0},{3,8},{4,6},{5,14},{6,4},{7,12},{8,3},{9,11},{1... | collective-permute-start | bytes 491528 | tf_op jit(solution)/shard_map/ppermute | solution.py:95
  41.6 1.0 %collective-permute-start.16 = (bf16[1,320,128]{2,1,0:T(8,128)(2,1)S(1)}, bf16[1,320,128]{2,1,0:T(8,128)(2,1)S(1)}, u32[]{:S(2)}, u32[]{:S(2)}) collective-permute-start(bf16[1,320,128]{2,1,0:T(8,128)(2,1)S(1)} %get-tuple-element.30), channel_id=1, source_target_pairs={{0,6},{1,14},{2,4},{3,12},{4,2},{5,10},{6,0},{7,8},{8,7},{9,15},{1... | collective-permute-start | bytes 245768 | tf_op jit(solution)/shard_map/ppermute | solution.py:95
  42.6 2.4 %collective-permute-start.15 = (bf16[1,320,128]{2,1,0:T(8,128)(2,1)S(1)}, bf16[1,320,128]{2,1,0:T(8,128)(2,1)S(1)}, u32[]{:S(2)}, u32[]{:S(2)}) collective-permute-start(bf16[1,320,128]{2,1,0:T(8,128)(2,1)S(1)} %get-tuple-element.33), channel_id=1, source_target_pairs={{0,4},{1,12},{2,6},{3,14},{4,0},{5,8},{6,2},{7,10},{8,5},{9,13},{1... | collective-permute-start | bytes 245768 | tf_op jit(solution)/shard_map/ppermute | solution.py:95
  45.0 2.1 %collective-permute-start.14 = (bf16[1,320,128]{2,1,0:T(8,128)(2,1)S(1)}, bf16[1,320,128]{2,1,0:T(8,128)(2,1)S(1)}, u32[]{:S(2)}, u32[]{:S(2)}) collective-permute-start(bf16[1,320,128]{2,1,0:T(8,128)(2,1)S(1)} %get-tuple-element.34), channel_id=1, source_target_pairs={{0,6},{1,14},{2,4},{3,12},{4,2},{5,10},{6,0},{7,8},{8,7},{9,15},{1... | collective-permute-start | bytes 245768 | tf_op jit(solution)/shard_map/ppermute | solution.py:95
  47.1 2.8 %collective-permute-done.16.refs_4_ = bf16[1,320,128]{2,1,0:T(8,128)(2,1)S(1)} collective-permute-done((bf16[1,320,128]{2,1,0:T(8,128)(2,1)S(1)}, bf16[1,320,128]{2,1,0:T(8,128)(2,1)S(1)}, u32[]{:S(2)}, u32[]{:S(2)}) %collective-permute-start.16) | collective-permute-done | bytes 81952 | tf_op jit(solution)/shard_map/ppermute | solution.py:95
  49.9 1.6 %collective-permute-done.15.refs_3_ = bf16[1,320,128]{2,1,0:T(8,128)(2,1)S(1)} collective-permute-done((bf16[1,320,128]{2,1,0:T(8,128)(2,1)S(1)}, bf16[1,320,128]{2,1,0:T(8,128)(2,1)S(1)}, u32[]{:S(2)}, u32[]{:S(2)}) %collective-permute-start.15) | collective-permute-done | bytes 81952 | tf_op jit(solution)/shard_map/ppermute | solution.py:95
  51.5 2.1 %collective-permute-done.14.refs_2_ = bf16[1,320,128]{2,1,0:T(8,128)(2,1)S(1)} collective-permute-done((bf16[1,320,128]{2,1,0:T(8,128)(2,1)S(1)}, bf16[1,320,128]{2,1,0:T(8,128)(2,1)S(1)}, u32[]{:S(2)}, u32[]{:S(2)}) %collective-permute-start.14) | collective-permute-done | bytes 81952 | tf_op jit(solution)/shard_map/ppermute | solution.py:95
  53.6 1.0 %join.1 = bf16[320,1024]{1,0:T(8,128)(2,1)} custom-call(bf16[2,320,128]{2,1,0:T(8,128)(2,1)S(1)} %collective-permute-done.12.refs_0_, bf16[2,320,128]{2,1,0:T(8,128)(2,1)S(1)} %collective-permute-done.13.refs_1_, bf16[1,320,128]{2,1,0:T(8,128)(2,1)S(1)} %collective-permute-done.14.refs_2_, bf16[1,320,128]{2,1,0:T(8,128)(2,1)S(1)} %collective-permute-done.15.refs_3_, ...), custom_call_target="tpu_custom_call" | custom-call | tf_op jit(solution)/shard_map/join/pallas_call | solution.py:170
  (25 shorter events, 1.1 us)
Async XLA Ops:
  2.0 24.6 %copy-start = (f32[4,320]{1,0:T(4,128)S(1)}, f32[4,320]{1,0:T(4,128)}, u32[]{:S(2)}) copy-start(f32[4,320]{1,0:T(4,128)} %refs_13_.1) | copy-start | bytes 15364
  2.0 20.1 %collective-permute-start = (bf16[336,1280]{1,0:T(8,128)(2,1)S(1)}, bf16[336,1280]{1,0:T(8,128)(2,1)S(1)}, u32[]{:S(2)}, u32[]{:S(2)}) collective-permute-start(bf16[336,1280]{1,0:T(8,128)(2,1)S(1)} %get-tuple-element.17.refs_8_), channel_id=1, source_target_pairs={{0,16},{1,17},{2,18},{3,19},{4,20},{5,21},{6,22},{7,23},{8,24},{9,... | collective-permute-start | bytes 2580488 | tf_op jit(solution)/shard_map/ppermute | solution.py:95
  3.3 12.8 %collective-permute-start.1 = (bf16[2,320,128]{2,1,0:T(8,128)(2,1)S(1)}, bf16[2,320,128]{2,1,0:T(8,128)(2,1)S(1)}, u32[]{:S(2)}, u32[]{:S(2)}) collective-permute-start(bf16[2,320,128]{2,1,0:T(8,128)(2,1)S(1)} %get-tuple-element.18), channel_id=1, source_target_pairs={{0,4},{1,12},{2,6},{3,14},{4,0},{5,8},{6,2},{7,10},{8,5},{9,13},{1... | collective-permute-start | bytes 491528 | tf_op jit(solution)/shard_map/ppermute | solution.py:95
  5.1 16.5 %collective-permute-start.2 = (bf16[2,320,128]{2,1,0:T(8,128)(2,1)S(1)}, bf16[2,320,128]{2,1,0:T(8,128)(2,1)S(1)}, u32[]{:S(2)}, u32[]{:S(2)}) collective-permute-start(bf16[2,320,128]{2,1,0:T(8,128)(2,1)S(1)} %get-tuple-element.19), channel_id=1, source_target_pairs={{0,6},{1,14},{2,4},{3,12},{4,2},{5,10},{6,0},{7,8},{8,7},{9,15},{1... | collective-permute-start | bytes 491528 | tf_op jit(solution)/shard_map/ppermute | solution.py:95
  7.0 14.7 %collective-permute-start.3 = (bf16[2,320,128]{2,1,0:T(8,128)(2,1)S(1)}, bf16[2,320,128]{2,1,0:T(8,128)(2,1)S(1)}, u32[]{:S(2)}, u32[]{:S(2)}) collective-permute-start(bf16[2,320,128]{2,1,0:T(8,128)(2,1)S(1)} %get-tuple-element.20), channel_id=1, source_target_pairs={{0,2},{1,10},{2,0},{3,8},{4,6},{5,14},{6,4},{7,12},{8,3},{9,11},{1... | collective-permute-start | bytes 491528 | tf_op jit(solution)/shard_map/ppermute | solution.py:95
  9.8 11.8 %collective-permute-start.4 = (bf16[2,320,128]{2,1,0:T(8,128)(2,1)S(1)}, bf16[2,320,128]{2,1,0:T(8,128)(2,1)S(1)}, u32[]{:S(2)}, u32[]{:S(2)}) collective-permute-start(bf16[2,320,128]{2,1,0:T(8,128)(2,1)S(1)} %get-tuple-element.21), channel_id=1, source_target_pairs={{0,0},{1,8},{2,2},{3,10},{4,4},{5,12},{6,6},{7,14},{8,1},{9,9},{10... | collective-permute-start | bytes 491528 | tf_op jit(solution)/shard_map/ppermute | solution.py:95
  16.1 8.0 %collective-permute-start.9 = (bf16[336,1280]{1,0:T(8,128)(2,1)S(1)}, bf16[336,1280]{1,0:T(8,128)(2,1)S(1)}, u32[]{:S(2)}, u32[]{:S(2)}) collective-permute-start(bf16[336,1280]{1,0:T(8,128)(2,1)S(1)} %get-tuple-element.17.refs_8_), channel_id=1, source_target_pairs={{0,8},{1,9},{2,10},{3,11},{4,12},{5,13},{6,14},{7,15},{8,0},{9,1},... | collective-permute-start | bytes 2580488 | tf_op jit(solution)/shard_map/ppermute | solution.py:95
  22.1 4.5 %copy-start.1 = (bf16[336,1280]{1,0:T(8,128)(2,1)}, bf16[336,1280]{1,0:T(8,128)(2,1)S(1)}, u32[]{:S(2)}) copy-start(bf16[336,1280]{1,0:T(8,128)(2,1)S(1)} %collective-permute-done.refs_10_) | copy-start | bytes 2580484
  22.1 4.5 %collective-permute-start.10 = (bf16[336,1280]{1,0:T(8,128)(2,1)S(1)}, bf16[336,1280]{1,0:T(8,128)(2,1)S(1)}, u32[]{:S(2)}, u32[]{:S(2)}) collective-permute-start(bf16[336,1280]{1,0:T(8,128)(2,1)S(1)} %collective-permute-done.refs_10_), channel_id=1, source_target_pairs={{0,8},{1,9},{2,10},{3,11},{4,12},{5,13},{6,14},{7,15},{8,0},{9,1},... | collective-permute-start | bytes 2580488 | tf_op jit(solution)/shard_map/ppermute | solution.py:95
  23.6 2.3 %collective-permute-start.5 = (bf16[2,320,128]{2,1,0:T(8,128)(2,1)S(1)}, bf16[2,320,128]{2,1,0:T(8,128)(2,1)S(1)}, u32[]{:S(2)}, u32[]{:S(2)}) collective-permute-start(bf16[2,320,128]{2,1,0:T(8,128)(2,1)S(1)} %collective-permute-done.1.refs_0_), channel_id=1, source_target_pairs={{0,8},{1,9},{2,10},{3,11},{4,12},{5,13},{6,14},{7,15},{8,0},{9,1},... | collective-permute-start | bytes 491528 | tf_op jit(solution)/shard_map/ppermute | solution.py:95
  23.6 2.5 %collective-permute-start.6 = (bf16[2,320,128]{2,1,0:T(8,128)(2,1)S(1)}, bf16[2,320,128]{2,1,0:T(8,128)(2,1)S(1)}, u32[]{:S(2)}, u32[]{:S(2)}) collective-permute-start(bf16[2,320,128]{2,1,0:T(8,128)(2,1)S(1)} %collective-permute-done.2.refs_1_), channel_id=1, source_target_pairs={{0,8},{1,9},{2,10},{3,11},{4,12},{5,13},{6,14},{7,15},{8,0},{9,1},... | collective-permute-start | bytes 491528 | tf_op jit(solution)/shard_map/ppermute | solution.py:95
  24.1 2.2 %collective-permute-start.7 = (bf16[2,320,128]{2,1,0:T(8,128)(2,1)S(1)}, bf16[2,320,128]{2,1,0:T(8,128)(2,1)S(1)}, u32[]{:S(2)}, u32[]{:S(2)}) collective-permute-start(bf16[2,320,128]{2,1,0:T(8,128)(2,1)S(1)} %collective-permute-done.3.refs_2_), channel_id=1, source_target_pairs={{0,8},{1,9},{2,10},{3,11},{4,12},{5,13},{6,14},{7,15},{8,0},{9,1},... | collective-permute-start | bytes 491528 | tf_op jit(solution)/shard_map/ppermute | solution.py:95
  24.1 2.4 %copy-start.2 = (bf16[336,1280]{1,0:T(8,128)(2,1)}, bf16[336,1280]{1,0:T(8,128)(2,1)S(1)}, u32[]{:S(2)}) copy-start(bf16[336,1280]{1,0:T(8,128)(2,1)S(1)} %collective-permute-done.9.refs_9_) | copy-start | bytes 2580484
  24.1 2.4 %collective-permute-start.8 = (bf16[2,320,128]{2,1,0:T(8,128)(2,1)S(1)}, bf16[2,320,128]{2,1,0:T(8,128)(2,1)S(1)}, u32[]{:S(2)}, u32[]{:S(2)}) collective-permute-start(bf16[2,320,128]{2,1,0:T(8,128)(2,1)S(1)} %collective-permute-done.4.refs_3_), channel_id=1, source_target_pairs={{0,8},{1,9},{2,10},{3,11},{4,12},{5,13},{6,14},{7,15},{8,0},{9,1},... | collective-permute-start | bytes 491528 | tf_op jit(solution)/shard_map/ppermute | solution.py:95
  35.0 1.7 %collective-permute-start.11 = (bf16[4,320,128]{2,1,0:T(8,128)(2,1)S(1)}, bf16[4,320,128]{2,1,0:T(8,128)(2,1)S(1)}, u32[]{:S(2)}, u32[]{:S(2)}) collective-permute-start(bf16[4,320,128]{2,1,0:T(8,128)(2,1)S(1)} %get-tuple-element.28), channel_id=1, source_target_pairs={{0,8},{1,9},{2,10},{3,11},{4,12},{5,13},{6,14},{7,15},{8,0},{9,1},... | collective-permute-start | bytes 983048 | tf_op jit(solution)/shard_map/ppermute | solution.py:95
  35.2 9.8 %collective-permute-start.17 = (bf16[1,320,128]{2,1,0:T(8,128)(2,1)S(1)}, bf16[1,320,128]{2,1,0:T(8,128)(2,1)S(1)}, u32[]{:S(2)}, u32[]{:S(2)}) collective-permute-start(bf16[1,320,128]{2,1,0:T(8,128)(2,1)S(1)} %get-tuple-element.29), channel_id=1, source_target_pairs={{0,4},{1,12},{2,6},{3,14},{4,0},{5,8},{6,2},{7,10},{8,5},{9,13},{1... | collective-permute-start | bytes 245768 | tf_op jit(solution)/shard_map/ppermute | solution.py:95
  36.8 16.8 %collective-permute-start.12 = (bf16[2,320,128]{2,1,0:T(8,128)(2,1)S(1)}, bf16[2,320,128]{2,1,0:T(8,128)(2,1)S(1)}, u32[]{:S(2)}, u32[]{:S(2)}) collective-permute-start(bf16[2,320,128]{2,1,0:T(8,128)(2,1)S(1)} %pad_maximum_fusion), channel_id=1, source_target_pairs={{0,0},{1,8},{2,2},{3,10},{4,4},{5,12},{6,6},{7,14},{8,1},{9,9},{10... | collective-permute-start | bytes 491528 | tf_op jit(solution)/shard_map/ppermute | solution.py:95
  40.0 13.6 %collective-permute-start.13 = (bf16[2,320,128]{2,1,0:T(8,128)(2,1)S(1)}, bf16[2,320,128]{2,1,0:T(8,128)(2,1)S(1)}, u32[]{:S(2)}, u32[]{:S(2)}) collective-permute-start(bf16[2,320,128]{2,1,0:T(8,128)(2,1)S(1)} %pad_maximum_fusion.1), channel_id=1, source_target_pairs={{0,2},{1,10},{2,0},{3,8},{4,6},{5,14},{6,4},{7,12},{8,3},{9,11},{1... | collective-permute-start | bytes 491528 | tf_op jit(solution)/shard_map/ppermute | solution.py:95
  41.6 8.3 %collective-permute-start.16 = (bf16[1,320,128]{2,1,0:T(8,128)(2,1)S(1)}, bf16[1,320,128]{2,1,0:T(8,128)(2,1)S(1)}, u32[]{:S(2)}, u32[]{:S(2)}) collective-permute-start(bf16[1,320,128]{2,1,0:T(8,128)(2,1)S(1)} %get-tuple-element.30), channel_id=1, source_target_pairs={{0,6},{1,14},{2,4},{3,12},{4,2},{5,10},{6,0},{7,8},{8,7},{9,15},{1... | collective-permute-start | bytes 245768 | tf_op jit(solution)/shard_map/ppermute | solution.py:95
  42.6 8.8 %collective-permute-start.15 = (bf16[1,320,128]{2,1,0:T(8,128)(2,1)S(1)}, bf16[1,320,128]{2,1,0:T(8,128)(2,1)S(1)}, u32[]{:S(2)}, u32[]{:S(2)}) collective-permute-start(bf16[1,320,128]{2,1,0:T(8,128)(2,1)S(1)} %get-tuple-element.33), channel_id=1, source_target_pairs={{0,4},{1,12},{2,6},{3,14},{4,0},{5,8},{6,2},{7,10},{8,5},{9,13},{1... | collective-permute-start | bytes 245768 | tf_op jit(solution)/shard_map/ppermute | solution.py:95
  45.0 8.6 %collective-permute-start.14 = (bf16[1,320,128]{2,1,0:T(8,128)(2,1)S(1)}, bf16[1,320,128]{2,1,0:T(8,128)(2,1)S(1)}, u32[]{:S(2)}, u32[]{:S(2)}) collective-permute-start(bf16[1,320,128]{2,1,0:T(8,128)(2,1)S(1)} %get-tuple-element.34), channel_id=1, source_target_pairs={{0,6},{1,14},{2,4},{3,12},{4,2},{5,10},{6,0},{7,8},{8,7},{9,15},{1... | collective-permute-start | bytes 245768 | tf_op jit(solution)/shard_map/ppermute | solution.py:95

commit v5 on v4

--- a/solution.py
+++ b/solution.py
@@ -74,6 +74,7 @@
 
 
 FILM_ROWS = 16
+JOIN_STEPS = 4
 
 
 def place():
@@ -154,13 +155,21 @@
 
 
 def join_kernel(parts, *refs):
-    blocks, out = refs[: len(parts)], refs[len(parts)]
+    blocks, out, joined, sem = refs[: len(parts)], *refs[len(parts) :]
     frame = lax.axis_index("frame")
     z, x = frame // 2, frame % 2
-    for block, (d, halves) in zip(blocks, parts, strict=True):
-        for n, k in enumerate(halves):
-            at = pl.multiple_of(((z ^ d) * 2 + (x ^ k)) * LANES, LANES)
-            out[:, pl.ds(at, LANES)] = block[n]
+    stores = []
+    step = joined.shape[0] // JOIN_STEPS
+    for low in range(0, joined.shape[0], step):
+        rows = pl.ds(low, step)
+        for block, (d, halves) in zip(blocks, parts, strict=True):
+            for n, k in enumerate(halves):
+                at = pl.multiple_of(((z ^ d) * 2 + (x ^ k)) * LANES, LANES)
+                joined[rows, pl.ds(at, LANES)] = block[n, rows]
+        stores.append(pltpu.make_async_copy(joined.at[rows], out.at[rows], sem.at[low // step]))
+        stores[-1].start()
+    for store in stores:
+        store.wait()
 
 
 def join_blocks(blocks, parts):
@@ -171,12 +180,16 @@
         functools.partial(join_kernel, parts),
         out_shape=jax.ShapeDtypeStruct((width, columns), BF),
         in_specs=[vmem] * len(blocks),
-        out_specs=vmem,
+        out_specs=pl.BlockSpec(memory_space=pltpu.HBM),
+        scratch_shapes=[
+            pltpu.VMEM((width, columns), BF),
+            pltpu.SemaphoreType.DMA((JOIN_STEPS,)),
+        ],
         name="join",
     )(*pin(blocks, pltpu.VMEM))
 
 
-def sections_kernel(spans, dests, borders, levels, width, loaded, *refs):
+def sections_kernel(dests, levels, width, loaded, *refs):
     refs = list(refs)
 
     def take(count):
@@ -184,23 +197,16 @@
         del refs[:count]
         return taken
 
-    near = borders is not None and spans[0][0] == 0
     turned, swapped = take(len(loaded)), take(len(loaded))
     packs = take(4)
     skip_in, gain_ref = take(2)
-    if near:
-        (border_in,) = take(1)
     kept, given = take(2)
-    if borders and not near:
-        (border_out,) = take(1)
-    weights, skip, unfolded, with_one, with_first, two, three, last, bordering = take(9)
-    sem_w, sem_s, sem_b = take(3)
+    weights, skip, around, with_one, with_first, two, three, last = take(8)
+    sem_w, sem_s = take(2)
     y, core, z, x = place()
     clip = 2 * y + x
     segment = 2 * y + core
     frames = 2 * levels
-    upper = jnp.where(z >= levels // 2, 1, 0)
-    mirror = upper * (frames - 1)
 
     def load_weights(s):
         for b in range(4):
@@ -210,25 +216,18 @@
                 pltpu.make_async_copy(packs[b], weights.at[s], sem_w.at[s]).start()
 
     load_weights(0)
-    if near:
-        border_load = pltpu.make_async_copy(border_in, bordering, sem_b)
-        border_load.start()
     skip_load = pltpu.make_async_copy(skip_in, skip, sem_s)
 
-    def rows_of(step):
-        return pl.ds(pl.multiple_of((1 - step + 2 * step * upper) * width, 64), width)
-
     def lanes_of(d, k):
-        slot = (2 * (z ^ d) + (core ^ k)) ^ mirror
+        slot = 2 * (z ^ d) + (core ^ k)
         return pl.ds(pl.multiple_of(slot * LANES, LANES), LANES)
 
     def span(f, count=1):
         return slice(f * LANES, (f + count) * LANES)
 
     zeros = jnp.zeros((width, LANES), BF)
-    unfolded[3 * width :, :] = jnp.zeros((unfolded.shape[0] - 3 * width, frames * LANES), BF)
-    unfolded[rows_of(1), span(0)] = zeros
-    unfolded[rows_of(-1), span(frames - 1)] = zeros
+    around[:, span(0)] = zeros
+    around[:, span(frames + 1)] = zeros
     for ref in (with_one, with_first):
         ref[0:64, :] = jnp.zeros((64, frames * LANES), BF)
 
@@ -250,105 +249,84 @@
     gains = jnp.concatenate(gains + [jnp.zeros_like(rest)], axis=0).astype(BF)
 
     one, zero = with_one.at[64 + width :, :], with_first.at[64 + width :, :]
-    states = (zero, one, two, three)
     for n, d in enumerate(loaded):
         for k in range(2):
             zero[:, lanes_of(d, k)] = (turned, swapped)[k][n][core]
-    if near:
-        border_load.wait()
-        for n, (s, f) in enumerate(borders):
-            states[s][:, span(f)] = bordering[n]
-
-    for s, (low, high) in enumerate(spans):
-        source = states[s]
+
+    for s in range(4):
+        source, target = ((zero, one), (one, two), (two, three), (three, last))[s]
         gain = column_of(gains, [s, 4 + s, 8 + s])
-        for f in range(max(low - 1, 0), min(high + 1, frames)):
-            values = source[:, span(f)].astype(F32)
-            scale = lax.rsqrt(jnp.mean(values * values, axis=0, keepdims=True) + EPS)
-            normed = (values * scale * gain).astype(BF)
-            for step in (-1, 0, 1):
-                if low <= f + step < high:
-                    unfolded[rows_of(step), span(f + step)] = normed
+        values = source[...].astype(F32)
+        scale = lax.rsqrt(jnp.mean(values * values, axis=0, keepdims=True) + EPS)
+        wide = jnp.concatenate([gain] * frames, axis=1)
+        around[:, span(1, frames)] = (values * scale * wide).astype(BF)
         pltpu.make_async_copy(packs[0], weights.at[s], sem_w.at[s]).wait()
         if s < 3:
             load_weights(s + 1)
         if s == 0:
             skip_load.start()
-        film = 1.0 + column_of(weights[s, width:, 0:width], [clip, 4 + clip])
-        film = jnp.concatenate([film] * (high - low), axis=1)
-        cols = span(low, high - low)
-        taps = weights[s, 0:width, 0 : unfolded.shape[0]]
-        mixed = jnp.dot(taps, unfolded[:, cols], preferred_element_type=F32) * film
-        hidden = (mixed * (0.5 + 0.5 * jnp.tanh(0.5 * mixed))).astype(BF)
+        half = 0.5 + 0.5 * column_of(weights[s, width:, 0:width], [clip, 4 + clip])
+        half = jnp.concatenate([half] * frames, axis=1)
+        three_frames = jnp.concatenate(
+            [around[:, span(tau, frames)] for tau in range(3)]
+            + [jnp.zeros((64, frames * LANES), BF)],
+            axis=0,
+        )
+        mixed = jnp.dot(
+            weights[s, 0:width, 0 : 3 * width + 64], three_frames, preferred_element_type=F32
+        )
+        mixed = mixed * half
+        beside = with_first if s == 3 else with_one
+        beside[64 : 64 + width, :] = (mixed * (1.0 + jnp.tanh(mixed))).astype(BF)
         projection = weights[s, 0:width, 3 * width - 64 :]
-        if s < 2:
-            with_one[64 : 64 + width, cols] = hidden
-            right = with_one[0 : 64 + width, cols]
-        else:
+        right = beside[0 : 64 + width, :]
+        if s >= 2:
             if s == 2:
                 skip_load.wait()
-            beside = with_one if s == 2 else with_first
-            beside[64 : 64 + width, cols] = hidden
-            right = beside[:, cols]
             projection = jnp.concatenate([projection, skip[s - 2].T], axis=1)
-        total = source[:, cols].astype(F32)
+            right = beside[...]
+        total = source[...].astype(F32)
         total = (total + jnp.dot(projection, right, preferred_element_type=F32)).astype(BF)
-        (one, two, three, last)[s][:, cols] = total
+        target[...] = total
     for n, d in enumerate(dests):
         for k, out in enumerate((kept, given)):
             out[n] = last[:, lanes_of(d, k)]
-    if borders and not near:
-        for n, (s, f) in enumerate(borders):
-            border_out[n] = states[s][:, span(f)]
-
-
-def run_sections(
-    spans, dests, borders, loaded, turned, swapped, weights, skip, gain, border=None
-):
+
+
+def run_sections(dests, loaded, turned, swapped, weights, skip, gain):
     levels = lax.axis_size("frame") // 2
     frames = 2 * levels
     width = gain.shape[1]
     columns = frames * LANES
-    hbm = pl.BlockSpec(memory_space=pltpu.HBM)
     vmem = pl.BlockSpec(memory_space=pltpu.VMEM)
-    given_out = [pltpu.VMEM((len(dests), width, LANES), BF)] * 2
     blocks = [*turned, *swapped]
-    places = [pltpu.VMEM, pltpu.HBM, pltpu.HBM, pltpu.VMEM, pltpu.HBM]
+    places = [pltpu.VMEM] * 4 + [pltpu.HBM]
     inputs = [pin([a], place)[0] for a, place in zip([*weights, skip], places, strict=True)]
-    after = []
-    if border is not None:
-        after = pin([border], pltpu.HBM)
-    elif borders:
-        given_out.append(jax.ShapeDtypeStruct((len(borders), width, LANES), BF))
-    flops = sum(high - low for low, high in spans) * LANES * 2 * 5 * width * width
     return pl.pallas_call(
-        functools.partial(
-            sections_kernel, spans, dests, borders, levels, width, loaded
-        ),
-        out_shape=given_out,
+        functools.partial(sections_kernel, dests, levels, width, loaded),
+        out_shape=[pltpu.VMEM((len(dests), width, LANES), BF)] * 2,
         in_specs=[vmem] * len(blocks)
         + [pl.BlockSpec(memory_space=place) for place in places]
-        + [pl.BlockSpec(memory_space=pltpu.VMEM)]
-        + [hbm] * len(after),
-        out_specs=[vmem] * len(given_out),
+        + [vmem],
+        out_specs=[vmem] * 2,
         scratch_shapes=[
             pltpu.VMEM((4, width + FILM_ROWS, 4 * width), BF),
             pltpu.VMEM((2, width, width), BF),
-            pltpu.VMEM((3 * width + 64, columns), BF),
+            pltpu.VMEM((width, columns + 2 * LANES), BF),
             pltpu.VMEM((2 * width + 64, columns), BF),
             pltpu.VMEM((2 * width + 64, columns), BF),
             pltpu.VMEM((width, columns), BF),
             pltpu.VMEM((width, columns), BF),
             pltpu.VMEM((width, columns), BF),
-            pltpu.VMEM((6, width, LANES), BF),
             pltpu.SemaphoreType.DMA((4,)),
-            pltpu.SemaphoreType.DMA,
             pltpu.SemaphoreType.DMA,
         ],
         compiler_params=pltpu.CompilerParams(vmem_limit_bytes=40 << 20),
-        cost_estimate=pl.CostEstimate(flops=flops, bytes_accessed=4 << 20, transcendentals=0),
+        cost_estimate=pl.CostEstimate(
+            flops=columns * 2 * 18 * width * width, bytes_accessed=4 << 20, transcendentals=0
+        ),
         name="sections",
-    )(*pin(blocks, pltpu.VMEM), *inputs, gain, *after)
+    )(*pin(blocks, pltpu.VMEM), *inputs, gain)
 
 
 IN_ORDER = (2, 3, 1, 0)
@@ -369,16 +347,9 @@
     pack3 = swap_cores(pack2)
     swapped = [swap_cores(block) for block in turned]
 
+    weights = [pack0, pack1, pack2, pack3]
     kept, given = run_sections(
-        [(0, 2 * levels)] * 4,
-        OUT_ORDER,
-        None,
-        IN_ORDER,
-        turned,
-        swapped,
-        [pack0, pack1, pack2, pack3],
-        skip_weight,
-        gain,
+        OUT_ORDER, IN_ORDER, turned, swapped, weights, skip_weight, gain
     )
     swapped = swap_cores(given)
     back = []

time: 55.6 us -> 54.5 us (0.980)
  Pallas kernels: 11.5 us -> 10.1 us
    pallas_call x1, Pallas kernels: 8.47 us -> 7.16 us  [run_sections(): pl.pallas_call(functools.partial(sections_kernel, dests, levels, width, l...]
where the time goes in v5:
time: 54.5 us; the launch traced here: 53.5 us
  starting transfers between devices  24.5 us (45%)
  waiting for transfers between devices  18.8 us (34%)
  Pallas kernels  10.1 us (19%)
    ppermute x18, starting transfers between devices, move(): return lax.ppermute(array, ('segment', 'frame'), pairs)  24.5 us
    ppermute x18, waiting for transfers between devices, move(): return lax.ppermute(array, ('segment', 'frame'), pairs)  18.8 us
    pallas_call x1, Pallas kernels, run_sections(): pl.pallas_call(functools.partial(sections_kernel, dests, levels, width, l...  7.16 us
    pallas_call x1, Pallas kernels, pack_and_cut(): pl.pallas_call(functools.partial(pack_kernel, levels), out_shape=[pltpu.V...  1.98 us
  transfers between devices with their start and end apart: 18, of which 11 were waited for; matrix products, arithmetic and copies ran while one was open for 0% of the time, Pallas kernels for 0%

profile of v5, /device:TPU:17, one launch (start us, length us, event | category | flops | bytes accessed | tf_op | source)
XLA Modules:
  0.0 53.5 jit_solution(8687879019868453166)
XLA Ops:
  0.0 2.0 %pack.1 = (bf16[2,320,128]{2,1,0:T(8,128)(2,1)S(1)}, bf16[2,320,128]{2,1,0:T(8,128)(2,1)S(1)}, bf16[2,320,128]{2,1,0:T(8,128)(2,1)S(1)}, bf16[2,320,128]{2,1,0:T(8,128)(2,1)S(1)}, bf16[336,1280]{1,0:T(8,128)(2,1)S(1)}) custom-call(s32[4]{0:T(128)} %times_ref.1, bf16[320,1024]{1,0:T(8,128)(2,1)} %bitcast.6, bf16[3,320,320]{2,1,0:T(8,128)(2,1)} %bitcast.5, ...), custom_call_target="tpu_custom_call" | custom-call | tf_op jit(solution)/shard_map/pack/pallas_call | solution.py:147
  2.0 1.3 %collective-permute-start = (bf16[336,1280]{1,0:T(8,128)(2,1)S(1)}, bf16[336,1280]{1,0:T(8,128)(2,1)S(1)}, u32[]{:S(2)}, u32[]{:S(2)}) collective-permute-start(bf16[336,1280]{1,0:T(8,128)(2,1)S(1)} %get-tuple-element.17.refs_8_), channel_id=1, source_target_pairs={{0,16},{1,17},{2,18},{3,19},{4,20},{5,21},{6,22},{7,23},{8,24},{9,... | collective-permute-start | bytes 2580488 | tf_op jit(solution)/shard_map/ppermute | solution.py:96
  3.3 1.8 %collective-permute-start.1 = (bf16[2,320,128]{2,1,0:T(8,128)(2,1)S(1)}, bf16[2,320,128]{2,1,0:T(8,128)(2,1)S(1)}, u32[]{:S(2)}, u32[]{:S(2)}) collective-permute-start(bf16[2,320,128]{2,1,0:T(8,128)(2,1)S(1)} %get-tuple-element.18), channel_id=1, source_target_pairs={{0,4},{1,12},{2,6},{3,14},{4,0},{5,8},{6,2},{7,10},{8,5},{9,13},{1... | collective-permute-start | bytes 491528 | tf_op jit(solution)/shard_map/ppermute | solution.py:96
  5.1 1.8 %collective-permute-start.2 = (bf16[2,320,128]{2,1,0:T(8,128)(2,1)S(1)}, bf16[2,320,128]{2,1,0:T(8,128)(2,1)S(1)}, u32[]{:S(2)}, u32[]{:S(2)}) collective-permute-start(bf16[2,320,128]{2,1,0:T(8,128)(2,1)S(1)} %get-tuple-element.19), channel_id=1, source_target_pairs={{0,6},{1,14},{2,4},{3,12},{4,2},{5,10},{6,0},{7,8},{8,7},{9,15},{1... | collective-permute-start | bytes 491528 | tf_op jit(solution)/shard_map/ppermute | solution.py:96
  7.0 2.8 %collective-permute-start.3 = (bf16[2,320,128]{2,1,0:T(8,128)(2,1)S(1)}, bf16[2,320,128]{2,1,0:T(8,128)(2,1)S(1)}, u32[]{:S(2)}, u32[]{:S(2)}) collective-permute-start(bf16[2,320,128]{2,1,0:T(8,128)(2,1)S(1)} %get-tuple-element.20), channel_id=1, source_target_pairs={{0,2},{1,10},{2,0},{3,8},{4,6},{5,14},{6,4},{7,12},{8,3},{9,11},{1... | collective-permute-start | bytes 491528 | tf_op jit(solution)/shard_map/ppermute | solution.py:96
  9.8 1.9 %collective-permute-start.4 = (bf16[2,320,128]{2,1,0:T(8,128)(2,1)S(1)}, bf16[2,320,128]{2,1,0:T(8,128)(2,1)S(1)}, u32[]{:S(2)}, u32[]{:S(2)}) collective-permute-start(bf16[2,320,128]{2,1,0:T(8,128)(2,1)S(1)} %get-tuple-element.21), channel_id=1, source_target_pairs={{0,0},{1,8},{2,2},{3,10},{4,4},{5,12},{6,6},{7,14},{8,1},{9,9},{10... | collective-permute-start | bytes 491528 | tf_op jit(solution)/shard_map/ppermute | solution.py:96
  11.7 4.4 %collective-permute-done.1.refs_0_ = bf16[2,320,128]{2,1,0:T(8,128)(2,1)S(1)} collective-permute-done((bf16[2,320,128]{2,1,0:T(8,128)(2,1)S(1)}, bf16[2,320,128]{2,1,0:T(8,128)(2,1)S(1)}, u32[]{:S(2)}, u32[]{:S(2)}) %collective-permute-start.1) | collective-permute-done | bytes 163872 | tf_op jit(solution)/shard_map/ppermute | solution.py:96
  16.1 5.5 %collective-permute-done.2.refs_1_ = bf16[2,320,128]{2,1,0:T(8,128)(2,1)S(1)} collective-permute-done((bf16[2,320,128]{2,1,0:T(8,128)(2,1)S(1)}, bf16[2,320,128]{2,1,0:T(8,128)(2,1)S(1)}, u32[]{:S(2)}, u32[]{:S(2)}) %collective-permute-start.2) | collective-permute-done | bytes 163872 | tf_op jit(solution)/shard_map/ppermute | solution.py:96
  22.1 1.5 %collective-permute-start.10 = (bf16[336,1280]{1,0:T(8,128)(2,1)S(1)}, bf16[336,1280]{1,0:T(8,128)(2,1)S(1)}, u32[]{:S(2)}, u32[]{:S(2)}) collective-permute-start(bf16[336,1280]{1,0:T(8,128)(2,1)S(1)} %collective-permute-done.refs_10_), channel_id=1, source_target_pairs={{0,8},{1,9},{2,10},{3,11},{4,12},{5,13},{6,14},{7,15},{8,0},{9,1},... | collective-permute-start | bytes 2580488 | tf_op jit(solution)/shard_map/ppermute | solution.py:96
  23.6 0.5 collective-permute-start.6
  24.1 0.5 collective-permute-start.8
  24.6 1.2 %collective-permute-done.5.refs_4_ = bf16[2,320,128]{2,1,0:T(8,128)(2,1)S(1)} collective-permute-done((bf16[2,320,128]{2,1,0:T(8,128)(2,1)S(1)}, bf16[2,320,128]{2,1,0:T(8,128)(2,1)S(1)}, u32[]{:S(2)}, u32[]{:S(2)}) %collective-permute-start.5) | collective-permute-done | bytes 163872 | tf_op jit(solution)/shard_map/ppermute | solution.py:96
  26.6 7.2 %sections.1 = (bf16[4,320,128]{2,1,0:T(8,128)(2,1)S(1)}, bf16[4,320,128]{2,1,0:T(8,128)(2,1)S(1)}) custom-call(bf16[2,320,128]{2,1,0:T(8,128)(2,1)S(1)} %collective-permute-done.1.refs_0_, bf16[2,320,128]{2,1,0:T(8,128)(2,1)S(1)} %collective-permute-done.2.refs_1_, bf16[2,320,128]{2,1,0:T(8,128)(2,1)S(1)} %collective-permute-done.3.refs_2_, ...), custom_call_target="tpu_custom_call" | custom-call | flops 3774873600 | bytes 4194304 | tf_op jit(solution)/shard_map/sections/pallas_call | solution.py:305
  33.7 0.4 collective-permute-start.11
  34.2 1.1 %collective-permute-start.17 = (bf16[1,320,128]{2,1,0:T(8,128)(2,1)S(1)}, bf16[1,320,128]{2,1,0:T(8,128)(2,1)S(1)}, u32[]{:S(2)}, u32[]{:S(2)}) collective-permute-start(bf16[1,320,128]{2,1,0:T(8,128)(2,1)S(1)} %get-tuple-element.29), channel_id=1, source_target_pairs={{0,4},{1,12},{2,6},{3,14},{4,0},{5,8},{6,2},{7,10},{8,5},{9,13},{1... | collective-permute-start | bytes 245768 | tf_op jit(solution)/shard_map/ppermute | solution.py:96
  35.5 3.4 %collective-permute-start.12 = (bf16[2,320,128]{2,1,0:T(8,128)(2,1)S(1)}, bf16[2,320,128]{2,1,0:T(8,128)(2,1)S(1)}, u32[]{:S(2)}, u32[]{:S(2)}) collective-permute-start(bf16[2,320,128]{2,1,0:T(8,128)(2,1)S(1)} %pad_maximum_fusion), channel_id=1, source_target_pairs={{0,0},{1,8},{2,2},{3,10},{4,4},{5,12},{6,6},{7,14},{8,1},{9,9},{10... | collective-permute-start | bytes 491528 | tf_op jit(solution)/shard_map/ppermute | solution.py:96
  38.9 1.4 %collective-permute-start.13 = (bf16[2,320,128]{2,1,0:T(8,128)(2,1)S(1)}, bf16[2,320,128]{2,1,0:T(8,128)(2,1)S(1)}, u32[]{:S(2)}, u32[]{:S(2)}) collective-permute-start(bf16[2,320,128]{2,1,0:T(8,128)(2,1)S(1)} %pad_maximum_fusion.1), channel_id=1, source_target_pairs={{0,2},{1,10},{2,0},{3,8},{4,6},{5,14},{6,4},{7,12},{8,3},{9,11},{1... | collective-permute-start | bytes 491528 | tf_op jit(solution)/shard_map/ppermute | solution.py:96
  40.3 1.4 %collective-permute-start.16 = (bf16[1,320,128]{2,1,0:T(8,128)(2,1)S(1)}, bf16[1,320,128]{2,1,0:T(8,128)(2,1)S(1)}, u32[]{:S(2)}, u32[]{:S(2)}) collective-permute-start(bf16[1,320,128]{2,1,0:T(8,128)(2,1)S(1)} %get-tuple-element.30), channel_id=1, source_target_pairs={{0,6},{1,14},{2,4},{3,12},{4,2},{5,10},{6,0},{7,8},{8,7},{9,15},{1... | collective-permute-start | bytes 245768 | tf_op jit(solution)/shard_map/ppermute | solution.py:96
  41.6 2.1 %collective-permute-start.15 = (bf16[1,320,128]{2,1,0:T(8,128)(2,1)S(1)}, bf16[1,320,128]{2,1,0:T(8,128)(2,1)S(1)}, u32[]{:S(2)}, u32[]{:S(2)}) collective-permute-start(bf16[1,320,128]{2,1,0:T(8,128)(2,1)S(1)} %get-tuple-element.33), channel_id=1, source_target_pairs={{0,4},{1,12},{2,6},{3,14},{4,0},{5,8},{6,2},{7,10},{8,5},{9,13},{1... | collective-permute-start | bytes 245768 | tf_op jit(solution)/shard_map/ppermute | solution.py:96
  43.7 2.5 %collective-permute-start.14 = (bf16[1,320,128]{2,1,0:T(8,128)(2,1)S(1)}, bf16[1,320,128]{2,1,0:T(8,128)(2,1)S(1)}, u32[]{:S(2)}, u32[]{:S(2)}) collective-permute-start(bf16[1,320,128]{2,1,0:T(8,128)(2,1)S(1)} %get-tuple-element.34), channel_id=1, source_target_pairs={{0,6},{1,14},{2,4},{3,12},{4,2},{5,10},{6,0},{7,8},{8,7},{9,15},{1... | collective-permute-start | bytes 245768 | tf_op jit(solution)/shard_map/ppermute | solution.py:96
  46.2 3.4 %collective-permute-done.16.refs_4_ = bf16[1,320,128]{2,1,0:T(8,128)(2,1)S(1)} collective-permute-done((bf16[1,320,128]{2,1,0:T(8,128)(2,1)S(1)}, bf16[1,320,128]{2,1,0:T(8,128)(2,1)S(1)}, u32[]{:S(2)}, u32[]{:S(2)}) %collective-permute-start.16) | collective-permute-done | bytes 81952 | tf_op jit(solution)/shard_map/ppermute | solution.py:96
  49.6 0.7 %collective-permute-done.15.refs_3_ = bf16[1,320,128]{2,1,0:T(8,128)(2,1)S(1)} collective-permute-done((bf16[1,320,128]{2,1,0:T(8,128)(2,1)S(1)}, bf16[1,320,128]{2,1,0:T(8,128)(2,1)S(1)}, u32[]{:S(2)}, u32[]{:S(2)}) %collective-permute-start.15) | collective-permute-done | bytes 81952 | tf_op jit(solution)/shard_map/ppermute | solution.py:96
  50.3 2.3 %collective-permute-done.14.refs_2_ = bf16[1,320,128]{2,1,0:T(8,128)(2,1)S(1)} collective-permute-done((bf16[1,320,128]{2,1,0:T(8,128)(2,1)S(1)}, bf16[1,320,128]{2,1,0:T(8,128)(2,1)S(1)}, u32[]{:S(2)}, u32[]{:S(2)}) %collective-permute-start.14) | collective-permute-done | bytes 81952 | tf_op jit(solution)/shard_map/ppermute | solution.py:96
  52.6 0.9 %join.1 = bf16[320,1024]{1,0:T(8,128)(2,1)} custom-call(bf16[2,320,128]{2,1,0:T(8,128)(2,1)S(1)} %collective-permute-done.12.refs_0_, bf16[2,320,128]{2,1,0:T(8,128)(2,1)S(1)} %collective-permute-done.13.refs_1_, bf16[1,320,128]{2,1,0:T(8,128)(2,1)S(1)} %collective-permute-done.14.refs_2_, bf16[1,320,128]{2,1,0:T(8,128)(2,1)S(1)} %collective-permute-done.15.refs_3_, ...), custom_call_target="tpu_custom_call" | custom-call | tf_op jit(solution)/shard_map/join/pallas_call | solution.py:179
  (21 shorter events, 1.4 us)
Async XLA Ops:
  2.0 24.6 %copy-start = (f32[4,320]{1,0:T(4,128)S(1)}, f32[4,320]{1,0:T(4,128)}, u32[]{:S(2)}) copy-start(f32[4,320]{1,0:T(4,128)} %refs_13_.1) | copy-start | bytes 15364
  2.0 20.1 %collective-permute-start = (bf16[336,1280]{1,0:T(8,128)(2,1)S(1)}, bf16[336,1280]{1,0:T(8,128)(2,1)S(1)}, u32[]{:S(2)}, u32[]{:S(2)}) collective-permute-start(bf16[336,1280]{1,0:T(8,128)(2,1)S(1)} %get-tuple-element.17.refs_8_), channel_id=1, source_target_pairs={{0,16},{1,17},{2,18},{3,19},{4,20},{5,21},{6,22},{7,23},{8,24},{9,... | collective-permute-start | bytes 2580488 | tf_op jit(solution)/shard_map/ppermute | solution.py:96
  3.3 12.8 %collective-permute-start.1 = (bf16[2,320,128]{2,1,0:T(8,128)(2,1)S(1)}, bf16[2,320,128]{2,1,0:T(8,128)(2,1)S(1)}, u32[]{:S(2)}, u32[]{:S(2)}) collective-permute-start(bf16[2,320,128]{2,1,0:T(8,128)(2,1)S(1)} %get-tuple-element.18), channel_id=1, source_target_pairs={{0,4},{1,12},{2,6},{3,14},{4,0},{5,8},{6,2},{7,10},{8,5},{9,13},{1... | collective-permute-start | bytes 491528 | tf_op jit(solution)/shard_map/ppermute | solution.py:96
  5.1 16.5 %collective-permute-start.2 = (bf16[2,320,128]{2,1,0:T(8,128)(2,1)S(1)}, bf16[2,320,128]{2,1,0:T(8,128)(2,1)S(1)}, u32[]{:S(2)}, u32[]{:S(2)}) collective-permute-start(bf16[2,320,128]{2,1,0:T(8,128)(2,1)S(1)} %get-tuple-element.19), channel_id=1, source_target_pairs={{0,6},{1,14},{2,4},{3,12},{4,2},{5,10},{6,0},{7,8},{8,7},{9,15},{1... | collective-permute-start | bytes 491528 | tf_op jit(solution)/shard_map/ppermute | solution.py:96
  7.0 14.7 %collective-permute-start.3 = (bf16[2,320,128]{2,1,0:T(8,128)(2,1)S(1)}, bf16[2,320,128]{2,1,0:T(8,128)(2,1)S(1)}, u32[]{:S(2)}, u32[]{:S(2)}) collective-permute-start(bf16[2,320,128]{2,1,0:T(8,128)(2,1)S(1)} %get-tuple-element.20), channel_id=1, source_target_pairs={{0,2},{1,10},{2,0},{3,8},{4,6},{5,14},{6,4},{7,12},{8,3},{9,11},{1... | collective-permute-start | bytes 491528 | tf_op jit(solution)/shard_map/ppermute | solution.py:96
  9.8 11.8 %collective-permute-start.4 = (bf16[2,320,128]{2,1,0:T(8,128)(2,1)S(1)}, bf16[2,320,128]{2,1,0:T(8,128)(2,1)S(1)}, u32[]{:S(2)}, u32[]{:S(2)}) collective-permute-start(bf16[2,320,128]{2,1,0:T(8,128)(2,1)S(1)} %get-tuple-element.21), channel_id=1, source_target_pairs={{0,0},{1,8},{2,2},{3,10},{4,4},{5,12},{6,6},{7,14},{8,1},{9,9},{10... | collective-permute-start | bytes 491528 | tf_op jit(solution)/shard_map/ppermute | solution.py:96
  16.1 8.0 %collective-permute-start.9 = (bf16[336,1280]{1,0:T(8,128)(2,1)S(1)}, bf16[336,1280]{1,0:T(8,128)(2,1)S(1)}, u32[]{:S(2)}, u32[]{:S(2)}) collective-permute-start(bf16[336,1280]{1,0:T(8,128)(2,1)S(1)} %get-tuple-element.17.refs_8_), channel_id=1, source_target_pairs={{0,8},{1,9},{2,10},{3,11},{4,12},{5,13},{6,14},{7,15},{8,0},{9,1},... | collective-permute-start | bytes 2580488 | tf_op jit(solution)/shard_map/ppermute | solution.py:96
  22.1 4.5 %collective-permute-start.10 = (bf16[336,1280]{1,0:T(8,128)(2,1)S(1)}, bf16[336,1280]{1,0:T(8,128)(2,1)S(1)}, u32[]{:S(2)}, u32[]{:S(2)}) collective-permute-start(bf16[336,1280]{1,0:T(8,128)(2,1)S(1)} %collective-permute-done.refs_10_), channel_id=1, source_target_pairs={{0,8},{1,9},{2,10},{3,11},{4,12},{5,13},{6,14},{7,15},{8,0},{9,1},... | collective-permute-start | bytes 2580488 | tf_op jit(solution)/shard_map/ppermute | solution.py:96
  23.6 2.3 %collective-permute-start.5 = (bf16[2,320,128]{2,1,0:T(8,128)(2,1)S(1)}, bf16[2,320,128]{2,1,0:T(8,128)(2,1)S(1)}, u32[]{:S(2)}, u32[]{:S(2)}) collective-permute-start(bf16[2,320,128]{2,1,0:T(8,128)(2,1)S(1)} %collective-permute-done.1.refs_0_), channel_id=1, source_target_pairs={{0,8},{1,9},{2,10},{3,11},{4,12},{5,13},{6,14},{7,15},{8,0},{9,1},... | collective-permute-start | bytes 491528 | tf_op jit(solution)/shard_map/ppermute | solution.py:96
  23.6 2.5 %collective-permute-start.6 = (bf16[2,320,128]{2,1,0:T(8,128)(2,1)S(1)}, bf16[2,320,128]{2,1,0:T(8,128)(2,1)S(1)}, u32[]{:S(2)}, u32[]{:S(2)}) collective-permute-start(bf16[2,320,128]{2,1,0:T(8,128)(2,1)S(1)} %collective-permute-done.2.refs_1_), channel_id=1, source_target_pairs={{0,8},{1,9},{2,10},{3,11},{4,12},{5,13},{6,14},{7,15},{8,0},{9,1},... | collective-permute-start | bytes 491528 | tf_op jit(solution)/shard_map/ppermute | solution.py:96
  24.1 2.2 %collective-permute-start.7 = (bf16[2,320,128]{2,1,0:T(8,128)(2,1)S(1)}, bf16[2,320,128]{2,1,0:T(8,128)(2,1)S(1)}, u32[]{:S(2)}, u32[]{:S(2)}) collective-permute-start(bf16[2,320,128]{2,1,0:T(8,128)(2,1)S(1)} %collective-permute-done.3.refs_2_), channel_id=1, source_target_pairs={{0,8},{1,9},{2,10},{3,11},{4,12},{5,13},{6,14},{7,15},{8,0},{9,1},... | collective-permute-start | bytes 491528 | tf_op jit(solution)/shard_map/ppermute | solution.py:96
  24.1 2.4 %collective-permute-start.8 = (bf16[2,320,128]{2,1,0:T(8,128)(2,1)S(1)}, bf16[2,320,128]{2,1,0:T(8,128)(2,1)S(1)}, u32[]{:S(2)}, u32[]{:S(2)}) collective-permute-start(bf16[2,320,128]{2,1,0:T(8,128)(2,1)S(1)} %collective-permute-done.4.refs_3_), channel_id=1, source_target_pairs={{0,8},{1,9},{2,10},{3,11},{4,12},{5,13},{6,14},{7,15},{8,0},{9,1},... | collective-permute-start | bytes 491528 | tf_op jit(solution)/shard_map/ppermute | solution.py:96
  33.7 1.7 %collective-permute-start.11 = (bf16[4,320,128]{2,1,0:T(8,128)(2,1)S(1)}, bf16[4,320,128]{2,1,0:T(8,128)(2,1)S(1)}, u32[]{:S(2)}, u32[]{:S(2)}) collective-permute-start(bf16[4,320,128]{2,1,0:T(8,128)(2,1)S(1)} %get-tuple-element.28), channel_id=1, source_target_pairs={{0,8},{1,9},{2,10},{3,11},{4,12},{5,13},{6,14},{7,15},{8,0},{9,1},... | collective-permute-start | bytes 983048 | tf_op jit(solution)/shard_map/ppermute | solution.py:96
  34.2 9.5 %collective-permute-start.17 = (bf16[1,320,128]{2,1,0:T(8,128)(2,1)S(1)}, bf16[1,320,128]{2,1,0:T(8,128)(2,1)S(1)}, u32[]{:S(2)}, u32[]{:S(2)}) collective-permute-start(bf16[1,320,128]{2,1,0:T(8,128)(2,1)S(1)} %get-tuple-element.29), channel_id=1, source_target_pairs={{0,4},{1,12},{2,6},{3,14},{4,0},{5,8},{6,2},{7,10},{8,5},{9,13},{1... | collective-permute-start | bytes 245768 | tf_op jit(solution)/shard_map/ppermute | solution.py:96
  35.5 17.1 %collective-permute-start.12 = (bf16[2,320,128]{2,1,0:T(8,128)(2,1)S(1)}, bf16[2,320,128]{2,1,0:T(8,128)(2,1)S(1)}, u32[]{:S(2)}, u32[]{:S(2)}) collective-permute-start(bf16[2,320,128]{2,1,0:T(8,128)(2,1)S(1)} %pad_maximum_fusion), channel_id=1, source_target_pairs={{0,0},{1,8},{2,2},{3,10},{4,4},{5,12},{6,6},{7,14},{8,1},{9,9},{10... | collective-permute-start | bytes 491528 | tf_op jit(solution)/shard_map/ppermute | solution.py:96
  38.9 13.7 %collective-permute-start.13 = (bf16[2,320,128]{2,1,0:T(8,128)(2,1)S(1)}, bf16[2,320,128]{2,1,0:T(8,128)(2,1)S(1)}, u32[]{:S(2)}, u32[]{:S(2)}) collective-permute-start(bf16[2,320,128]{2,1,0:T(8,128)(2,1)S(1)} %pad_maximum_fusion.1), channel_id=1, source_target_pairs={{0,2},{1,10},{2,0},{3,8},{4,6},{5,14},{6,4},{7,12},{8,3},{9,11},{1... | collective-permute-start | bytes 491528 | tf_op jit(solution)/shard_map/ppermute | solution.py:96
  40.3 9.4 %collective-permute-start.16 = (bf16[1,320,128]{2,1,0:T(8,128)(2,1)S(1)}, bf16[1,320,128]{2,1,0:T(8,128)(2,1)S(1)}, u32[]{:S(2)}, u32[]{:S(2)}) collective-permute-start(bf16[1,320,128]{2,1,0:T(8,128)(2,1)S(1)} %get-tuple-element.30), channel_id=1, source_target_pairs={{0,6},{1,14},{2,4},{3,12},{4,2},{5,10},{6,0},{7,8},{8,7},{9,15},{1... | collective-permute-start | bytes 245768 | tf_op jit(solution)/shard_map/ppermute | solution.py:96
  41.6 8.6 %collective-permute-start.15 = (bf16[1,320,128]{2,1,0:T(8,128)(2,1)S(1)}, bf16[1,320,128]{2,1,0:T(8,128)(2,1)S(1)}, u32[]{:S(2)}, u32[]{:S(2)}) collective-permute-start(bf16[1,320,128]{2,1,0:T(8,128)(2,1)S(1)} %get-tuple-element.33), channel_id=1, source_target_pairs={{0,4},{1,12},{2,6},{3,14},{4,0},{5,8},{6,2},{7,10},{8,5},{9,13},{1... | collective-permute-start | bytes 245768 | tf_op jit(solution)/shard_map/ppermute | solution.py:96
  43.7 8.9 %collective-permute-start.14 = (bf16[1,320,128]{2,1,0:T(8,128)(2,1)S(1)}, bf16[1,320,128]{2,1,0:T(8,128)(2,1)S(1)}, u32[]{:S(2)}, u32[]{:S(2)}) collective-permute-start(bf16[1,320,128]{2,1,0:T(8,128)(2,1)S(1)} %get-tuple-element.34), channel_id=1, source_target_pairs={{0,6},{1,14},{2,4},{3,12},{4,2},{5,10},{6,0},{7,8},{8,7},{9,15},{1... | collective-permute-start | bytes 245768 | tf_op jit(solution)/shard_map/ppermute | solution.py:96

commit v6 on v5

--- a/solution.py
+++ b/solution.py
@@ -154,6 +154,23 @@
     )(times, own, taps, projection, film_weight)
 
 
+def pick_kernel(*refs):
+    other = 1 - lax.axis_index("segment") % 2
+    for n, block in enumerate(refs[:-1]):
+        refs[-1][n] = block[other]
+
+
+def pick_others(blocks):
+    vmem = pl.BlockSpec(memory_space=pltpu.VMEM)
+    return pl.pallas_call(
+        pick_kernel,
+        out_shape=pltpu.VMEM((len(blocks), *blocks[0].shape[1:]), BF),
+        in_specs=[vmem] * len(blocks),
+        out_specs=vmem,
+        name="pick",
+    )(*pin(blocks, pltpu.VMEM))
+
+
 def join_kernel(parts, *refs):
     blocks, out, joined, sem = refs[: len(parts)], *refs[len(parts) :]
     frame = lax.axis_index("frame")
@@ -197,7 +214,7 @@
         del refs[:count]
         return taken
 
-    turned, swapped = take(len(loaded)), take(len(loaded))
+    turned, (swapped,) = take(len(loaded)), take(1)
     packs = take(4)
     skip_in, gain_ref = take(2)
     kept, given = take(2)
@@ -251,7 +268,7 @@
     one, zero = with_one.at[64 + width :, :], with_first.at[64 + width :, :]
     for n, d in enumerate(loaded):
         for k in range(2):
-            zero[:, lanes_of(d, k)] = (turned, swapped)[k][n][core]
+            zero[:, lanes_of(d, k)] = turned[n][core] if k == 0 else swapped[n]
 
     for s in range(4):
         source, target = ((zero, one), (one, two), (two, three), (three, last))[s]
@@ -299,8 +316,8 @@
     width = gain.shape[1]
     columns = frames * LANES
     vmem = pl.BlockSpec(memory_space=pltpu.VMEM)
-    blocks = [*turned, *swapped]
-    places = [pltpu.VMEM] * 4 + [pltpu.HBM]
+    blocks = [*turned, swapped]
+    places = [pltpu.VMEM, pltpu.HBM, pltpu.VMEM, pltpu.VMEM, pltpu.HBM]
     inputs = [pin([a], place)[0] for a, place in zip([*weights, skip], places, strict=True)]
     return pl.pallas_call(
         functools.partial(sections_kernel, dests, levels, width, loaded),
@@ -343,9 +360,10 @@
     pack2 = swap_planes(pack0)
     turned = [turn(cut[d], d) for d in IN_ORDER]
     pack1 = swap_cores(pack0)
-    pack2, *turned = lax.optimization_barrier((pack2, *turned))
+    picked = pick_others(turned)
+    pack2, picked = lax.optimization_barrier((pack2, picked))
+    swapped = swap_cores(picked)
     pack3 = swap_cores(pack2)
-    swapped = [swap_cores(block) for block in turned]
 
     weights = [pack0, pack1, pack2, pack3]
     kept, given = run_sections(

time: 54.5 us -> 54.3 us (level)
  starting transfers between devices: 24.5 us -> 23.2 us
    ppermute x18 -> x15, starting transfers between devices: 24.5 us -> 23.2 us  [move(): return lax.ppermute(array, ('segment', 'frame'), pairs)]
    ppermute x18 -> x15, waiting for transfers between devices: 18.8 us -> 19.2 us  [move(): return lax.ppermute(array, ('segment', 'frame'), pairs)]
  transfers between devices with their start and end apart: 18 -> 15, of which waited for: 11 -> 8; matrix products, arithmetic and copies ran while one was open for 0% -> 0% of each run, Pallas kernels for 0% -> 0%
where the time goes in v6:
time: 54.3 us; the launch traced here: 53.2 us
  starting transfers between devices  23.2 us (43%)
  waiting for transfers between devices  19.2 us (35%)
  Pallas kernels  10.6 us (20%)
    ppermute x15, starting transfers between devices, move(): return lax.ppermute(array, ('segment', 'frame'), pairs)  23.2 us
    ppermute x15, waiting for transfers between devices, move(): return lax.ppermute(array, ('segment', 'frame'), pairs)  19.2 us
    pallas_call x1, Pallas kernels, run_sections(): pl.pallas_call(functools.partial(sections_kernel, dests, levels, width, l...  7.71 us
    pallas_call x1, Pallas kernels, pack_and_cut(): pl.pallas_call(functools.partial(pack_kernel, levels), out_shape=[pltpu.V...  1.98 us
  transfers between devices with their start and end apart: 15, of which 8 were waited for; matrix products, arithmetic and copies ran while one was open for 0% of the time, Pallas kernels for 0%

profile of v6, /device:TPU:17, one launch (start us, length us, event | category | flops | bytes accessed | tf_op | source)
XLA Modules:
  0.0 53.2 jit_solution(15880012154597707140)
XLA Ops:
  0.0 2.0 %pack.1 = (bf16[2,320,128]{2,1,0:T(8,128)(2,1)S(1)}, bf16[2,320,128]{2,1,0:T(8,128)(2,1)S(1)}, bf16[2,320,128]{2,1,0:T(8,128)(2,1)S(1)}, bf16[2,320,128]{2,1,0:T(8,128)(2,1)S(1)}, bf16[336,1280]{1,0:T(8,128)(2,1)S(1)}) custom-call(s32[4]{0:T(128)} %times_ref.1, bf16[320,1024]{1,0:T(8,128)(2,1)} %bitcast.6, bf16[3,320,320]{2,1,0:T(8,128)(2,1)} %bitcast.5, ...), custom_call_target="tpu_custom_call" | custom-call | tf_op jit(solution)/shard_map/pack/pallas_call | solution.py:147
  2.0 1.3 %collective-permute-start.4 = (bf16[336,1280]{1,0:T(8,128)(2,1)S(1)}, bf16[336,1280]{1,0:T(8,128)(2,1)S(1)}, u32[]{:S(2)}, u32[]{:S(2)}) collective-permute-start(bf16[336,1280]{1,0:T(8,128)(2,1)S(1)} %get-tuple-element.18.refs_5_), channel_id=1, source_target_pairs={{0,16},{1,17},{2,18},{3,19},{4,20},{5,21},{6,22},{7,23},{8,24},{9,... | collective-permute-start | bytes 2580488 | tf_op jit(solution)/shard_map/ppermute | solution.py:96
  3.3 1.8 %collective-permute-start = (bf16[2,320,128]{2,1,0:T(8,128)(2,1)S(1)}, bf16[2,320,128]{2,1,0:T(8,128)(2,1)S(1)}, u32[]{:S(2)}, u32[]{:S(2)}) collective-permute-start(bf16[2,320,128]{2,1,0:T(8,128)(2,1)S(1)} %get-tuple-element.14), channel_id=1, source_target_pairs={{0,4},{1,12},{2,6},{3,14},{4,0},{5,8},{6,2},{7,10},{8,5},{9,13},{1... | collective-permute-start | bytes 491528 | tf_op jit(solution)/shard_map/ppermute | solution.py:96
  5.1 1.8 %collective-permute-start.1 = (bf16[2,320,128]{2,1,0:T(8,128)(2,1)S(1)}, bf16[2,320,128]{2,1,0:T(8,128)(2,1)S(1)}, u32[]{:S(2)}, u32[]{:S(2)}) collective-permute-start(bf16[2,320,128]{2,1,0:T(8,128)(2,1)S(1)} %get-tuple-element.15), channel_id=1, source_target_pairs={{0,6},{1,14},{2,4},{3,12},{4,2},{5,10},{6,0},{7,8},{8,7},{9,15},{1... | collective-permute-start | bytes 491528 | tf_op jit(solution)/shard_map/ppermute | solution.py:96
  7.0 2.8 %collective-permute-start.2 = (bf16[2,320,128]{2,1,0:T(8,128)(2,1)S(1)}, bf16[2,320,128]{2,1,0:T(8,128)(2,1)S(1)}, u32[]{:S(2)}, u32[]{:S(2)}) collective-permute-start(bf16[2,320,128]{2,1,0:T(8,128)(2,1)S(1)} %get-tuple-element.16), channel_id=1, source_target_pairs={{0,2},{1,10},{2,0},{3,8},{4,6},{5,14},{6,4},{7,12},{8,3},{9,11},{1... | collective-permute-start | bytes 491528 | tf_op jit(solution)/shard_map/ppermute | solution.py:96
  9.8 2.0 %collective-permute-start.3 = (bf16[2,320,128]{2,1,0:T(8,128)(2,1)S(1)}, bf16[2,320,128]{2,1,0:T(8,128)(2,1)S(1)}, u32[]{:S(2)}, u32[]{:S(2)}) collective-permute-start(bf16[2,320,128]{2,1,0:T(8,128)(2,1)S(1)} %get-tuple-element.17), channel_id=1, source_target_pairs={{0,0},{1,8},{2,2},{3,10},{4,4},{5,12},{6,6},{7,14},{8,1},{9,9},{10... | collective-permute-start | bytes 491528 | tf_op jit(solution)/shard_map/ppermute | solution.py:96
  11.8 4.3 %collective-permute-done.refs_0_ = bf16[2,320,128]{2,1,0:T(8,128)(2,1)S(1)} collective-permute-done((bf16[2,320,128]{2,1,0:T(8,128)(2,1)S(1)}, bf16[2,320,128]{2,1,0:T(8,128)(2,1)S(1)}, u32[]{:S(2)}, u32[]{:S(2)}) %collective-permute-start) | collective-permute-done | bytes 163872 | tf_op jit(solution)/shard_map/ppermute | solution.py:96
  16.1 5.5 %collective-permute-done.1.refs_1_ = bf16[2,320,128]{2,1,0:T(8,128)(2,1)S(1)} collective-permute-done((bf16[2,320,128]{2,1,0:T(8,128)(2,1)S(1)}, bf16[2,320,128]{2,1,0:T(8,128)(2,1)S(1)}, u32[]{:S(2)}, u32[]{:S(2)}) %collective-permute-start.1) | collective-permute-done | bytes 163872 | tf_op jit(solution)/shard_map/ppermute | solution.py:96
  21.7 0.4 collective-permute-done.4.refs_7_
  22.0 1.5 %collective-permute-start.7 = (bf16[336,1280]{1,0:T(8,128)(2,1)S(1)}, bf16[336,1280]{1,0:T(8,128)(2,1)S(1)}, u32[]{:S(2)}, u32[]{:S(2)}) collective-permute-start(bf16[336,1280]{1,0:T(8,128)(2,1)S(1)} %collective-permute-done.4.refs_7_), channel_id=1, source_target_pairs={{0,8},{1,9},{2,10},{3,11},{4,12},{5,13},{6,14},{7,15},{8,0},{9,1},... | collective-permute-start | bytes 2580488 | tf_op jit(solution)/shard_map/ppermute | solution.py:96
  23.6 2.5 %collective-permute-done.5.refs_4_ = bf16[4,320,128]{2,1,0:T(8,128)(2,1)S(1)} collective-permute-done((bf16[4,320,128]{2,1,0:T(8,128)(2,1)S(1)}, bf16[4,320,128]{2,1,0:T(8,128)(2,1)S(1)}, u32[]{:S(2)}, u32[]{:S(2)}) %collective-permute-start.5) | collective-permute-done | bytes 327712 | tf_op jit(solution)/shard_map/ppermute | solution.py:96
  26.1 7.7 %sections.1 = (bf16[4,320,128]{2,1,0:T(8,128)(2,1)S(1)}, bf16[4,320,128]{2,1,0:T(8,128)(2,1)S(1)}) custom-call(bf16[2,320,128]{2,1,0:T(8,128)(2,1)S(1)} %collective-permute-done.refs_0_, bf16[2,320,128]{2,1,0:T(8,128)(2,1)S(1)} %collective-permute-done.1.refs_1_, bf16[2,320,128]{2,1,0:T(8,128)(2,1)S(1)} %collective-permute-done.2.refs_2_, ...), custom_call_target="tpu_custom_call" | custom-call | flops 3774873600 | bytes 4194304 | tf_op jit(solution)/shard_map/sections/pallas_call | solution.py:322
  33.8 0.1 collective-permute-start.8
  33.9 1.4 %collective-permute-start.14 = (bf16[1,320,128]{2,1,0:T(8,128)(2,1)S(1)}, bf16[1,320,128]{2,1,0:T(8,128)(2,1)S(1)}, u32[]{:S(2)}, u32[]{:S(2)}) collective-permute-start(bf16[1,320,128]{2,1,0:T(8,128)(2,1)S(1)} %get-tuple-element.23), channel_id=1, source_target_pairs={{0,4},{1,12},{2,6},{3,14},{4,0},{5,8},{6,2},{7,10},{8,5},{9,13},{1... | collective-permute-start | bytes 245768 | tf_op jit(solution)/shard_map/ppermute | solution.py:96
  35.3 0.2 collective-permute-done.8
  35.5 3.1 %collective-permute-start.9 = (bf16[2,320,128]{2,1,0:T(8,128)(2,1)S(1)}, bf16[2,320,128]{2,1,0:T(8,128)(2,1)S(1)}, u32[]{:S(2)}, u32[]{:S(2)}) collective-permute-start(bf16[2,320,128]{2,1,0:T(8,128)(2,1)S(1)} %pad_maximum_fusion), channel_id=1, source_target_pairs={{0,0},{1,8},{2,2},{3,10},{4,4},{5,12},{6,6},{7,14},{8,1},{9,9},{10... | collective-permute-start | bytes 491528 | tf_op jit(solution)/shard_map/ppermute | solution.py:96
  38.7 1.6 %collective-permute-start.10 = (bf16[2,320,128]{2,1,0:T(8,128)(2,1)S(1)}, bf16[2,320,128]{2,1,0:T(8,128)(2,1)S(1)}, u32[]{:S(2)}, u32[]{:S(2)}) collective-permute-start(bf16[2,320,128]{2,1,0:T(8,128)(2,1)S(1)} %pad_maximum_fusion.1), channel_id=1, source_target_pairs={{0,2},{1,10},{2,0},{3,8},{4,6},{5,14},{6,4},{7,12},{8,3},{9,11},{1... | collective-permute-start | bytes 491528 | tf_op jit(solution)/shard_map/ppermute | solution.py:96
  40.3 1.1 %collective-permute-start.13 = (bf16[1,320,128]{2,1,0:T(8,128)(2,1)S(1)}, bf16[1,320,128]{2,1,0:T(8,128)(2,1)S(1)}, u32[]{:S(2)}, u32[]{:S(2)}) collective-permute-start(bf16[1,320,128]{2,1,0:T(8,128)(2,1)S(1)} %get-tuple-element.24), channel_id=1, source_target_pairs={{0,6},{1,14},{2,4},{3,12},{4,2},{5,10},{6,0},{7,8},{8,7},{9,15},{1... | collective-permute-start | bytes 245768 | tf_op jit(solution)/shard_map/ppermute | solution.py:96
  41.4 2.4 %collective-permute-start.12 = (bf16[1,320,128]{2,1,0:T(8,128)(2,1)S(1)}, bf16[1,320,128]{2,1,0:T(8,128)(2,1)S(1)}, u32[]{:S(2)}, u32[]{:S(2)}) collective-permute-start(bf16[1,320,128]{2,1,0:T(8,128)(2,1)S(1)} %get-tuple-element.27), channel_id=1, source_target_pairs={{0,4},{1,12},{2,6},{3,14},{4,0},{5,8},{6,2},{7,10},{8,5},{9,13},{1... | collective-permute-start | bytes 245768 | tf_op jit(solution)/shard_map/ppermute | solution.py:96
  43.7 2.1 %collective-permute-start.11 = (bf16[1,320,128]{2,1,0:T(8,128)(2,1)S(1)}, bf16[1,320,128]{2,1,0:T(8,128)(2,1)S(1)}, u32[]{:S(2)}, u32[]{:S(2)}) collective-permute-start(bf16[1,320,128]{2,1,0:T(8,128)(2,1)S(1)} %get-tuple-element.28), channel_id=1, source_target_pairs={{0,6},{1,14},{2,4},{3,12},{4,2},{5,10},{6,0},{7,8},{8,7},{9,15},{1... | collective-permute-start | bytes 245768 | tf_op jit(solution)/shard_map/ppermute | solution.py:96
  45.9 3.6 %collective-permute-done.13.refs_4_ = bf16[1,320,128]{2,1,0:T(8,128)(2,1)S(1)} collective-permute-done((bf16[1,320,128]{2,1,0:T(8,128)(2,1)S(1)}, bf16[1,320,128]{2,1,0:T(8,128)(2,1)S(1)}, u32[]{:S(2)}, u32[]{:S(2)}) %collective-permute-start.13) | collective-permute-done | bytes 81952 | tf_op jit(solution)/shard_map/ppermute | solution.py:96
  49.5 0.7 %collective-permute-done.12.refs_3_ = bf16[1,320,128]{2,1,0:T(8,128)(2,1)S(1)} collective-permute-done((bf16[1,320,128]{2,1,0:T(8,128)(2,1)S(1)}, bf16[1,320,128]{2,1,0:T(8,128)(2,1)S(1)}, u32[]{:S(2)}, u32[]{:S(2)}) %collective-permute-start.12) | collective-permute-done | bytes 81952 | tf_op jit(solution)/shard_map/ppermute | solution.py:96
  50.2 2.1 %collective-permute-done.11.refs_2_ = bf16[1,320,128]{2,1,0:T(8,128)(2,1)S(1)} collective-permute-done((bf16[1,320,128]{2,1,0:T(8,128)(2,1)S(1)}, bf16[1,320,128]{2,1,0:T(8,128)(2,1)S(1)}, u32[]{:S(2)}, u32[]{:S(2)}) %collective-permute-start.11) | collective-permute-done | bytes 81952 | tf_op jit(solution)/shard_map/ppermute | solution.py:96
  52.3 0.9 %join.1 = bf16[320,1024]{1,0:T(8,128)(2,1)} custom-call(bf16[2,320,128]{2,1,0:T(8,128)(2,1)S(1)} %collective-permute-done.9.refs_0_, bf16[2,320,128]{2,1,0:T(8,128)(2,1)S(1)} %collective-permute-done.10.refs_1_, bf16[1,320,128]{2,1,0:T(8,128)(2,1)S(1)} %collective-permute-done.11.refs_2_, bf16[1,320,128]{2,1,0:T(8,128)(2,1)S(1)} %collective-permute-done.12.refs_3_, ...), custom_call_target="tpu_custom_call" | custom-call | tf_op jit(solution)/shard_map/join/pallas_call | solution.py:196
  (16 shorter events, 0.1 us)
Async XLA Ops:
  2.0 20.1 %collective-permute-start.4 = (bf16[336,1280]{1,0:T(8,128)(2,1)S(1)}, bf16[336,1280]{1,0:T(8,128)(2,1)S(1)}, u32[]{:S(2)}, u32[]{:S(2)}) collective-permute-start(bf16[336,1280]{1,0:T(8,128)(2,1)S(1)} %get-tuple-element.18.refs_5_), channel_id=1, source_target_pairs={{0,16},{1,17},{2,18},{3,19},{4,20},{5,21},{6,22},{7,23},{8,24},{9,... | collective-permute-start | bytes 2580488 | tf_op jit(solution)/shard_map/ppermute | solution.py:96
  3.3 12.8 %collective-permute-start = (bf16[2,320,128]{2,1,0:T(8,128)(2,1)S(1)}, bf16[2,320,128]{2,1,0:T(8,128)(2,1)S(1)}, u32[]{:S(2)}, u32[]{:S(2)}) collective-permute-start(bf16[2,320,128]{2,1,0:T(8,128)(2,1)S(1)} %get-tuple-element.14), channel_id=1, source_target_pairs={{0,4},{1,12},{2,6},{3,14},{4,0},{5,8},{6,2},{7,10},{8,5},{9,13},{1... | collective-permute-start | bytes 491528 | tf_op jit(solution)/shard_map/ppermute | solution.py:96
  5.1 16.5 %collective-permute-start.1 = (bf16[2,320,128]{2,1,0:T(8,128)(2,1)S(1)}, bf16[2,320,128]{2,1,0:T(8,128)(2,1)S(1)}, u32[]{:S(2)}, u32[]{:S(2)}) collective-permute-start(bf16[2,320,128]{2,1,0:T(8,128)(2,1)S(1)} %get-tuple-element.15), channel_id=1, source_target_pairs={{0,6},{1,14},{2,4},{3,12},{4,2},{5,10},{6,0},{7,8},{8,7},{9,15},{1... | collective-permute-start | bytes 491528 | tf_op jit(solution)/shard_map/ppermute | solution.py:96
  7.0 14.7 %collective-permute-start.2 = (bf16[2,320,128]{2,1,0:T(8,128)(2,1)S(1)}, bf16[2,320,128]{2,1,0:T(8,128)(2,1)S(1)}, u32[]{:S(2)}, u32[]{:S(2)}) collective-permute-start(bf16[2,320,128]{2,1,0:T(8,128)(2,1)S(1)} %get-tuple-element.16), channel_id=1, source_target_pairs={{0,2},{1,10},{2,0},{3,8},{4,6},{5,14},{6,4},{7,12},{8,3},{9,11},{1... | collective-permute-start | bytes 491528 | tf_op jit(solution)/shard_map/ppermute | solution.py:96
  9.8 16.3 %copy-start = (f32[4,320]{1,0:T(4,128)S(1)}, f32[4,320]{1,0:T(4,128)}, u32[]{:S(2)}) copy-start(f32[4,320]{1,0:T(4,128)} %refs_10_.1) | copy-start | bytes 15364
  9.8 11.8 %collective-permute-start.3 = (bf16[2,320,128]{2,1,0:T(8,128)(2,1)S(1)}, bf16[2,320,128]{2,1,0:T(8,128)(2,1)S(1)}, u32[]{:S(2)}, u32[]{:S(2)}) collective-permute-start(bf16[2,320,128]{2,1,0:T(8,128)(2,1)S(1)} %get-tuple-element.17), channel_id=1, source_target_pairs={{0,0},{1,8},{2,2},{3,10},{4,4},{5,12},{6,6},{7,14},{8,1},{9,9},{10... | collective-permute-start | bytes 491528 | tf_op jit(solution)/shard_map/ppermute | solution.py:96
  16.1 7.5 %collective-permute-start.6 = (bf16[336,1280]{1,0:T(8,128)(2,1)S(1)}, bf16[336,1280]{1,0:T(8,128)(2,1)}, u32[]{:S(2)}, u32[]{:S(2)}) collective-permute-start(bf16[336,1280]{1,0:T(8,128)(2,1)S(1)} %get-tuple-element.18.refs_5_), channel_id=1, source_target_pairs={{0,8},{1,9},{2,10},{3,11},{4,12},{5,13},{6,14},{7,15},{8,0},{9,1},... | collective-permute-start | bytes 2580488 | tf_op jit(solution)/shard_map/ppermute | solution.py:96
  22.0 4.0 %collective-permute-start.7 = (bf16[336,1280]{1,0:T(8,128)(2,1)S(1)}, bf16[336,1280]{1,0:T(8,128)(2,1)S(1)}, u32[]{:S(2)}, u32[]{:S(2)}) collective-permute-start(bf16[336,1280]{1,0:T(8,128)(2,1)S(1)} %collective-permute-done.4.refs_7_), channel_id=1, source_target_pairs={{0,8},{1,9},{2,10},{3,11},{4,12},{5,13},{6,14},{7,15},{8,0},{9,1},... | collective-permute-start | bytes 2580488 | tf_op jit(solution)/shard_map/ppermute | solution.py:96
  23.6 2.5 %collective-permute-start.5 = (bf16[4,320,128]{2,1,0:T(8,128)(2,1)S(1)}, bf16[4,320,128]{2,1,0:T(8,128)(2,1)S(1)}, u32[]{:S(2)}, u32[]{:S(2)}) collective-permute-start(bf16[4,320,128]{2,1,0:T(8,128)(2,1)S(1)} %pick.1), channel_id=1, source_target_pairs={{0,8},{1,9},{2,10},{3,11},{4,12},{5,13},{6,14},{7,15},{8,0},{9,1},... | collective-permute-start | bytes 983048 | tf_op jit(solution)/shard_map/ppermute | solution.py:96
  33.8 1.7 %collective-permute-start.8 = (bf16[4,320,128]{2,1,0:T(8,128)(2,1)S(1)}, bf16[4,320,128]{2,1,0:T(8,128)(2,1)S(1)}, u32[]{:S(2)}, u32[]{:S(2)}) collective-permute-start(bf16[4,320,128]{2,1,0:T(8,128)(2,1)S(1)} %get-tuple-element.22), channel_id=1, source_target_pairs={{0,8},{1,9},{2,10},{3,11},{4,12},{5,13},{6,14},{7,15},{8,0},{9,1},... | collective-permute-start | bytes 983048 | tf_op jit(solution)/shard_map/ppermute | solution.py:96
  33.9 9.8 %collective-permute-start.14 = (bf16[1,320,128]{2,1,0:T(8,128)(2,1)S(1)}, bf16[1,320,128]{2,1,0:T(8,128)(2,1)S(1)}, u32[]{:S(2)}, u32[]{:S(2)}) collective-permute-start(bf16[1,320,128]{2,1,0:T(8,128)(2,1)S(1)} %get-tuple-element.23), channel_id=1, source_target_pairs={{0,4},{1,12},{2,6},{3,14},{4,0},{5,8},{6,2},{7,10},{8,5},{9,13},{1... | collective-permute-start | bytes 245768 | tf_op jit(solution)/shard_map/ppermute | solution.py:96
  35.5 16.8 %collective-permute-start.9 = (bf16[2,320,128]{2,1,0:T(8,128)(2,1)S(1)}, bf16[2,320,128]{2,1,0:T(8,128)(2,1)S(1)}, u32[]{:S(2)}, u32[]{:S(2)}) collective-permute-start(bf16[2,320,128]{2,1,0:T(8,128)(2,1)S(1)} %pad_maximum_fusion), channel_id=1, source_target_pairs={{0,0},{1,8},{2,2},{3,10},{4,4},{5,12},{6,6},{7,14},{8,1},{9,9},{10... | collective-permute-start | bytes 491528 | tf_op jit(solution)/shard_map/ppermute | solution.py:96
  38.7 13.6 %collective-permute-start.10 = (bf16[2,320,128]{2,1,0:T(8,128)(2,1)S(1)}, bf16[2,320,128]{2,1,0:T(8,128)(2,1)S(1)}, u32[]{:S(2)}, u32[]{:S(2)}) collective-permute-start(bf16[2,320,128]{2,1,0:T(8,128)(2,1)S(1)} %pad_maximum_fusion.1), channel_id=1, source_target_pairs={{0,2},{1,10},{2,0},{3,8},{4,6},{5,14},{6,4},{7,12},{8,3},{9,11},{1... | collective-permute-start | bytes 491528 | tf_op jit(solution)/shard_map/ppermute | solution.py:96
  40.3 9.2 %collective-permute-start.13 = (bf16[1,320,128]{2,1,0:T(8,128)(2,1)S(1)}, bf16[1,320,128]{2,1,0:T(8,128)(2,1)S(1)}, u32[]{:S(2)}, u32[]{:S(2)}) collective-permute-start(bf16[1,320,128]{2,1,0:T(8,128)(2,1)S(1)} %get-tuple-element.24), channel_id=1, source_target_pairs={{0,6},{1,14},{2,4},{3,12},{4,2},{5,10},{6,0},{7,8},{8,7},{9,15},{1... | collective-permute-start | bytes 245768 | tf_op jit(solution)/shard_map/ppermute | solution.py:96
  41.4 8.9 %collective-permute-start.12 = (bf16[1,320,128]{2,1,0:T(8,128)(2,1)S(1)}, bf16[1,320,128]{2,1,0:T(8,128)(2,1)S(1)}, u32[]{:S(2)}, u32[]{:S(2)}) collective-permute-start(bf16[1,320,128]{2,1,0:T(8,128)(2,1)S(1)} %get-tuple-element.27), channel_id=1, source_target_pairs={{0,4},{1,12},{2,6},{3,14},{4,0},{5,8},{6,2},{7,10},{8,5},{9,13},{1... | collective-permute-start | bytes 245768 | tf_op jit(solution)/shard_map/ppermute | solution.py:96
  43.7 8.6 %collective-permute-start.11 = (bf16[1,320,128]{2,1,0:T(8,128)(2,1)S(1)}, bf16[1,320,128]{2,1,0:T(8,128)(2,1)S(1)}, u32[]{:S(2)}, u32[]{:S(2)}) collective-permute-start(bf16[1,320,128]{2,1,0:T(8,128)(2,1)S(1)} %get-tuple-element.28), channel_id=1, source_target_pairs={{0,6},{1,14},{2,4},{3,12},{4,2},{5,10},{6,0},{7,8},{8,7},{9,15},{1... | collective-permute-start | bytes 245768 | tf_op jit(solution)/shard_map/ppermute | solution.py:96

commit v7 on v6

--- a/solution.py
+++ b/solution.py
@@ -232,8 +232,13 @@
             def _():
                 pltpu.make_async_copy(packs[b], weights.at[s], sem_w.at[s]).start()
 
-    load_weights(0)
+    def wait_weights(s):
+        pltpu.make_async_copy(packs[0], weights.at[s], sem_w.at[s]).wait()
+
+    for s in range(4):
+        load_weights(s)
     skip_load = pltpu.make_async_copy(skip_in, skip, sem_s)
+    skip_load.start()
 
     def lanes_of(d, k):
         slot = 2 * (z ^ d) + (core ^ k)
@@ -270,18 +275,20 @@
         for k in range(2):
             zero[:, lanes_of(d, k)] = turned[n][core] if k == 0 else swapped[n]
 
+    gain_columns = [column_of(gains, [s, 4 + s, 8 + s]) for s in range(4)]
     for s in range(4):
         source, target = ((zero, one), (one, two), (two, three), (three, last))[s]
-        gain = column_of(gains, [s, 4 + s, 8 + s])
+        gain = gain_columns[s]
         values = source[...].astype(F32)
         scale = lax.rsqrt(jnp.mean(values * values, axis=0, keepdims=True) + EPS)
         wide = jnp.concatenate([gain] * frames, axis=1)
         around[:, span(1, frames)] = (values * scale * wide).astype(BF)
-        pltpu.make_async_copy(packs[0], weights.at[s], sem_w.at[s]).wait()
-        if s < 3:
-            load_weights(s + 1)
         if s == 0:
-            skip_load.start()
+            wait_weights(0)
+        if s == 1:
+            for later in range(1, 4):
+                wait_weights(later)
+            skip_load.wait()
         half = 0.5 + 0.5 * column_of(weights[s, width:, 0:width], [clip, 4 + clip])
         half = jnp.concatenate([half] * frames, axis=1)
         three_frames = jnp.concatenate(
@@ -298,8 +305,6 @@
         projection = weights[s, 0:width, 3 * width - 64 :]
         right = beside[0 : 64 + width, :]
         if s >= 2:
-            if s == 2:
-                skip_load.wait()
             projection = jnp.concatenate([projection, skip[s - 2].T], axis=1)
             right = beside[...]
         total = source[...].astype(F32)

time: 54.3 us -> 53.3 us (0.982)
  Pallas kernels: 10.6 us -> 9.53 us
    pallas_call x1, Pallas kernels: 7.71 us -> 6.62 us  [run_sections(): pl.pallas_call(functools.partial(sections_kernel, dests, levels, width, l...]
where the time goes in v7:
time: 53.3 us; the launch traced here: 52.3 us
  starting transfers between devices  23.4 us (44%)
  waiting for transfers between devices  19.2 us (36%)
  Pallas kernels  9.53 us (18%)
    ppermute x15, starting transfers between devices, move(): return lax.ppermute(array, ('segment', 'frame'), pairs)  23.4 us
    ppermute x15, waiting for transfers between devices, move(): return lax.ppermute(array, ('segment', 'frame'), pairs)  19.2 us
    pallas_call x1, Pallas kernels, run_sections(): pl.pallas_call(functools.partial(sections_kernel, dests, levels, width, l...  6.62 us
    pallas_call x1, Pallas kernels, pack_and_cut(): pl.pallas_call(functools.partial(pack_kernel, levels), out_shape=[pltpu.V...  1.98 us
  transfers between devices with their start and end apart: 15, of which 8 were waited for; matrix products, arithmetic and copies ran while one was open for 0% of the time, Pallas kernels for 0%

profile of v7, /device:TPU:17, one launch (start us, length us, event | category | flops | bytes accessed | tf_op | source)
XLA Modules:
  0.0 52.3 jit_solution(11945293401258991055)
XLA Ops:
  0.0 2.0 %pack.1 = (bf16[2,320,128]{2,1,0:T(8,128)(2,1)S(1)}, bf16[2,320,128]{2,1,0:T(8,128)(2,1)S(1)}, bf16[2,320,128]{2,1,0:T(8,128)(2,1)S(1)}, bf16[2,320,128]{2,1,0:T(8,128)(2,1)S(1)}, bf16[336,1280]{1,0:T(8,128)(2,1)S(1)}) custom-call(s32[4]{0:T(128)} %times_ref.1, bf16[320,1024]{1,0:T(8,128)(2,1)} %bitcast.6, bf16[3,320,320]{2,1,0:T(8,128)(2,1)} %bitcast.5, ...), custom_call_target="tpu_custom_call" | custom-call | tf_op jit(solution)/shard_map/pack/pallas_call | solution.py:147
  2.0 1.3 %collective-permute-start.4 = (bf16[336,1280]{1,0:T(8,128)(2,1)S(1)}, bf16[336,1280]{1,0:T(8,128)(2,1)S(1)}, u32[]{:S(2)}, u32[]{:S(2)}) collective-permute-start(bf16[336,1280]{1,0:T(8,128)(2,1)S(1)} %get-tuple-element.18.refs_5_), channel_id=1, source_target_pairs={{0,16},{1,17},{2,18},{3,19},{4,20},{5,21},{6,22},{7,23},{8,24},{9,... | collective-permute-start | bytes 2580488 | tf_op jit(solution)/shard_map/ppermute | solution.py:96
  3.3 1.8 %collective-permute-start = (bf16[2,320,128]{2,1,0:T(8,128)(2,1)S(1)}, bf16[2,320,128]{2,1,0:T(8,128)(2,1)S(1)}, u32[]{:S(2)}, u32[]{:S(2)}) collective-permute-start(bf16[2,320,128]{2,1,0:T(8,128)(2,1)S(1)} %get-tuple-element.14), channel_id=1, source_target_pairs={{0,4},{1,12},{2,6},{3,14},{4,0},{5,8},{6,2},{7,10},{8,5},{9,13},{1... | collective-permute-start | bytes 491528 | tf_op jit(solution)/shard_map/ppermute | solution.py:96
  5.1 1.8 %collective-permute-start.1 = (bf16[2,320,128]{2,1,0:T(8,128)(2,1)S(1)}, bf16[2,320,128]{2,1,0:T(8,128)(2,1)S(1)}, u32[]{:S(2)}, u32[]{:S(2)}) collective-permute-start(bf16[2,320,128]{2,1,0:T(8,128)(2,1)S(1)} %get-tuple-element.15), channel_id=1, source_target_pairs={{0,6},{1,14},{2,4},{3,12},{4,2},{5,10},{6,0},{7,8},{8,7},{9,15},{1... | collective-permute-start | bytes 491528 | tf_op jit(solution)/shard_map/ppermute | solution.py:96
  7.0 2.8 %collective-permute-start.2 = (bf16[2,320,128]{2,1,0:T(8,128)(2,1)S(1)}, bf16[2,320,128]{2,1,0:T(8,128)(2,1)S(1)}, u32[]{:S(2)}, u32[]{:S(2)}) collective-permute-start(bf16[2,320,128]{2,1,0:T(8,128)(2,1)S(1)} %get-tuple-element.16), channel_id=1, source_target_pairs={{0,2},{1,10},{2,0},{3,8},{4,6},{5,14},{6,4},{7,12},{8,3},{9,11},{1... | collective-permute-start | bytes 491528 | tf_op jit(solution)/shard_map/ppermute | solution.py:96
  9.8 2.0 %collective-permute-start.3 = (bf16[2,320,128]{2,1,0:T(8,128)(2,1)S(1)}, bf16[2,320,128]{2,1,0:T(8,128)(2,1)S(1)}, u32[]{:S(2)}, u32[]{:S(2)}) collective-permute-start(bf16[2,320,128]{2,1,0:T(8,128)(2,1)S(1)} %get-tuple-element.17), channel_id=1, source_target_pairs={{0,0},{1,8},{2,2},{3,10},{4,4},{5,12},{6,6},{7,14},{8,1},{9,9},{10... | collective-permute-start | bytes 491528 | tf_op jit(solution)/shard_map/ppermute | solution.py:96
  11.8 4.3 %collective-permute-done.refs_0_ = bf16[2,320,128]{2,1,0:T(8,128)(2,1)S(1)} collective-permute-done((bf16[2,320,128]{2,1,0:T(8,128)(2,1)S(1)}, bf16[2,320,128]{2,1,0:T(8,128)(2,1)S(1)}, u32[]{:S(2)}, u32[]{:S(2)}) %collective-permute-start) | collective-permute-done | bytes 163872 | tf_op jit(solution)/shard_map/ppermute | solution.py:96
  16.1 5.5 %collective-permute-done.1.refs_1_ = bf16[2,320,128]{2,1,0:T(8,128)(2,1)S(1)} collective-permute-done((bf16[2,320,128]{2,1,0:T(8,128)(2,1)S(1)}, bf16[2,320,128]{2,1,0:T(8,128)(2,1)S(1)}, u32[]{:S(2)}, u32[]{:S(2)}) %collective-permute-start.1) | collective-permute-done | bytes 163872 | tf_op jit(solution)/shard_map/ppermute | solution.py:96
  21.7 0.4 collective-permute-done.4.refs_7_
  22.0 1.5 %collective-permute-start.7 = (bf16[336,1280]{1,0:T(8,128)(2,1)S(1)}, bf16[336,1280]{1,0:T(8,128)(2,1)S(1)}, u32[]{:S(2)}, u32[]{:S(2)}) collective-permute-start(bf16[336,1280]{1,0:T(8,128)(2,1)S(1)} %collective-permute-done.4.refs_7_), channel_id=1, source_target_pairs={{0,8},{1,9},{2,10},{3,11},{4,12},{5,13},{6,14},{7,15},{8,0},{9,1},... | collective-permute-start | bytes 2580488 | tf_op jit(solution)/shard_map/ppermute | solution.py:96
  23.6 2.5 %collective-permute-done.5.refs_4_ = bf16[4,320,128]{2,1,0:T(8,128)(2,1)S(1)} collective-permute-done((bf16[4,320,128]{2,1,0:T(8,128)(2,1)S(1)}, bf16[4,320,128]{2,1,0:T(8,128)(2,1)S(1)}, u32[]{:S(2)}, u32[]{:S(2)}) %collective-permute-start.5) | collective-permute-done | bytes 327712 | tf_op jit(solution)/shard_map/ppermute | solution.py:96
  26.1 6.6 %sections.1 = (bf16[4,320,128]{2,1,0:T(8,128)(2,1)S(1)}, bf16[4,320,128]{2,1,0:T(8,128)(2,1)S(1)}) custom-call(bf16[2,320,128]{2,1,0:T(8,128)(2,1)S(1)} %collective-permute-done.refs_0_, bf16[2,320,128]{2,1,0:T(8,128)(2,1)S(1)} %collective-permute-done.1.refs_1_, bf16[2,320,128]{2,1,0:T(8,128)(2,1)S(1)} %collective-permute-done.2.refs_2_, ...), custom_call_target="tpu_custom_call" | custom-call | flops 3774873600 | bytes 4194304 | tf_op jit(solution)/shard_map/sections/pallas_call | solution.py:327
  32.7 0.3 collective-permute-start.8
  33.0 1.3 %collective-permute-start.14 = (bf16[1,320,128]{2,1,0:T(8,128)(2,1)S(1)}, bf16[1,320,128]{2,1,0:T(8,128)(2,1)S(1)}, u32[]{:S(2)}, u32[]{:S(2)}) collective-permute-start(bf16[1,320,128]{2,1,0:T(8,128)(2,1)S(1)} %get-tuple-element.23), channel_id=1, source_target_pairs={{0,4},{1,12},{2,6},{3,14},{4,0},{5,8},{6,2},{7,10},{8,5},{9,13},{1... | collective-permute-start | bytes 245768 | tf_op jit(solution)/shard_map/ppermute | solution.py:96
  34.2 0.2 collective-permute-done.8
  34.5 3.2 %collective-permute-start.9 = (bf16[2,320,128]{2,1,0:T(8,128)(2,1)S(1)}, bf16[2,320,128]{2,1,0:T(8,128)(2,1)S(1)}, u32[]{:S(2)}, u32[]{:S(2)}) collective-permute-start(bf16[2,320,128]{2,1,0:T(8,128)(2,1)S(1)} %pad_maximum_fusion), channel_id=1, source_target_pairs={{0,0},{1,8},{2,2},{3,10},{4,4},{5,12},{6,6},{7,14},{8,1},{9,9},{10... | collective-permute-start | bytes 491528 | tf_op jit(solution)/shard_map/ppermute | solution.py:96
  37.7 1.5 %collective-permute-start.10 = (bf16[2,320,128]{2,1,0:T(8,128)(2,1)S(1)}, bf16[2,320,128]{2,1,0:T(8,128)(2,1)S(1)}, u32[]{:S(2)}, u32[]{:S(2)}) collective-permute-start(bf16[2,320,128]{2,1,0:T(8,128)(2,1)S(1)} %pad_maximum_fusion.1), channel_id=1, source_target_pairs={{0,2},{1,10},{2,0},{3,8},{4,6},{5,14},{6,4},{7,12},{8,3},{9,11},{1... | collective-permute-start | bytes 491528 | tf_op jit(solution)/shard_map/ppermute | solution.py:96
  39.2 1.2 %collective-permute-start.13 = (bf16[1,320,128]{2,1,0:T(8,128)(2,1)S(1)}, bf16[1,320,128]{2,1,0:T(8,128)(2,1)S(1)}, u32[]{:S(2)}, u32[]{:S(2)}) collective-permute-start(bf16[1,320,128]{2,1,0:T(8,128)(2,1)S(1)} %get-tuple-element.24), channel_id=1, source_target_pairs={{0,6},{1,14},{2,4},{3,12},{4,2},{5,10},{6,0},{7,8},{8,7},{9,15},{1... | collective-permute-start | bytes 245768 | tf_op jit(solution)/shard_map/ppermute | solution.py:96
  40.4 2.2 %collective-permute-start.12 = (bf16[1,320,128]{2,1,0:T(8,128)(2,1)S(1)}, bf16[1,320,128]{2,1,0:T(8,128)(2,1)S(1)}, u32[]{:S(2)}, u32[]{:S(2)}) collective-permute-start(bf16[1,320,128]{2,1,0:T(8,128)(2,1)S(1)} %get-tuple-element.27), channel_id=1, source_target_pairs={{0,4},{1,12},{2,6},{3,14},{4,0},{5,8},{6,2},{7,10},{8,5},{9,13},{1... | collective-permute-start | bytes 245768 | tf_op jit(solution)/shard_map/ppermute | solution.py:96
  42.7 2.3 %collective-permute-start.11 = (bf16[1,320,128]{2,1,0:T(8,128)(2,1)S(1)}, bf16[1,320,128]{2,1,0:T(8,128)(2,1)S(1)}, u32[]{:S(2)}, u32[]{:S(2)}) collective-permute-start(bf16[1,320,128]{2,1,0:T(8,128)(2,1)S(1)} %get-tuple-element.28), channel_id=1, source_target_pairs={{0,6},{1,14},{2,4},{3,12},{4,2},{5,10},{6,0},{7,8},{8,7},{9,15},{1... | collective-permute-start | bytes 245768 | tf_op jit(solution)/shard_map/ppermute | solution.py:96
  45.0 3.5 %collective-permute-done.13.refs_4_ = bf16[1,320,128]{2,1,0:T(8,128)(2,1)S(1)} collective-permute-done((bf16[1,320,128]{2,1,0:T(8,128)(2,1)S(1)}, bf16[1,320,128]{2,1,0:T(8,128)(2,1)S(1)}, u32[]{:S(2)}, u32[]{:S(2)}) %collective-permute-start.13) | collective-permute-done | bytes 81952 | tf_op jit(solution)/shard_map/ppermute | solution.py:96
  48.5 0.7 %collective-permute-done.12.refs_3_ = bf16[1,320,128]{2,1,0:T(8,128)(2,1)S(1)} collective-permute-done((bf16[1,320,128]{2,1,0:T(8,128)(2,1)S(1)}, bf16[1,320,128]{2,1,0:T(8,128)(2,1)S(1)}, u32[]{:S(2)}, u32[]{:S(2)}) %collective-permute-start.12) | collective-permute-done | bytes 81952 | tf_op jit(solution)/shard_map/ppermute | solution.py:96
  49.1 2.2 %collective-permute-done.11.refs_2_ = bf16[1,320,128]{2,1,0:T(8,128)(2,1)S(1)} collective-permute-done((bf16[1,320,128]{2,1,0:T(8,128)(2,1)S(1)}, bf16[1,320,128]{2,1,0:T(8,128)(2,1)S(1)}, u32[]{:S(2)}, u32[]{:S(2)}) %collective-permute-start.11) | collective-permute-done | bytes 81952 | tf_op jit(solution)/shard_map/ppermute | solution.py:96
  51.4 0.9 %join.1 = bf16[320,1024]{1,0:T(8,128)(2,1)} custom-call(bf16[2,320,128]{2,1,0:T(8,128)(2,1)S(1)} %collective-permute-done.9.refs_0_, bf16[2,320,128]{2,1,0:T(8,128)(2,1)S(1)} %collective-permute-done.10.refs_1_, bf16[1,320,128]{2,1,0:T(8,128)(2,1)S(1)} %collective-permute-done.11.refs_2_, bf16[1,320,128]{2,1,0:T(8,128)(2,1)S(1)} %collective-permute-done.12.refs_3_, ...), custom_call_target="tpu_custom_call" | custom-call | tf_op jit(solution)/shard_map/join/pallas_call | solution.py:196
  (16 shorter events, 0.1 us)
Async XLA Ops:
  2.0 20.1 %collective-permute-start.4 = (bf16[336,1280]{1,0:T(8,128)(2,1)S(1)}, bf16[336,1280]{1,0:T(8,128)(2,1)S(1)}, u32[]{:S(2)}, u32[]{:S(2)}) collective-permute-start(bf16[336,1280]{1,0:T(8,128)(2,1)S(1)} %get-tuple-element.18.refs_5_), channel_id=1, source_target_pairs={{0,16},{1,17},{2,18},{3,19},{4,20},{5,21},{6,22},{7,23},{8,24},{9,... | collective-permute-start | bytes 2580488 | tf_op jit(solution)/shard_map/ppermute | solution.py:96
  3.3 12.8 %collective-permute-start = (bf16[2,320,128]{2,1,0:T(8,128)(2,1)S(1)}, bf16[2,320,128]{2,1,0:T(8,128)(2,1)S(1)}, u32[]{:S(2)}, u32[]{:S(2)}) collective-permute-start(bf16[2,320,128]{2,1,0:T(8,128)(2,1)S(1)} %get-tuple-element.14), channel_id=1, source_target_pairs={{0,4},{1,12},{2,6},{3,14},{4,0},{5,8},{6,2},{7,10},{8,5},{9,13},{1... | collective-permute-start | bytes 491528 | tf_op jit(solution)/shard_map/ppermute | solution.py:96
  5.1 16.5 %collective-permute-start.1 = (bf16[2,320,128]{2,1,0:T(8,128)(2,1)S(1)}, bf16[2,320,128]{2,1,0:T(8,128)(2,1)S(1)}, u32[]{:S(2)}, u32[]{:S(2)}) collective-permute-start(bf16[2,320,128]{2,1,0:T(8,128)(2,1)S(1)} %get-tuple-element.15), channel_id=1, source_target_pairs={{0,6},{1,14},{2,4},{3,12},{4,2},{5,10},{6,0},{7,8},{8,7},{9,15},{1... | collective-permute-start | bytes 491528 | tf_op jit(solution)/shard_map/ppermute | solution.py:96
  7.0 14.7 %collective-permute-start.2 = (bf16[2,320,128]{2,1,0:T(8,128)(2,1)S(1)}, bf16[2,320,128]{2,1,0:T(8,128)(2,1)S(1)}, u32[]{:S(2)}, u32[]{:S(2)}) collective-permute-start(bf16[2,320,128]{2,1,0:T(8,128)(2,1)S(1)} %get-tuple-element.16), channel_id=1, source_target_pairs={{0,2},{1,10},{2,0},{3,8},{4,6},{5,14},{6,4},{7,12},{8,3},{9,11},{1... | collective-permute-start | bytes 491528 | tf_op jit(solution)/shard_map/ppermute | solution.py:96
  9.8 16.3 %copy-start = (f32[4,320]{1,0:T(4,128)S(1)}, f32[4,320]{1,0:T(4,128)}, u32[]{:S(2)}) copy-start(f32[4,320]{1,0:T(4,128)} %refs_10_.1) | copy-start | bytes 15364
  9.8 11.8 %collective-permute-start.3 = (bf16[2,320,128]{2,1,0:T(8,128)(2,1)S(1)}, bf16[2,320,128]{2,1,0:T(8,128)(2,1)S(1)}, u32[]{:S(2)}, u32[]{:S(2)}) collective-permute-start(bf16[2,320,128]{2,1,0:T(8,128)(2,1)S(1)} %get-tuple-element.17), channel_id=1, source_target_pairs={{0,0},{1,8},{2,2},{3,10},{4,4},{5,12},{6,6},{7,14},{8,1},{9,9},{10... | collective-permute-start | bytes 491528 | tf_op jit(solution)/shard_map/ppermute | solution.py:96
  16.1 7.5 %collective-permute-start.6 = (bf16[336,1280]{1,0:T(8,128)(2,1)S(1)}, bf16[336,1280]{1,0:T(8,128)(2,1)}, u32[]{:S(2)}, u32[]{:S(2)}) collective-permute-start(bf16[336,1280]{1,0:T(8,128)(2,1)S(1)} %get-tuple-element.18.refs_5_), channel_id=1, source_target_pairs={{0,8},{1,9},{2,10},{3,11},{4,12},{5,13},{6,14},{7,15},{8,0},{9,1},... | collective-permute-start | bytes 2580488 | tf_op jit(solution)/shard_map/ppermute | solution.py:96
  22.0 4.0 %collective-permute-start.7 = (bf16[336,1280]{1,0:T(8,128)(2,1)S(1)}, bf16[336,1280]{1,0:T(8,128)(2,1)S(1)}, u32[]{:S(2)}, u32[]{:S(2)}) collective-permute-start(bf16[336,1280]{1,0:T(8,128)(2,1)S(1)} %collective-permute-done.4.refs_7_), channel_id=1, source_target_pairs={{0,8},{1,9},{2,10},{3,11},{4,12},{5,13},{6,14},{7,15},{8,0},{9,1},... | collective-permute-start | bytes 2580488 | tf_op jit(solution)/shard_map/ppermute | solution.py:96
  23.6 2.5 %collective-permute-start.5 = (bf16[4,320,128]{2,1,0:T(8,128)(2,1)S(1)}, bf16[4,320,128]{2,1,0:T(8,128)(2,1)S(1)}, u32[]{:S(2)}, u32[]{:S(2)}) collective-permute-start(bf16[4,320,128]{2,1,0:T(8,128)(2,1)S(1)} %pick.1), channel_id=1, source_target_pairs={{0,8},{1,9},{2,10},{3,11},{4,12},{5,13},{6,14},{7,15},{8,0},{9,1},... | collective-permute-start | bytes 983048 | tf_op jit(solution)/shard_map/ppermute | solution.py:96
  32.7 1.7 %collective-permute-start.8 = (bf16[4,320,128]{2,1,0:T(8,128)(2,1)S(1)}, bf16[4,320,128]{2,1,0:T(8,128)(2,1)S(1)}, u32[]{:S(2)}, u32[]{:S(2)}) collective-permute-start(bf16[4,320,128]{2,1,0:T(8,128)(2,1)S(1)} %get-tuple-element.22), channel_id=1, source_target_pairs={{0,8},{1,9},{2,10},{3,11},{4,12},{5,13},{6,14},{7,15},{8,0},{9,1},... | collective-permute-start | bytes 983048 | tf_op jit(solution)/shard_map/ppermute | solution.py:96
  33.0 9.7 %collective-permute-start.14 = (bf16[1,320,128]{2,1,0:T(8,128)(2,1)S(1)}, bf16[1,320,128]{2,1,0:T(8,128)(2,1)S(1)}, u32[]{:S(2)}, u32[]{:S(2)}) collective-permute-start(bf16[1,320,128]{2,1,0:T(8,128)(2,1)S(1)} %get-tuple-element.23), channel_id=1, source_target_pairs={{0,4},{1,12},{2,6},{3,14},{4,0},{5,8},{6,2},{7,10},{8,5},{9,13},{1... | collective-permute-start | bytes 245768 | tf_op jit(solution)/shard_map/ppermute | solution.py:96
  34.5 16.9 %collective-permute-start.9 = (bf16[2,320,128]{2,1,0:T(8,128)(2,1)S(1)}, bf16[2,320,128]{2,1,0:T(8,128)(2,1)S(1)}, u32[]{:S(2)}, u32[]{:S(2)}) collective-permute-start(bf16[2,320,128]{2,1,0:T(8,128)(2,1)S(1)} %pad_maximum_fusion), channel_id=1, source_target_pairs={{0,0},{1,8},{2,2},{3,10},{4,4},{5,12},{6,6},{7,14},{8,1},{9,9},{10... | collective-permute-start | bytes 491528 | tf_op jit(solution)/shard_map/ppermute | solution.py:96
  37.7 13.7 %collective-permute-start.10 = (bf16[2,320,128]{2,1,0:T(8,128)(2,1)S(1)}, bf16[2,320,128]{2,1,0:T(8,128)(2,1)S(1)}, u32[]{:S(2)}, u32[]{:S(2)}) collective-permute-start(bf16[2,320,128]{2,1,0:T(8,128)(2,1)S(1)} %pad_maximum_fusion.1), channel_id=1, source_target_pairs={{0,2},{1,10},{2,0},{3,8},{4,6},{5,14},{6,4},{7,12},{8,3},{9,11},{1... | collective-permute-start | bytes 491528 | tf_op jit(solution)/shard_map/ppermute | solution.py:96
  39.2 9.3 %collective-permute-start.13 = (bf16[1,320,128]{2,1,0:T(8,128)(2,1)S(1)}, bf16[1,320,128]{2,1,0:T(8,128)(2,1)S(1)}, u32[]{:S(2)}, u32[]{:S(2)}) collective-permute-start(bf16[1,320,128]{2,1,0:T(8,128)(2,1)S(1)} %get-tuple-element.24), channel_id=1, source_target_pairs={{0,6},{1,14},{2,4},{3,12},{4,2},{5,10},{6,0},{7,8},{8,7},{9,15},{1... | collective-permute-start | bytes 245768 | tf_op jit(solution)/shard_map/ppermute | solution.py:96
  40.4 8.7 %collective-permute-start.12 = (bf16[1,320,128]{2,1,0:T(8,128)(2,1)S(1)}, bf16[1,320,128]{2,1,0:T(8,128)(2,1)S(1)}, u32[]{:S(2)}, u32[]{:S(2)}) collective-permute-start(bf16[1,320,128]{2,1,0:T(8,128)(2,1)S(1)} %get-tuple-element.27), channel_id=1, source_target_pairs={{0,4},{1,12},{2,6},{3,14},{4,0},{5,8},{6,2},{7,10},{8,5},{9,13},{1... | collective-permute-start | bytes 245768 | tf_op jit(solution)/shard_map/ppermute | solution.py:96
  42.7 8.7 %collective-permute-start.11 = (bf16[1,320,128]{2,1,0:T(8,128)(2,1)S(1)}, bf16[1,320,128]{2,1,0:T(8,128)(2,1)S(1)}, u32[]{:S(2)}, u32[]{:S(2)}) collective-permute-start(bf16[1,320,128]{2,1,0:T(8,128)(2,1)S(1)} %get-tuple-element.28), channel_id=1, source_target_pairs={{0,6},{1,14},{2,4},{3,12},{4,2},{5,10},{6,0},{7,8},{8,7},{9,15},{1... | collective-permute-start | bytes 245768 | tf_op jit(solution)/shard_map/ppermute | solution.py:96

commit v8 on v7

--- a/solution.py
+++ b/solution.py
@@ -218,7 +218,7 @@
     packs = take(4)
     skip_in, gain_ref = take(2)
     kept, given = take(2)
-    weights, skip, around, with_one, with_first, two, three, last = take(8)
+    weights, skip, around, with_one, with_first, two, three = take(7)
     sem_w, sem_s = take(2)
     y, core, z, x = place()
     clip = 2 * y + x
@@ -277,7 +277,7 @@
 
     gain_columns = [column_of(gains, [s, 4 + s, 8 + s]) for s in range(4)]
     for s in range(4):
-        source, target = ((zero, one), (one, two), (two, three), (three, last))[s]
+        source, target = ((zero, one), (one, two), (two, three), (three, None))[s]
         gain = gain_columns[s]
         values = source[...].astype(F32)
         scale = lax.rsqrt(jnp.mean(values * values, axis=0, keepdims=True) + EPS)
@@ -309,10 +309,18 @@
             right = beside[...]
         total = source[...].astype(F32)
         total = (total + jnp.dot(projection, right, preferred_element_type=F32)).astype(BF)
-        target[...] = total
-    for n, d in enumerate(dests):
-        for k, out in enumerate((kept, given)):
-            out[n] = last[:, lanes_of(d, k)]
+        if s < 3:
+            target[...] = total
+        else:
+            outcome = total
+    for c in range(2):
+
+        @pl.when(core == c)
+        def _():
+            for f in range(frames):
+                level = z ^ (f // 2)
+                at = sum(jnp.where(level == d, n, 0) for n, d in enumerate(dests))
+                (kept, given)[(f + c) % 2][at] = outcome[:, span(f)]
 
 
 def run_sections(dests, loaded, turned, swapped, weights, skip, gain):
@@ -339,7 +347,6 @@
             pltpu.VMEM((2 * width + 64, columns), BF),
             pltpu.VMEM((width, columns), BF),
             pltpu.VMEM((width, columns), BF),
-            pltpu.VMEM((width, columns), BF),
             pltpu.SemaphoreType.DMA((4,)),
             pltpu.SemaphoreType.DMA,
         ],

time: 53.3 us -> 53.2 us (level)
  no operation moved by 1% of the time
where the time goes in v8:
time: 53.2 us; the launch traced here: 52.2 us
  starting transfers between devices  23.4 us (44%)
  waiting for transfers between devices  19.2 us (36%)
  Pallas kernels  9.42 us (18%)
    ppermute x15, starting transfers between devices, move(): return lax.ppermute(array, ('segment', 'frame'), pairs)  23.4 us
    ppermute x15, waiting for transfers between devices, move(): return lax.ppermute(array, ('segment', 'frame'), pairs)  19.2 us
    pallas_call x1, Pallas kernels, run_sections(): pl.pallas_call(functools.partial(sections_kernel, dests, levels, width, l...  6.51 us
    pallas_call x1, Pallas kernels, pack_and_cut(): pl.pallas_call(functools.partial(pack_kernel, levels), out_shape=[pltpu.V...  1.98 us
  transfers between devices with their start and end apart: 15, of which 8 were waited for; matrix products, arithmetic and copies ran while one was open for 0% of the time, Pallas kernels for 0%

profile of v8, /device:TPU:17, one launch (start us, length us, event | category | flops | bytes accessed | tf_op | source)
XLA Modules:
  0.0 52.2 jit_solution(9140128399604501149)
XLA Ops:
  0.0 2.0 %pack.1 = (bf16[2,320,128]{2,1,0:T(8,128)(2,1)S(1)}, bf16[2,320,128]{2,1,0:T(8,128)(2,1)S(1)}, bf16[2,320,128]{2,1,0:T(8,128)(2,1)S(1)}, bf16[2,320,128]{2,1,0:T(8,128)(2,1)S(1)}, bf16[336,1280]{1,0:T(8,128)(2,1)S(1)}) custom-call(s32[4]{0:T(128)} %times_ref.1, bf16[320,1024]{1,0:T(8,128)(2,1)} %bitcast.6, bf16[3,320,320]{2,1,0:T(8,128)(2,1)} %bitcast.5, ...), custom_call_target="tpu_custom_call" | custom-call | tf_op jit(solution)/shard_map/pack/pallas_call | solution.py:147
  2.0 1.3 %collective-permute-start.4 = (bf16[336,1280]{1,0:T(8,128)(2,1)S(1)}, bf16[336,1280]{1,0:T(8,128)(2,1)S(1)}, u32[]{:S(2)}, u32[]{:S(2)}) collective-permute-start(bf16[336,1280]{1,0:T(8,128)(2,1)S(1)} %get-tuple-element.18.refs_5_), channel_id=1, source_target_pairs={{0,16},{1,17},{2,18},{3,19},{4,20},{5,21},{6,22},{7,23},{8,24},{9,... | collective-permute-start | bytes 2580488 | tf_op jit(solution)/shard_map/ppermute | solution.py:96
  3.3 1.8 %collective-permute-start = (bf16[2,320,128]{2,1,0:T(8,128)(2,1)S(1)}, bf16[2,320,128]{2,1,0:T(8,128)(2,1)S(1)}, u32[]{:S(2)}, u32[]{:S(2)}) collective-permute-start(bf16[2,320,128]{2,1,0:T(8,128)(2,1)S(1)} %get-tuple-element.14), channel_id=1, source_target_pairs={{0,4},{1,12},{2,6},{3,14},{4,0},{5,8},{6,2},{7,10},{8,5},{9,13},{1... | collective-permute-start | bytes 491528 | tf_op jit(solution)/shard_map/ppermute | solution.py:96
  5.1 1.8 %collective-permute-start.1 = (bf16[2,320,128]{2,1,0:T(8,128)(2,1)S(1)}, bf16[2,320,128]{2,1,0:T(8,128)(2,1)S(1)}, u32[]{:S(2)}, u32[]{:S(2)}) collective-permute-start(bf16[2,320,128]{2,1,0:T(8,128)(2,1)S(1)} %get-tuple-element.15), channel_id=1, source_target_pairs={{0,6},{1,14},{2,4},{3,12},{4,2},{5,10},{6,0},{7,8},{8,7},{9,15},{1... | collective-permute-start | bytes 491528 | tf_op jit(solution)/shard_map/ppermute | solution.py:96
  7.0 2.8 %collective-permute-start.2 = (bf16[2,320,128]{2,1,0:T(8,128)(2,1)S(1)}, bf16[2,320,128]{2,1,0:T(8,128)(2,1)S(1)}, u32[]{:S(2)}, u32[]{:S(2)}) collective-permute-start(bf16[2,320,128]{2,1,0:T(8,128)(2,1)S(1)} %get-tuple-element.16), channel_id=1, source_target_pairs={{0,2},{1,10},{2,0},{3,8},{4,6},{5,14},{6,4},{7,12},{8,3},{9,11},{1... | collective-permute-start | bytes 491528 | tf_op jit(solution)/shard_map/ppermute | solution.py:96
  9.8 2.0 %collective-permute-start.3 = (bf16[2,320,128]{2,1,0:T(8,128)(2,1)S(1)}, bf16[2,320,128]{2,1,0:T(8,128)(2,1)S(1)}, u32[]{:S(2)}, u32[]{:S(2)}) collective-permute-start(bf16[2,320,128]{2,1,0:T(8,128)(2,1)S(1)} %get-tuple-element.17), channel_id=1, source_target_pairs={{0,0},{1,8},{2,2},{3,10},{4,4},{5,12},{6,6},{7,14},{8,1},{9,9},{10... | collective-permute-start | bytes 491528 | tf_op jit(solution)/shard_map/ppermute | solution.py:96
  11.8 4.3 %collective-permute-done.refs_0_ = bf16[2,320,128]{2,1,0:T(8,128)(2,1)S(1)} collective-permute-done((bf16[2,320,128]{2,1,0:T(8,128)(2,1)S(1)}, bf16[2,320,128]{2,1,0:T(8,128)(2,1)S(1)}, u32[]{:S(2)}, u32[]{:S(2)}) %collective-permute-start) | collective-permute-done | bytes 163872 | tf_op jit(solution)/shard_map/ppermute | solution.py:96
  16.1 5.5 %collective-permute-done.1.refs_1_ = bf16[2,320,128]{2,1,0:T(8,128)(2,1)S(1)} collective-permute-done((bf16[2,320,128]{2,1,0:T(8,128)(2,1)S(1)}, bf16[2,320,128]{2,1,0:T(8,128)(2,1)S(1)}, u32[]{:S(2)}, u32[]{:S(2)}) %collective-permute-start.1) | collective-permute-done | bytes 163872 | tf_op jit(solution)/shard_map/ppermute | solution.py:96
  21.7 0.4 collective-permute-done.4.refs_7_
  22.0 1.5 %collective-permute-start.7 = (bf16[336,1280]{1,0:T(8,128)(2,1)S(1)}, bf16[336,1280]{1,0:T(8,128)(2,1)S(1)}, u32[]{:S(2)}, u32[]{:S(2)}) collective-permute-start(bf16[336,1280]{1,0:T(8,128)(2,1)S(1)} %collective-permute-done.4.refs_7_), channel_id=1, source_target_pairs={{0,8},{1,9},{2,10},{3,11},{4,12},{5,13},{6,14},{7,15},{8,0},{9,1},... | collective-permute-start | bytes 2580488 | tf_op jit(solution)/shard_map/ppermute | solution.py:96
  23.6 2.5 %collective-permute-done.5.refs_4_ = bf16[4,320,128]{2,1,0:T(8,128)(2,1)S(1)} collective-permute-done((bf16[4,320,128]{2,1,0:T(8,128)(2,1)S(1)}, bf16[4,320,128]{2,1,0:T(8,128)(2,1)S(1)}, u32[]{:S(2)}, u32[]{:S(2)}) %collective-permute-start.5) | collective-permute-done | bytes 327712 | tf_op jit(solution)/shard_map/ppermute | solution.py:96
  26.1 6.5 %sections.1 = (bf16[4,320,128]{2,1,0:T(8,128)(2,1)S(1)}, bf16[4,320,128]{2,1,0:T(8,128)(2,1)S(1)}) custom-call(bf16[2,320,128]{2,1,0:T(8,128)(2,1)S(1)} %collective-permute-done.refs_0_, bf16[2,320,128]{2,1,0:T(8,128)(2,1)S(1)} %collective-permute-done.1.refs_1_, bf16[2,320,128]{2,1,0:T(8,128)(2,1)S(1)} %collective-permute-done.2.refs_2_, ...), custom_call_target="tpu_custom_call" | custom-call | flops 3774873600 | bytes 4194304 | tf_op jit(solution)/shard_map/sections/pallas_call | solution.py:335
  32.6 0.2 collective-permute-start.8
  32.9 1.3 %collective-permute-start.14 = (bf16[1,320,128]{2,1,0:T(8,128)(2,1)S(1)}, bf16[1,320,128]{2,1,0:T(8,128)(2,1)S(1)}, u32[]{:S(2)}, u32[]{:S(2)}) collective-permute-start(bf16[1,320,128]{2,1,0:T(8,128)(2,1)S(1)} %get-tuple-element.23), channel_id=1, source_target_pairs={{0,4},{1,12},{2,6},{3,14},{4,0},{5,8},{6,2},{7,10},{8,5},{9,13},{1... | collective-permute-start | bytes 245768 | tf_op jit(solution)/shard_map/ppermute | solution.py:96
  34.1 0.2 collective-permute-done.8
  34.4 3.2 %collective-permute-start.9 = (bf16[2,320,128]{2,1,0:T(8,128)(2,1)S(1)}, bf16[2,320,128]{2,1,0:T(8,128)(2,1)S(1)}, u32[]{:S(2)}, u32[]{:S(2)}) collective-permute-start(bf16[2,320,128]{2,1,0:T(8,128)(2,1)S(1)} %pad_maximum_fusion), channel_id=1, source_target_pairs={{0,0},{1,8},{2,2},{3,10},{4,4},{5,12},{6,6},{7,14},{8,1},{9,9},{10... | collective-permute-start | bytes 491528 | tf_op jit(solution)/shard_map/ppermute | solution.py:96
  37.6 1.6 %collective-permute-start.10 = (bf16[2,320,128]{2,1,0:T(8,128)(2,1)S(1)}, bf16[2,320,128]{2,1,0:T(8,128)(2,1)S(1)}, u32[]{:S(2)}, u32[]{:S(2)}) collective-permute-start(bf16[2,320,128]{2,1,0:T(8,128)(2,1)S(1)} %pad_maximum_fusion.1), channel_id=1, source_target_pairs={{0,2},{1,10},{2,0},{3,8},{4,6},{5,14},{6,4},{7,12},{8,3},{9,11},{1... | collective-permute-start | bytes 491528 | tf_op jit(solution)/shard_map/ppermute | solution.py:96
  39.1 1.2 %collective-permute-start.13 = (bf16[1,320,128]{2,1,0:T(8,128)(2,1)S(1)}, bf16[1,320,128]{2,1,0:T(8,128)(2,1)S(1)}, u32[]{:S(2)}, u32[]{:S(2)}) collective-permute-start(bf16[1,320,128]{2,1,0:T(8,128)(2,1)S(1)} %get-tuple-element.24), channel_id=1, source_target_pairs={{0,6},{1,14},{2,4},{3,12},{4,2},{5,10},{6,0},{7,8},{8,7},{9,15},{1... | collective-permute-start | bytes 245768 | tf_op jit(solution)/shard_map/ppermute | solution.py:96
  40.3 2.3 %collective-permute-start.12 = (bf16[1,320,128]{2,1,0:T(8,128)(2,1)S(1)}, bf16[1,320,128]{2,1,0:T(8,128)(2,1)S(1)}, u32[]{:S(2)}, u32[]{:S(2)}) collective-permute-start(bf16[1,320,128]{2,1,0:T(8,128)(2,1)S(1)} %get-tuple-element.27), channel_id=1, source_target_pairs={{0,4},{1,12},{2,6},{3,14},{4,0},{5,8},{6,2},{7,10},{8,5},{9,13},{1... | collective-permute-start | bytes 245768 | tf_op jit(solution)/shard_map/ppermute | solution.py:96
  42.6 2.3 %collective-permute-start.11 = (bf16[1,320,128]{2,1,0:T(8,128)(2,1)S(1)}, bf16[1,320,128]{2,1,0:T(8,128)(2,1)S(1)}, u32[]{:S(2)}, u32[]{:S(2)}) collective-permute-start(bf16[1,320,128]{2,1,0:T(8,128)(2,1)S(1)} %get-tuple-element.28), channel_id=1, source_target_pairs={{0,6},{1,14},{2,4},{3,12},{4,2},{5,10},{6,0},{7,8},{8,7},{9,15},{1... | collective-permute-start | bytes 245768 | tf_op jit(solution)/shard_map/ppermute | solution.py:96
  44.9 3.5 %collective-permute-done.13.refs_4_ = bf16[1,320,128]{2,1,0:T(8,128)(2,1)S(1)} collective-permute-done((bf16[1,320,128]{2,1,0:T(8,128)(2,1)S(1)}, bf16[1,320,128]{2,1,0:T(8,128)(2,1)S(1)}, u32[]{:S(2)}, u32[]{:S(2)}) %collective-permute-start.13) | collective-permute-done | bytes 81952 | tf_op jit(solution)/shard_map/ppermute | solution.py:96
  48.4 0.7 %collective-permute-done.12.refs_3_ = bf16[1,320,128]{2,1,0:T(8,128)(2,1)S(1)} collective-permute-done((bf16[1,320,128]{2,1,0:T(8,128)(2,1)S(1)}, bf16[1,320,128]{2,1,0:T(8,128)(2,1)S(1)}, u32[]{:S(2)}, u32[]{:S(2)}) %collective-permute-start.12) | collective-permute-done | bytes 81952 | tf_op jit(solution)/shard_map/ppermute | solution.py:96
  49.0 2.2 %collective-permute-done.11.refs_2_ = bf16[1,320,128]{2,1,0:T(8,128)(2,1)S(1)} collective-permute-done((bf16[1,320,128]{2,1,0:T(8,128)(2,1)S(1)}, bf16[1,320,128]{2,1,0:T(8,128)(2,1)S(1)}, u32[]{:S(2)}, u32[]{:S(2)}) %collective-permute-start.11) | collective-permute-done | bytes 81952 | tf_op jit(solution)/shard_map/ppermute | solution.py:96
  51.3 0.9 %join.1 = bf16[320,1024]{1,0:T(8,128)(2,1)} custom-call(bf16[2,320,128]{2,1,0:T(8,128)(2,1)S(1)} %collective-permute-done.9.refs_0_, bf16[2,320,128]{2,1,0:T(8,128)(2,1)S(1)} %collective-permute-done.10.refs_1_, bf16[1,320,128]{2,1,0:T(8,128)(2,1)S(1)} %collective-permute-done.11.refs_2_, bf16[1,320,128]{2,1,0:T(8,128)(2,1)S(1)} %collective-permute-done.12.refs_3_, ...), custom_call_target="tpu_custom_call" | custom-call | tf_op jit(solution)/shard_map/join/pallas_call | solution.py:196
  (16 shorter events, 0.1 us)
Async XLA Ops:
  2.0 20.1 %collective-permute-start.4 = (bf16[336,1280]{1,0:T(8,128)(2,1)S(1)}, bf16[336,1280]{1,0:T(8,128)(2,1)S(1)}, u32[]{:S(2)}, u32[]{:S(2)}) collective-permute-start(bf16[336,1280]{1,0:T(8,128)(2,1)S(1)} %get-tuple-element.18.refs_5_), channel_id=1, source_target_pairs={{0,16},{1,17},{2,18},{3,19},{4,20},{5,21},{6,22},{7,23},{8,24},{9,... | collective-permute-start | bytes 2580488 | tf_op jit(solution)/shard_map/ppermute | solution.py:96
  3.3 12.8 %collective-permute-start = (bf16[2,320,128]{2,1,0:T(8,128)(2,1)S(1)}, bf16[2,320,128]{2,1,0:T(8,128)(2,1)S(1)}, u32[]{:S(2)}, u32[]{:S(2)}) collective-permute-start(bf16[2,320,128]{2,1,0:T(8,128)(2,1)S(1)} %get-tuple-element.14), channel_id=1, source_target_pairs={{0,4},{1,12},{2,6},{3,14},{4,0},{5,8},{6,2},{7,10},{8,5},{9,13},{1... | collective-permute-start | bytes 491528 | tf_op jit(solution)/shard_map/ppermute | solution.py:96
  5.1 16.5 %collective-permute-start.1 = (bf16[2,320,128]{2,1,0:T(8,128)(2,1)S(1)}, bf16[2,320,128]{2,1,0:T(8,128)(2,1)S(1)}, u32[]{:S(2)}, u32[]{:S(2)}) collective-permute-start(bf16[2,320,128]{2,1,0:T(8,128)(2,1)S(1)} %get-tuple-element.15), channel_id=1, source_target_pairs={{0,6},{1,14},{2,4},{3,12},{4,2},{5,10},{6,0},{7,8},{8,7},{9,15},{1... | collective-permute-start | bytes 491528 | tf_op jit(solution)/shard_map/ppermute | solution.py:96
  7.0 14.7 %collective-permute-start.2 = (bf16[2,320,128]{2,1,0:T(8,128)(2,1)S(1)}, bf16[2,320,128]{2,1,0:T(8,128)(2,1)S(1)}, u32[]{:S(2)}, u32[]{:S(2)}) collective-permute-start(bf16[2,320,128]{2,1,0:T(8,128)(2,1)S(1)} %get-tuple-element.16), channel_id=1, source_target_pairs={{0,2},{1,10},{2,0},{3,8},{4,6},{5,14},{6,4},{7,12},{8,3},{9,11},{1... | collective-permute-start | bytes 491528 | tf_op jit(solution)/shard_map/ppermute | solution.py:96
  9.8 16.3 %copy-start = (f32[4,320]{1,0:T(4,128)S(1)}, f32[4,320]{1,0:T(4,128)}, u32[]{:S(2)}) copy-start(f32[4,320]{1,0:T(4,128)} %refs_10_.1) | copy-start | bytes 15364
  9.8 11.8 %collective-permute-start.3 = (bf16[2,320,128]{2,1,0:T(8,128)(2,1)S(1)}, bf16[2,320,128]{2,1,0:T(8,128)(2,1)S(1)}, u32[]{:S(2)}, u32[]{:S(2)}) collective-permute-start(bf16[2,320,128]{2,1,0:T(8,128)(2,1)S(1)} %get-tuple-element.17), channel_id=1, source_target_pairs={{0,0},{1,8},{2,2},{3,10},{4,4},{5,12},{6,6},{7,14},{8,1},{9,9},{10... | collective-permute-start | bytes 491528 | tf_op jit(solution)/shard_map/ppermute | solution.py:96
  16.1 7.5 %collective-permute-start.6 = (bf16[336,1280]{1,0:T(8,128)(2,1)S(1)}, bf16[336,1280]{1,0:T(8,128)(2,1)}, u32[]{:S(2)}, u32[]{:S(2)}) collective-permute-start(bf16[336,1280]{1,0:T(8,128)(2,1)S(1)} %get-tuple-element.18.refs_5_), channel_id=1, source_target_pairs={{0,8},{1,9},{2,10},{3,11},{4,12},{5,13},{6,14},{7,15},{8,0},{9,1},... | collective-permute-start | bytes 2580488 | tf_op jit(solution)/shard_map/ppermute | solution.py:96
  22.0 4.0 %collective-permute-start.7 = (bf16[336,1280]{1,0:T(8,128)(2,1)S(1)}, bf16[336,1280]{1,0:T(8,128)(2,1)S(1)}, u32[]{:S(2)}, u32[]{:S(2)}) collective-permute-start(bf16[336,1280]{1,0:T(8,128)(2,1)S(1)} %collective-permute-done.4.refs_7_), channel_id=1, source_target_pairs={{0,8},{1,9},{2,10},{3,11},{4,12},{5,13},{6,14},{7,15},{8,0},{9,1},... | collective-permute-start | bytes 2580488 | tf_op jit(solution)/shard_map/ppermute | solution.py:96
  23.6 2.5 %collective-permute-start.5 = (bf16[4,320,128]{2,1,0:T(8,128)(2,1)S(1)}, bf16[4,320,128]{2,1,0:T(8,128)(2,1)S(1)}, u32[]{:S(2)}, u32[]{:S(2)}) collective-permute-start(bf16[4,320,128]{2,1,0:T(8,128)(2,1)S(1)} %pick.1), channel_id=1, source_target_pairs={{0,8},{1,9},{2,10},{3,11},{4,12},{5,13},{6,14},{7,15},{8,0},{9,1},... | collective-permute-start | bytes 983048 | tf_op jit(solution)/shard_map/ppermute | solution.py:96
  32.6 1.7 %collective-permute-start.8 = (bf16[4,320,128]{2,1,0:T(8,128)(2,1)S(1)}, bf16[4,320,128]{2,1,0:T(8,128)(2,1)S(1)}, u32[]{:S(2)}, u32[]{:S(2)}) collective-permute-start(bf16[4,320,128]{2,1,0:T(8,128)(2,1)S(1)} %get-tuple-element.22), channel_id=1, source_target_pairs={{0,8},{1,9},{2,10},{3,11},{4,12},{5,13},{6,14},{7,15},{8,0},{9,1},... | collective-permute-start | bytes 983048 | tf_op jit(solution)/shard_map/ppermute | solution.py:96
  32.9 9.7 %collective-permute-start.14 = (bf16[1,320,128]{2,1,0:T(8,128)(2,1)S(1)}, bf16[1,320,128]{2,1,0:T(8,128)(2,1)S(1)}, u32[]{:S(2)}, u32[]{:S(2)}) collective-permute-start(bf16[1,320,128]{2,1,0:T(8,128)(2,1)S(1)} %get-tuple-element.23), channel_id=1, source_target_pairs={{0,4},{1,12},{2,6},{3,14},{4,0},{5,8},{6,2},{7,10},{8,5},{9,13},{1... | collective-permute-start | bytes 245768 | tf_op jit(solution)/shard_map/ppermute | solution.py:96
  34.4 16.9 %collective-permute-start.9 = (bf16[2,320,128]{2,1,0:T(8,128)(2,1)S(1)}, bf16[2,320,128]{2,1,0:T(8,128)(2,1)S(1)}, u32[]{:S(2)}, u32[]{:S(2)}) collective-permute-start(bf16[2,320,128]{2,1,0:T(8,128)(2,1)S(1)} %pad_maximum_fusion), channel_id=1, source_target_pairs={{0,0},{1,8},{2,2},{3,10},{4,4},{5,12},{6,6},{7,14},{8,1},{9,9},{10... | collective-permute-start | bytes 491528 | tf_op jit(solution)/shard_map/ppermute | solution.py:96
  37.6 13.7 %collective-permute-start.10 = (bf16[2,320,128]{2,1,0:T(8,128)(2,1)S(1)}, bf16[2,320,128]{2,1,0:T(8,128)(2,1)S(1)}, u32[]{:S(2)}, u32[]{:S(2)}) collective-permute-start(bf16[2,320,128]{2,1,0:T(8,128)(2,1)S(1)} %pad_maximum_fusion.1), channel_id=1, source_target_pairs={{0,2},{1,10},{2,0},{3,8},{4,6},{5,14},{6,4},{7,12},{8,3},{9,11},{1... | collective-permute-start | bytes 491528 | tf_op jit(solution)/shard_map/ppermute | solution.py:96
  39.1 9.3 %collective-permute-start.13 = (bf16[1,320,128]{2,1,0:T(8,128)(2,1)S(1)}, bf16[1,320,128]{2,1,0:T(8,128)(2,1)S(1)}, u32[]{:S(2)}, u32[]{:S(2)}) collective-permute-start(bf16[1,320,128]{2,1,0:T(8,128)(2,1)S(1)} %get-tuple-element.24), channel_id=1, source_target_pairs={{0,6},{1,14},{2,4},{3,12},{4,2},{5,10},{6,0},{7,8},{8,7},{9,15},{1... | collective-permute-start | bytes 245768 | tf_op jit(solution)/shard_map/ppermute | solution.py:96
  40.3 8.7 %collective-permute-start.12 = (bf16[1,320,128]{2,1,0:T(8,128)(2,1)S(1)}, bf16[1,320,128]{2,1,0:T(8,128)(2,1)S(1)}, u32[]{:S(2)}, u32[]{:S(2)}) collective-permute-start(bf16[1,320,128]{2,1,0:T(8,128)(2,1)S(1)} %get-tuple-element.27), channel_id=1, source_target_pairs={{0,4},{1,12},{2,6},{3,14},{4,0},{5,8},{6,2},{7,10},{8,5},{9,13},{1... | collective-permute-start | bytes 245768 | tf_op jit(solution)/shard_map/ppermute | solution.py:96
  42.6 8.7 %collective-permute-start.11 = (bf16[1,320,128]{2,1,0:T(8,128)(2,1)S(1)}, bf16[1,320,128]{2,1,0:T(8,128)(2,1)S(1)}, u32[]{:S(2)}, u32[]{:S(2)}) collective-permute-start(bf16[1,320,128]{2,1,0:T(8,128)(2,1)S(1)} %get-tuple-element.28), channel_id=1, source_target_pairs={{0,6},{1,14},{2,4},{3,12},{4,2},{5,10},{6,0},{7,8},{8,7},{9,15},{1... | collective-permute-start | bytes 245768 | tf_op jit(solution)/shard_map/ppermute | solution.py:96

commit v9 on v8

--- a/solution.py
+++ b/solution.py
@@ -289,6 +289,7 @@
             for later in range(1, 4):
                 wait_weights(later)
             skip_load.wait()
+            turned_skip = [skip[n].T for n in range(2)]
         half = 0.5 + 0.5 * column_of(weights[s, width:, 0:width], [clip, 4 + clip])
         half = jnp.concatenate([half] * frames, axis=1)
         three_frames = jnp.concatenate(
@@ -305,7 +306,7 @@
         projection = weights[s, 0:width, 3 * width - 64 :]
         right = beside[0 : 64 + width, :]
         if s >= 2:
-            projection = jnp.concatenate([projection, skip[s - 2].T], axis=1)
+            projection = jnp.concatenate([projection, turned_skip[s - 2]], axis=1)
             right = beside[...]
         total = source[...].astype(F32)
         total = (total + jnp.dot(projection, right, preferred_element_type=F32)).astype(BF)

time: 53.2 us -> 53.2 us (level)
  no operation moved by 1% of the time
where the time goes in v9:
time: 53.2 us; the launch traced here: 52.2 us
  starting transfers between devices  23.4 us (44%)
  waiting for transfers between devices  19.2 us (36%)
  Pallas kernels  9.43 us (18%)
    ppermute x15, starting transfers between devices, move(): return lax.ppermute(array, ('segment', 'frame'), pairs)  23.4 us
    ppermute x15, waiting for transfers between devices, move(): return lax.ppermute(array, ('segment', 'frame'), pairs)  19.2 us
    pallas_call x1, Pallas kernels, run_sections(): pl.pallas_call(functools.partial(sections_kernel, dests, levels, width, l...  6.52 us
    pallas_call x1, Pallas kernels, pack_and_cut(): pl.pallas_call(functools.partial(pack_kernel, levels), out_shape=[pltpu.V...  1.98 us
  transfers between devices with their start and end apart: 15, of which 8 were waited for; matrix products, arithmetic and copies ran while one was open for 0% of the time, Pallas kernels for 0%

profile of v9, /device:TPU:17, one launch (start us, length us, event | category | flops | bytes accessed | tf_op | source)
XLA Modules:
  0.0 52.2 jit_solution(4382316268018479899)
XLA Ops:
  0.0 2.0 %pack.1 = (bf16[2,320,128]{2,1,0:T(8,128)(2,1)S(1)}, bf16[2,320,128]{2,1,0:T(8,128)(2,1)S(1)}, bf16[2,320,128]{2,1,0:T(8,128)(2,1)S(1)}, bf16[2,320,128]{2,1,0:T(8,128)(2,1)S(1)}, bf16[336,1280]{1,0:T(8,128)(2,1)S(1)}) custom-call(s32[4]{0:T(128)} %times_ref.1, bf16[320,1024]{1,0:T(8,128)(2,1)} %bitcast.6, bf16[3,320,320]{2,1,0:T(8,128)(2,1)} %bitcast.5, ...), custom_call_target="tpu_custom_call" | custom-call | tf_op jit(solution)/shard_map/pack/pallas_call | solution.py:147
  2.0 1.3 %collective-permute-start.4 = (bf16[336,1280]{1,0:T(8,128)(2,1)S(1)}, bf16[336,1280]{1,0:T(8,128)(2,1)S(1)}, u32[]{:S(2)}, u32[]{:S(2)}) collective-permute-start(bf16[336,1280]{1,0:T(8,128)(2,1)S(1)} %get-tuple-element.18.refs_5_), channel_id=1, source_target_pairs={{0,16},{1,17},{2,18},{3,19},{4,20},{5,21},{6,22},{7,23},{8,24},{9,... | collective-permute-start | bytes 2580488 | tf_op jit(solution)/shard_map/ppermute | solution.py:96
  3.3 1.8 %collective-permute-start = (bf16[2,320,128]{2,1,0:T(8,128)(2,1)S(1)}, bf16[2,320,128]{2,1,0:T(8,128)(2,1)S(1)}, u32[]{:S(2)}, u32[]{:S(2)}) collective-permute-start(bf16[2,320,128]{2,1,0:T(8,128)(2,1)S(1)} %get-tuple-element.14), channel_id=1, source_target_pairs={{0,4},{1,12},{2,6},{3,14},{4,0},{5,8},{6,2},{7,10},{8,5},{9,13},{1... | collective-permute-start | bytes 491528 | tf_op jit(solution)/shard_map/ppermute | solution.py:96
  5.1 1.8 %collective-permute-start.1 = (bf16[2,320,128]{2,1,0:T(8,128)(2,1)S(1)}, bf16[2,320,128]{2,1,0:T(8,128)(2,1)S(1)}, u32[]{:S(2)}, u32[]{:S(2)}) collective-permute-start(bf16[2,320,128]{2,1,0:T(8,128)(2,1)S(1)} %get-tuple-element.15), channel_id=1, source_target_pairs={{0,6},{1,14},{2,4},{3,12},{4,2},{5,10},{6,0},{7,8},{8,7},{9,15},{1... | collective-permute-start | bytes 491528 | tf_op jit(solution)/shard_map/ppermute | solution.py:96
  7.0 2.8 %collective-permute-start.2 = (bf16[2,320,128]{2,1,0:T(8,128)(2,1)S(1)}, bf16[2,320,128]{2,1,0:T(8,128)(2,1)S(1)}, u32[]{:S(2)}, u32[]{:S(2)}) collective-permute-start(bf16[2,320,128]{2,1,0:T(8,128)(2,1)S(1)} %get-tuple-element.16), channel_id=1, source_target_pairs={{0,2},{1,10},{2,0},{3,8},{4,6},{5,14},{6,4},{7,12},{8,3},{9,11},{1... | collective-permute-start | bytes 491528 | tf_op jit(solution)/shard_map/ppermute | solution.py:96
  9.8 2.0 %collective-permute-start.3 = (bf16[2,320,128]{2,1,0:T(8,128)(2,1)S(1)}, bf16[2,320,128]{2,1,0:T(8,128)(2,1)S(1)}, u32[]{:S(2)}, u32[]{:S(2)}) collective-permute-start(bf16[2,320,128]{2,1,0:T(8,128)(2,1)S(1)} %get-tuple-element.17), channel_id=1, source_target_pairs={{0,0},{1,8},{2,2},{3,10},{4,4},{5,12},{6,6},{7,14},{8,1},{9,9},{10... | collective-permute-start | bytes 491528 | tf_op jit(solution)/shard_map/ppermute | solution.py:96
  11.8 4.3 %collective-permute-done.refs_0_ = bf16[2,320,128]{2,1,0:T(8,128)(2,1)S(1)} collective-permute-done((bf16[2,320,128]{2,1,0:T(8,128)(2,1)S(1)}, bf16[2,320,128]{2,1,0:T(8,128)(2,1)S(1)}, u32[]{:S(2)}, u32[]{:S(2)}) %collective-permute-start) | collective-permute-done | bytes 163872 | tf_op jit(solution)/shard_map/ppermute | solution.py:96
  16.1 5.5 %collective-permute-done.1.refs_1_ = bf16[2,320,128]{2,1,0:T(8,128)(2,1)S(1)} collective-permute-done((bf16[2,320,128]{2,1,0:T(8,128)(2,1)S(1)}, bf16[2,320,128]{2,1,0:T(8,128)(2,1)S(1)}, u32[]{:S(2)}, u32[]{:S(2)}) %collective-permute-start.1) | collective-permute-done | bytes 163872 | tf_op jit(solution)/shard_map/ppermute | solution.py:96
  21.7 0.4 collective-permute-done.4.refs_7_
  22.0 1.5 %collective-permute-start.7 = (bf16[336,1280]{1,0:T(8,128)(2,1)S(1)}, bf16[336,1280]{1,0:T(8,128)(2,1)S(1)}, u32[]{:S(2)}, u32[]{:S(2)}) collective-permute-start(bf16[336,1280]{1,0:T(8,128)(2,1)S(1)} %collective-permute-done.4.refs_7_), channel_id=1, source_target_pairs={{0,8},{1,9},{2,10},{3,11},{4,12},{5,13},{6,14},{7,15},{8,0},{9,1},... | collective-permute-start | bytes 2580488 | tf_op jit(solution)/shard_map/ppermute | solution.py:96
  23.6 2.5 %collective-permute-done.5.refs_4_ = bf16[4,320,128]{2,1,0:T(8,128)(2,1)S(1)} collective-permute-done((bf16[4,320,128]{2,1,0:T(8,128)(2,1)S(1)}, bf16[4,320,128]{2,1,0:T(8,128)(2,1)S(1)}, u32[]{:S(2)}, u32[]{:S(2)}) %collective-permute-start.5) | collective-permute-done | bytes 327712 | tf_op jit(solution)/shard_map/ppermute | solution.py:96
  26.1 6.5 %sections.1 = (bf16[4,320,128]{2,1,0:T(8,128)(2,1)S(1)}, bf16[4,320,128]{2,1,0:T(8,128)(2,1)S(1)}) custom-call(bf16[2,320,128]{2,1,0:T(8,128)(2,1)S(1)} %collective-permute-done.refs_0_, bf16[2,320,128]{2,1,0:T(8,128)(2,1)S(1)} %collective-permute-done.1.refs_1_, bf16[2,320,128]{2,1,0:T(8,128)(2,1)S(1)} %collective-permute-done.2.refs_2_, ...), custom_call_target="tpu_custom_call" | custom-call | flops 3774873600 | bytes 4194304 | tf_op jit(solution)/shard_map/sections/pallas_call | solution.py:336
  32.6 0.2 collective-permute-start.8
  32.9 1.3 %collective-permute-start.14 = (bf16[1,320,128]{2,1,0:T(8,128)(2,1)S(1)}, bf16[1,320,128]{2,1,0:T(8,128)(2,1)S(1)}, u32[]{:S(2)}, u32[]{:S(2)}) collective-permute-start(bf16[1,320,128]{2,1,0:T(8,128)(2,1)S(1)} %get-tuple-element.23), channel_id=1, source_target_pairs={{0,4},{1,12},{2,6},{3,14},{4,0},{5,8},{6,2},{7,10},{8,5},{9,13},{1... | collective-permute-start | bytes 245768 | tf_op jit(solution)/shard_map/ppermute | solution.py:96
  34.1 0.2 collective-permute-done.8
  34.4 3.2 %collective-permute-start.9 = (bf16[2,320,128]{2,1,0:T(8,128)(2,1)S(1)}, bf16[2,320,128]{2,1,0:T(8,128)(2,1)S(1)}, u32[]{:S(2)}, u32[]{:S(2)}) collective-permute-start(bf16[2,320,128]{2,1,0:T(8,128)(2,1)S(1)} %pad_maximum_fusion), channel_id=1, source_target_pairs={{0,0},{1,8},{2,2},{3,10},{4,4},{5,12},{6,6},{7,14},{8,1},{9,9},{10... | collective-permute-start | bytes 491528 | tf_op jit(solution)/shard_map/ppermute | solution.py:96
  37.6 1.6 %collective-permute-start.10 = (bf16[2,320,128]{2,1,0:T(8,128)(2,1)S(1)}, bf16[2,320,128]{2,1,0:T(8,128)(2,1)S(1)}, u32[]{:S(2)}, u32[]{:S(2)}) collective-permute-start(bf16[2,320,128]{2,1,0:T(8,128)(2,1)S(1)} %pad_maximum_fusion.1), channel_id=1, source_target_pairs={{0,2},{1,10},{2,0},{3,8},{4,6},{5,14},{6,4},{7,12},{8,3},{9,11},{1... | collective-permute-start | bytes 491528 | tf_op jit(solution)/shard_map/ppermute | solution.py:96
  39.1 1.2 %collective-permute-start.13 = (bf16[1,320,128]{2,1,0:T(8,128)(2,1)S(1)}, bf16[1,320,128]{2,1,0:T(8,128)(2,1)S(1)}, u32[]{:S(2)}, u32[]{:S(2)}) collective-permute-start(bf16[1,320,128]{2,1,0:T(8,128)(2,1)S(1)} %get-tuple-element.24), channel_id=1, source_target_pairs={{0,6},{1,14},{2,4},{3,12},{4,2},{5,10},{6,0},{7,8},{8,7},{9,15},{1... | collective-permute-start | bytes 245768 | tf_op jit(solution)/shard_map/ppermute | solution.py:96
  40.3 2.3 %collective-permute-start.12 = (bf16[1,320,128]{2,1,0:T(8,128)(2,1)S(1)}, bf16[1,320,128]{2,1,0:T(8,128)(2,1)S(1)}, u32[]{:S(2)}, u32[]{:S(2)}) collective-permute-start(bf16[1,320,128]{2,1,0:T(8,128)(2,1)S(1)} %get-tuple-element.27), channel_id=1, source_target_pairs={{0,4},{1,12},{2,6},{3,14},{4,0},{5,8},{6,2},{7,10},{8,5},{9,13},{1... | collective-permute-start | bytes 245768 | tf_op jit(solution)/shard_map/ppermute | solution.py:96
  42.6 2.3 %collective-permute-start.11 = (bf16[1,320,128]{2,1,0:T(8,128)(2,1)S(1)}, bf16[1,320,128]{2,1,0:T(8,128)(2,1)S(1)}, u32[]{:S(2)}, u32[]{:S(2)}) collective-permute-start(bf16[1,320,128]{2,1,0:T(8,128)(2,1)S(1)} %get-tuple-element.28), channel_id=1, source_target_pairs={{0,6},{1,14},{2,4},{3,12},{4,2},{5,10},{6,0},{7,8},{8,7},{9,15},{1... | collective-permute-start | bytes 245768 | tf_op jit(solution)/shard_map/ppermute | solution.py:96
  44.9 3.5 %collective-permute-done.13.refs_4_ = bf16[1,320,128]{2,1,0:T(8,128)(2,1)S(1)} collective-permute-done((bf16[1,320,128]{2,1,0:T(8,128)(2,1)S(1)}, bf16[1,320,128]{2,1,0:T(8,128)(2,1)S(1)}, u32[]{:S(2)}, u32[]{:S(2)}) %collective-permute-start.13) | collective-permute-done | bytes 81952 | tf_op jit(solution)/shard_map/ppermute | solution.py:96
  48.4 0.6 %collective-permute-done.12.refs_3_ = bf16[1,320,128]{2,1,0:T(8,128)(2,1)S(1)} collective-permute-done((bf16[1,320,128]{2,1,0:T(8,128)(2,1)S(1)}, bf16[1,320,128]{2,1,0:T(8,128)(2,1)S(1)}, u32[]{:S(2)}, u32[]{:S(2)}) %collective-permute-start.12) | collective-permute-done | bytes 81952 | tf_op jit(solution)/shard_map/ppermute | solution.py:96
  49.0 2.2 %collective-permute-done.11.refs_2_ = bf16[1,320,128]{2,1,0:T(8,128)(2,1)S(1)} collective-permute-done((bf16[1,320,128]{2,1,0:T(8,128)(2,1)S(1)}, bf16[1,320,128]{2,1,0:T(8,128)(2,1)S(1)}, u32[]{:S(2)}, u32[]{:S(2)}) %collective-permute-start.11) | collective-permute-done | bytes 81952 | tf_op jit(solution)/shard_map/ppermute | solution.py:96
  51.3 0.9 %join.1 = bf16[320,1024]{1,0:T(8,128)(2,1)} custom-call(bf16[2,320,128]{2,1,0:T(8,128)(2,1)S(1)} %collective-permute-done.9.refs_0_, bf16[2,320,128]{2,1,0:T(8,128)(2,1)S(1)} %collective-permute-done.10.refs_1_, bf16[1,320,128]{2,1,0:T(8,128)(2,1)S(1)} %collective-permute-done.11.refs_2_, bf16[1,320,128]{2,1,0:T(8,128)(2,1)S(1)} %collective-permute-done.12.refs_3_, ...), custom_call_target="tpu_custom_call" | custom-call | tf_op jit(solution)/shard_map/join/pallas_call | solution.py:196
  (16 shorter events, 0.1 us)
Async XLA Ops:
  2.0 20.1 %collective-permute-start.4 = (bf16[336,1280]{1,0:T(8,128)(2,1)S(1)}, bf16[336,1280]{1,0:T(8,128)(2,1)S(1)}, u32[]{:S(2)}, u32[]{:S(2)}) collective-permute-start(bf16[336,1280]{1,0:T(8,128)(2,1)S(1)} %get-tuple-element.18.refs_5_), channel_id=1, source_target_pairs={{0,16},{1,17},{2,18},{3,19},{4,20},{5,21},{6,22},{7,23},{8,24},{9,... | collective-permute-start | bytes 2580488 | tf_op jit(solution)/shard_map/ppermute | solution.py:96
  3.3 12.8 %collective-permute-start = (bf16[2,320,128]{2,1,0:T(8,128)(2,1)S(1)}, bf16[2,320,128]{2,1,0:T(8,128)(2,1)S(1)}, u32[]{:S(2)}, u32[]{:S(2)}) collective-permute-start(bf16[2,320,128]{2,1,0:T(8,128)(2,1)S(1)} %get-tuple-element.14), channel_id=1, source_target_pairs={{0,4},{1,12},{2,6},{3,14},{4,0},{5,8},{6,2},{7,10},{8,5},{9,13},{1... | collective-permute-start | bytes 491528 | tf_op jit(solution)/shard_map/ppermute | solution.py:96
  5.1 16.5 %collective-permute-start.1 = (bf16[2,320,128]{2,1,0:T(8,128)(2,1)S(1)}, bf16[2,320,128]{2,1,0:T(8,128)(2,1)S(1)}, u32[]{:S(2)}, u32[]{:S(2)}) collective-permute-start(bf16[2,320,128]{2,1,0:T(8,128)(2,1)S(1)} %get-tuple-element.15), channel_id=1, source_target_pairs={{0,6},{1,14},{2,4},{3,12},{4,2},{5,10},{6,0},{7,8},{8,7},{9,15},{1... | collective-permute-start | bytes 491528 | tf_op jit(solution)/shard_map/ppermute | solution.py:96
  7.0 14.7 %collective-permute-start.2 = (bf16[2,320,128]{2,1,0:T(8,128)(2,1)S(1)}, bf16[2,320,128]{2,1,0:T(8,128)(2,1)S(1)}, u32[]{:S(2)}, u32[]{:S(2)}) collective-permute-start(bf16[2,320,128]{2,1,0:T(8,128)(2,1)S(1)} %get-tuple-element.16), channel_id=1, source_target_pairs={{0,2},{1,10},{2,0},{3,8},{4,6},{5,14},{6,4},{7,12},{8,3},{9,11},{1... | collective-permute-start | bytes 491528 | tf_op jit(solution)/shard_map/ppermute | solution.py:96
  9.8 16.3 %copy-start = (f32[4,320]{1,0:T(4,128)S(1)}, f32[4,320]{1,0:T(4,128)}, u32[]{:S(2)}) copy-start(f32[4,320]{1,0:T(4,128)} %refs_10_.1) | copy-start | bytes 15364
  9.8 11.8 %collective-permute-start.3 = (bf16[2,320,128]{2,1,0:T(8,128)(2,1)S(1)}, bf16[2,320,128]{2,1,0:T(8,128)(2,1)S(1)}, u32[]{:S(2)}, u32[]{:S(2)}) collective-permute-start(bf16[2,320,128]{2,1,0:T(8,128)(2,1)S(1)} %get-tuple-element.17), channel_id=1, source_target_pairs={{0,0},{1,8},{2,2},{3,10},{4,4},{5,12},{6,6},{7,14},{8,1},{9,9},{10... | collective-permute-start | bytes 491528 | tf_op jit(solution)/shard_map/ppermute | solution.py:96
  16.1 7.5 %collective-permute-start.6 = (bf16[336,1280]{1,0:T(8,128)(2,1)S(1)}, bf16[336,1280]{1,0:T(8,128)(2,1)}, u32[]{:S(2)}, u32[]{:S(2)}) collective-permute-start(bf16[336,1280]{1,0:T(8,128)(2,1)S(1)} %get-tuple-element.18.refs_5_), channel_id=1, source_target_pairs={{0,8},{1,9},{2,10},{3,11},{4,12},{5,13},{6,14},{7,15},{8,0},{9,1},... | collective-permute-start | bytes 2580488 | tf_op jit(solution)/shard_map/ppermute | solution.py:96
  22.0 4.0 %collective-permute-start.7 = (bf16[336,1280]{1,0:T(8,128)(2,1)S(1)}, bf16[336,1280]{1,0:T(8,128)(2,1)S(1)}, u32[]{:S(2)}, u32[]{:S(2)}) collective-permute-start(bf16[336,1280]{1,0:T(8,128)(2,1)S(1)} %collective-permute-done.4.refs_7_), channel_id=1, source_target_pairs={{0,8},{1,9},{2,10},{3,11},{4,12},{5,13},{6,14},{7,15},{8,0},{9,1},... | collective-permute-start | bytes 2580488 | tf_op jit(solution)/shard_map/ppermute | solution.py:96
  23.6 2.5 %collective-permute-start.5 = (bf16[4,320,128]{2,1,0:T(8,128)(2,1)S(1)}, bf16[4,320,128]{2,1,0:T(8,128)(2,1)S(1)}, u32[]{:S(2)}, u32[]{:S(2)}) collective-permute-start(bf16[4,320,128]{2,1,0:T(8,128)(2,1)S(1)} %pick.1), channel_id=1, source_target_pairs={{0,8},{1,9},{2,10},{3,11},{4,12},{5,13},{6,14},{7,15},{8,0},{9,1},... | collective-permute-start | bytes 983048 | tf_op jit(solution)/shard_map/ppermute | solution.py:96
  32.6 1.7 %collective-permute-start.8 = (bf16[4,320,128]{2,1,0:T(8,128)(2,1)S(1)}, bf16[4,320,128]{2,1,0:T(8,128)(2,1)S(1)}, u32[]{:S(2)}, u32[]{:S(2)}) collective-permute-start(bf16[4,320,128]{2,1,0:T(8,128)(2,1)S(1)} %get-tuple-element.22), channel_id=1, source_target_pairs={{0,8},{1,9},{2,10},{3,11},{4,12},{5,13},{6,14},{7,15},{8,0},{9,1},... | collective-permute-start | bytes 983048 | tf_op jit(solution)/shard_map/ppermute | solution.py:96
  32.9 9.7 %collective-permute-start.14 = (bf16[1,320,128]{2,1,0:T(8,128)(2,1)S(1)}, bf16[1,320,128]{2,1,0:T(8,128)(2,1)S(1)}, u32[]{:S(2)}, u32[]{:S(2)}) collective-permute-start(bf16[1,320,128]{2,1,0:T(8,128)(2,1)S(1)} %get-tuple-element.23), channel_id=1, source_target_pairs={{0,4},{1,12},{2,6},{3,14},{4,0},{5,8},{6,2},{7,10},{8,5},{9,13},{1... | collective-permute-start | bytes 245768 | tf_op jit(solution)/shard_map/ppermute | solution.py:96
  34.4 16.9 %collective-permute-start.9 = (bf16[2,320,128]{2,1,0:T(8,128)(2,1)S(1)}, bf16[2,320,128]{2,1,0:T(8,128)(2,1)S(1)}, u32[]{:S(2)}, u32[]{:S(2)}) collective-permute-start(bf16[2,320,128]{2,1,0:T(8,128)(2,1)S(1)} %pad_maximum_fusion), channel_id=1, source_target_pairs={{0,0},{1,8},{2,2},{3,10},{4,4},{5,12},{6,6},{7,14},{8,1},{9,9},{10... | collective-permute-start | bytes 491528 | tf_op jit(solution)/shard_map/ppermute | solution.py:96
  37.6 13.7 %collective-permute-start.10 = (bf16[2,320,128]{2,1,0:T(8,128)(2,1)S(1)}, bf16[2,320,128]{2,1,0:T(8,128)(2,1)S(1)}, u32[]{:S(2)}, u32[]{:S(2)}) collective-permute-start(bf16[2,320,128]{2,1,0:T(8,128)(2,1)S(1)} %pad_maximum_fusion.1), channel_id=1, source_target_pairs={{0,2},{1,10},{2,0},{3,8},{4,6},{5,14},{6,4},{7,12},{8,3},{9,11},{1... | collective-permute-start | bytes 491528 | tf_op jit(solution)/shard_map/ppermute | solution.py:96
  39.1 9.3 %collective-permute-start.13 = (bf16[1,320,128]{2,1,0:T(8,128)(2,1)S(1)}, bf16[1,320,128]{2,1,0:T(8,128)(2,1)S(1)}, u32[]{:S(2)}, u32[]{:S(2)}) collective-permute-start(bf16[1,320,128]{2,1,0:T(8,128)(2,1)S(1)} %get-tuple-element.24), channel_id=1, source_target_pairs={{0,6},{1,14},{2,4},{3,12},{4,2},{5,10},{6,0},{7,8},{8,7},{9,15},{1... | collective-permute-start | bytes 245768 | tf_op jit(solution)/shard_map/ppermute | solution.py:96
  40.3 8.7 %collective-permute-start.12 = (bf16[1,320,128]{2,1,0:T(8,128)(2,1)S(1)}, bf16[1,320,128]{2,1,0:T(8,128)(2,1)S(1)}, u32[]{:S(2)}, u32[]{:S(2)}) collective-permute-start(bf16[1,320,128]{2,1,0:T(8,128)(2,1)S(1)} %get-tuple-element.27), channel_id=1, source_target_pairs={{0,4},{1,12},{2,6},{3,14},{4,0},{5,8},{6,2},{7,10},{8,5},{9,13},{1... | collective-permute-start | bytes 245768 | tf_op jit(solution)/shard_map/ppermute | solution.py:96
  42.6 8.7 %collective-permute-start.11 = (bf16[1,320,128]{2,1,0:T(8,128)(2,1)S(1)}, bf16[1,320,128]{2,1,0:T(8,128)(2,1)S(1)}, u32[]{:S(2)}, u32[]{:S(2)}) collective-permute-start(bf16[1,320,128]{2,1,0:T(8,128)(2,1)S(1)} %get-tuple-element.28), channel_id=1, source_target_pairs={{0,6},{1,14},{2,4},{3,12},{4,2},{5,10},{6,0},{7,8},{8,7},{9,15},{1... | collective-permute-start | bytes 245768 | tf_op jit(solution)/shard_map/ppermute | solution.py:96

commit v10 on v9

--- a/solution.py
+++ b/solution.py
@@ -74,7 +74,7 @@
 
 
 FILM_ROWS = 16
-JOIN_STEPS = 4
+JOIN_STEPS = 2
 
 
 def place():

time: 53.2 us -> 53.3 us (level)
  no operation moved by 1% of the time
where the time goes in v10:
time: 53.3 us; the launch traced here: 52.2 us
  starting transfers between devices  23.4 us (44%)
  waiting for transfers between devices  19.2 us (36%)
  Pallas kernels  9.46 us (18%)
    ppermute x15, starting transfers between devices, move(): return lax.ppermute(array, ('segment', 'frame'), pairs)  23.4 us
    ppermute x15, waiting for transfers between devices, move(): return lax.ppermute(array, ('segment', 'frame'), pairs)  19.2 us
    pallas_call x1, Pallas kernels, run_sections(): pl.pallas_call(functools.partial(sections_kernel, dests, levels, width, l...  6.52 us
    pallas_call x1, Pallas kernels, pack_and_cut(): pl.pallas_call(functools.partial(pack_kernel, levels), out_shape=[pltpu.V...  1.98 us
  transfers between devices with their start and end apart: 15, of which 8 were waited for; matrix products, arithmetic and copies ran while one was open for 0% of the time, Pallas kernels for 0%

profile of v10, /device:TPU:17, one launch (start us, length us, event | category | flops | bytes accessed | tf_op | source)
XLA Modules:
  0.0 52.2 jit_solution(957419511446613657)
XLA Ops:
  0.0 2.0 %pack.1 = (bf16[2,320,128]{2,1,0:T(8,128)(2,1)S(1)}, bf16[2,320,128]{2,1,0:T(8,128)(2,1)S(1)}, bf16[2,320,128]{2,1,0:T(8,128)(2,1)S(1)}, bf16[2,320,128]{2,1,0:T(8,128)(2,1)S(1)}, bf16[336,1280]{1,0:T(8,128)(2,1)S(1)}) custom-call(s32[4]{0:T(128)} %times_ref.1, bf16[320,1024]{1,0:T(8,128)(2,1)} %bitcast.6, bf16[3,320,320]{2,1,0:T(8,128)(2,1)} %bitcast.5, ...), custom_call_target="tpu_custom_call" | custom-call | tf_op jit(solution)/shard_map/pack/pallas_call | solution.py:147
  2.0 1.3 %collective-permute-start.4 = (bf16[336,1280]{1,0:T(8,128)(2,1)S(1)}, bf16[336,1280]{1,0:T(8,128)(2,1)S(1)}, u32[]{:S(2)}, u32[]{:S(2)}) collective-permute-start(bf16[336,1280]{1,0:T(8,128)(2,1)S(1)} %get-tuple-element.18.refs_5_), channel_id=1, source_target_pairs={{0,16},{1,17},{2,18},{3,19},{4,20},{5,21},{6,22},{7,23},{8,24},{9,... | collective-permute-start | bytes 2580488 | tf_op jit(solution)/shard_map/ppermute | solution.py:96
  3.3 1.8 %collective-permute-start = (bf16[2,320,128]{2,1,0:T(8,128)(2,1)S(1)}, bf16[2,320,128]{2,1,0:T(8,128)(2,1)S(1)}, u32[]{:S(2)}, u32[]{:S(2)}) collective-permute-start(bf16[2,320,128]{2,1,0:T(8,128)(2,1)S(1)} %get-tuple-element.14), channel_id=1, source_target_pairs={{0,4},{1,12},{2,6},{3,14},{4,0},{5,8},{6,2},{7,10},{8,5},{9,13},{1... | collective-permute-start | bytes 491528 | tf_op jit(solution)/shard_map/ppermute | solution.py:96
  5.1 1.8 %collective-permute-start.1 = (bf16[2,320,128]{2,1,0:T(8,128)(2,1)S(1)}, bf16[2,320,128]{2,1,0:T(8,128)(2,1)S(1)}, u32[]{:S(2)}, u32[]{:S(2)}) collective-permute-start(bf16[2,320,128]{2,1,0:T(8,128)(2,1)S(1)} %get-tuple-element.15), channel_id=1, source_target_pairs={{0,6},{1,14},{2,4},{3,12},{4,2},{5,10},{6,0},{7,8},{8,7},{9,15},{1... | collective-permute-start | bytes 491528 | tf_op jit(solution)/shard_map/ppermute | solution.py:96
  7.0 2.8 %collective-permute-start.2 = (bf16[2,320,128]{2,1,0:T(8,128)(2,1)S(1)}, bf16[2,320,128]{2,1,0:T(8,128)(2,1)S(1)}, u32[]{:S(2)}, u32[]{:S(2)}) collective-permute-start(bf16[2,320,128]{2,1,0:T(8,128)(2,1)S(1)} %get-tuple-element.16), channel_id=1, source_target_pairs={{0,2},{1,10},{2,0},{3,8},{4,6},{5,14},{6,4},{7,12},{8,3},{9,11},{1... | collective-permute-start | bytes 491528 | tf_op jit(solution)/shard_map/ppermute | solution.py:96
  9.8 2.0 %collective-permute-start.3 = (bf16[2,320,128]{2,1,0:T(8,128)(2,1)S(1)}, bf16[2,320,128]{2,1,0:T(8,128)(2,1)S(1)}, u32[]{:S(2)}, u32[]{:S(2)}) collective-permute-start(bf16[2,320,128]{2,1,0:T(8,128)(2,1)S(1)} %get-tuple-element.17), channel_id=1, source_target_pairs={{0,0},{1,8},{2,2},{3,10},{4,4},{5,12},{6,6},{7,14},{8,1},{9,9},{10... | collective-permute-start | bytes 491528 | tf_op jit(solution)/shard_map/ppermute | solution.py:96
  11.8 4.3 %collective-permute-done.refs_0_ = bf16[2,320,128]{2,1,0:T(8,128)(2,1)S(1)} collective-permute-done((bf16[2,320,128]{2,1,0:T(8,128)(2,1)S(1)}, bf16[2,320,128]{2,1,0:T(8,128)(2,1)S(1)}, u32[]{:S(2)}, u32[]{:S(2)}) %collective-permute-start) | collective-permute-done | bytes 163872 | tf_op jit(solution)/shard_map/ppermute | solution.py:96
  16.1 5.5 %collective-permute-done.1.refs_1_ = bf16[2,320,128]{2,1,0:T(8,128)(2,1)S(1)} collective-permute-done((bf16[2,320,128]{2,1,0:T(8,128)(2,1)S(1)}, bf16[2,320,128]{2,1,0:T(8,128)(2,1)S(1)}, u32[]{:S(2)}, u32[]{:S(2)}) %collective-permute-start.1) | collective-permute-done | bytes 163872 | tf_op jit(solution)/shard_map/ppermute | solution.py:96
  21.7 0.4 collective-permute-done.4.refs_7_
  22.0 1.5 %collective-permute-start.7 = (bf16[336,1280]{1,0:T(8,128)(2,1)S(1)}, bf16[336,1280]{1,0:T(8,128)(2,1)S(1)}, u32[]{:S(2)}, u32[]{:S(2)}) collective-permute-start(bf16[336,1280]{1,0:T(8,128)(2,1)S(1)} %collective-permute-done.4.refs_7_), channel_id=1, source_target_pairs={{0,8},{1,9},{2,10},{3,11},{4,12},{5,13},{6,14},{7,15},{8,0},{9,1},... | collective-permute-start | bytes 2580488 | tf_op jit(solution)/shard_map/ppermute | solution.py:96
  23.6 2.5 %collective-permute-done.5.refs_4_ = bf16[4,320,128]{2,1,0:T(8,128)(2,1)S(1)} collective-permute-done((bf16[4,320,128]{2,1,0:T(8,128)(2,1)S(1)}, bf16[4,320,128]{2,1,0:T(8,128)(2,1)S(1)}, u32[]{:S(2)}, u32[]{:S(2)}) %collective-permute-start.5) | collective-permute-done | bytes 327712 | tf_op jit(solution)/shard_map/ppermute | solution.py:96
  26.1 6.5 %sections.1 = (bf16[4,320,128]{2,1,0:T(8,128)(2,1)S(1)}, bf16[4,320,128]{2,1,0:T(8,128)(2,1)S(1)}) custom-call(bf16[2,320,128]{2,1,0:T(8,128)(2,1)S(1)} %collective-permute-done.refs_0_, bf16[2,320,128]{2,1,0:T(8,128)(2,1)S(1)} %collective-permute-done.1.refs_1_, bf16[2,320,128]{2,1,0:T(8,128)(2,1)S(1)} %collective-permute-done.2.refs_2_, ...), custom_call_target="tpu_custom_call" | custom-call | flops 3774873600 | bytes 4194304 | tf_op jit(solution)/shard_map/sections/pallas_call | solution.py:336
  32.6 0.2 collective-permute-start.8
  32.9 1.3 %collective-permute-start.14 = (bf16[1,320,128]{2,1,0:T(8,128)(2,1)S(1)}, bf16[1,320,128]{2,1,0:T(8,128)(2,1)S(1)}, u32[]{:S(2)}, u32[]{:S(2)}) collective-permute-start(bf16[1,320,128]{2,1,0:T(8,128)(2,1)S(1)} %get-tuple-element.23), channel_id=1, source_target_pairs={{0,4},{1,12},{2,6},{3,14},{4,0},{5,8},{6,2},{7,10},{8,5},{9,13},{1... | collective-permute-start | bytes 245768 | tf_op jit(solution)/shard_map/ppermute | solution.py:96
  34.1 0.2 collective-permute-done.8
  34.4 3.2 %collective-permute-start.9 = (bf16[2,320,128]{2,1,0:T(8,128)(2,1)S(1)}, bf16[2,320,128]{2,1,0:T(8,128)(2,1)S(1)}, u32[]{:S(2)}, u32[]{:S(2)}) collective-permute-start(bf16[2,320,128]{2,1,0:T(8,128)(2,1)S(1)} %pad_maximum_fusion), channel_id=1, source_target_pairs={{0,0},{1,8},{2,2},{3,10},{4,4},{5,12},{6,6},{7,14},{8,1},{9,9},{10... | collective-permute-start | bytes 491528 | tf_op jit(solution)/shard_map/ppermute | solution.py:96
  37.6 1.6 %collective-permute-start.10 = (bf16[2,320,128]{2,1,0:T(8,128)(2,1)S(1)}, bf16[2,320,128]{2,1,0:T(8,128)(2,1)S(1)}, u32[]{:S(2)}, u32[]{:S(2)}) collective-permute-start(bf16[2,320,128]{2,1,0:T(8,128)(2,1)S(1)} %pad_maximum_fusion.1), channel_id=1, source_target_pairs={{0,2},{1,10},{2,0},{3,8},{4,6},{5,14},{6,4},{7,12},{8,3},{9,11},{1... | collective-permute-start | bytes 491528 | tf_op jit(solution)/shard_map/ppermute | solution.py:96
  39.1 1.2 %collective-permute-start.13 = (bf16[1,320,128]{2,1,0:T(8,128)(2,1)S(1)}, bf16[1,320,128]{2,1,0:T(8,128)(2,1)S(1)}, u32[]{:S(2)}, u32[]{:S(2)}) collective-permute-start(bf16[1,320,128]{2,1,0:T(8,128)(2,1)S(1)} %get-tuple-element.24), channel_id=1, source_target_pairs={{0,6},{1,14},{2,4},{3,12},{4,2},{5,10},{6,0},{7,8},{8,7},{9,15},{1... | collective-permute-start | bytes 245768 | tf_op jit(solution)/shard_map/ppermute | solution.py:96
  40.3 2.3 %collective-permute-start.12 = (bf16[1,320,128]{2,1,0:T(8,128)(2,1)S(1)}, bf16[1,320,128]{2,1,0:T(8,128)(2,1)S(1)}, u32[]{:S(2)}, u32[]{:S(2)}) collective-permute-start(bf16[1,320,128]{2,1,0:T(8,128)(2,1)S(1)} %get-tuple-element.27), channel_id=1, source_target_pairs={{0,4},{1,12},{2,6},{3,14},{4,0},{5,8},{6,2},{7,10},{8,5},{9,13},{1... | collective-permute-start | bytes 245768 | tf_op jit(solution)/shard_map/ppermute | solution.py:96
  42.6 2.3 %collective-permute-start.11 = (bf16[1,320,128]{2,1,0:T(8,128)(2,1)S(1)}, bf16[1,320,128]{2,1,0:T(8,128)(2,1)S(1)}, u32[]{:S(2)}, u32[]{:S(2)}) collective-permute-start(bf16[1,320,128]{2,1,0:T(8,128)(2,1)S(1)} %get-tuple-element.28), channel_id=1, source_target_pairs={{0,6},{1,14},{2,4},{3,12},{4,2},{5,10},{6,0},{7,8},{8,7},{9,15},{1... | collective-permute-start | bytes 245768 | tf_op jit(solution)/shard_map/ppermute | solution.py:96
  44.9 3.5 %collective-permute-done.13.refs_4_ = bf16[1,320,128]{2,1,0:T(8,128)(2,1)S(1)} collective-permute-done((bf16[1,320,128]{2,1,0:T(8,128)(2,1)S(1)}, bf16[1,320,128]{2,1,0:T(8,128)(2,1)S(1)}, u32[]{:S(2)}, u32[]{:S(2)}) %collective-permute-start.13) | collective-permute-done | bytes 81952 | tf_op jit(solution)/shard_map/ppermute | solution.py:96
  48.4 0.6 %collective-permute-done.12.refs_3_ = bf16[1,320,128]{2,1,0:T(8,128)(2,1)S(1)} collective-permute-done((bf16[1,320,128]{2,1,0:T(8,128)(2,1)S(1)}, bf16[1,320,128]{2,1,0:T(8,128)(2,1)S(1)}, u32[]{:S(2)}, u32[]{:S(2)}) %collective-permute-start.12) | collective-permute-done | bytes 81952 | tf_op jit(solution)/shard_map/ppermute | solution.py:96
  49.0 2.2 %collective-permute-done.11.refs_2_ = bf16[1,320,128]{2,1,0:T(8,128)(2,1)S(1)} collective-permute-done((bf16[1,320,128]{2,1,0:T(8,128)(2,1)S(1)}, bf16[1,320,128]{2,1,0:T(8,128)(2,1)S(1)}, u32[]{:S(2)}, u32[]{:S(2)}) %collective-permute-start.11) | collective-permute-done | bytes 81952 | tf_op jit(solution)/shard_map/ppermute | solution.py:96
  51.3 0.9 %join.1 = bf16[320,1024]{1,0:T(8,128)(2,1)} custom-call(bf16[2,320,128]{2,1,0:T(8,128)(2,1)S(1)} %collective-permute-done.9.refs_0_, bf16[2,320,128]{2,1,0:T(8,128)(2,1)S(1)} %collective-permute-done.10.refs_1_, bf16[1,320,128]{2,1,0:T(8,128)(2,1)S(1)} %collective-permute-done.11.refs_2_, bf16[1,320,128]{2,1,0:T(8,128)(2,1)S(1)} %collective-permute-done.12.refs_3_, ...), custom_call_target="tpu_custom_call" | custom-call | tf_op jit(solution)/shard_map/join/pallas_call | solution.py:196
  (16 shorter events, 0.1 us)
Async XLA Ops:
  2.0 20.1 %collective-permute-start.4 = (bf16[336,1280]{1,0:T(8,128)(2,1)S(1)}, bf16[336,1280]{1,0:T(8,128)(2,1)S(1)}, u32[]{:S(2)}, u32[]{:S(2)}) collective-permute-start(bf16[336,1280]{1,0:T(8,128)(2,1)S(1)} %get-tuple-element.18.refs_5_), channel_id=1, source_target_pairs={{0,16},{1,17},{2,18},{3,19},{4,20},{5,21},{6,22},{7,23},{8,24},{9,... | collective-permute-start | bytes 2580488 | tf_op jit(solution)/shard_map/ppermute | solution.py:96
  3.3 12.8 %collective-permute-start = (bf16[2,320,128]{2,1,0:T(8,128)(2,1)S(1)}, bf16[2,320,128]{2,1,0:T(8,128)(2,1)S(1)}, u32[]{:S(2)}, u32[]{:S(2)}) collective-permute-start(bf16[2,320,128]{2,1,0:T(8,128)(2,1)S(1)} %get-tuple-element.14), channel_id=1, source_target_pairs={{0,4},{1,12},{2,6},{3,14},{4,0},{5,8},{6,2},{7,10},{8,5},{9,13},{1... | collective-permute-start | bytes 491528 | tf_op jit(solution)/shard_map/ppermute | solution.py:96
  5.1 16.5 %collective-permute-start.1 = (bf16[2,320,128]{2,1,0:T(8,128)(2,1)S(1)}, bf16[2,320,128]{2,1,0:T(8,128)(2,1)S(1)}, u32[]{:S(2)}, u32[]{:S(2)}) collective-permute-start(bf16[2,320,128]{2,1,0:T(8,128)(2,1)S(1)} %get-tuple-element.15), channel_id=1, source_target_pairs={{0,6},{1,14},{2,4},{3,12},{4,2},{5,10},{6,0},{7,8},{8,7},{9,15},{1... | collective-permute-start | bytes 491528 | tf_op jit(solution)/shard_map/ppermute | solution.py:96
  7.0 14.7 %collective-permute-start.2 = (bf16[2,320,128]{2,1,0:T(8,128)(2,1)S(1)}, bf16[2,320,128]{2,1,0:T(8,128)(2,1)S(1)}, u32[]{:S(2)}, u32[]{:S(2)}) collective-permute-start(bf16[2,320,128]{2,1,0:T(8,128)(2,1)S(1)} %get-tuple-element.16), channel_id=1, source_target_pairs={{0,2},{1,10},{2,0},{3,8},{4,6},{5,14},{6,4},{7,12},{8,3},{9,11},{1... | collective-permute-start | bytes 491528 | tf_op jit(solution)/shard_map/ppermute | solution.py:96
  9.8 16.3 %copy-start = (f32[4,320]{1,0:T(4,128)S(1)}, f32[4,320]{1,0:T(4,128)}, u32[]{:S(2)}) copy-start(f32[4,320]{1,0:T(4,128)} %refs_10_.1) | copy-start | bytes 15364
  9.8 11.8 %collective-permute-start.3 = (bf16[2,320,128]{2,1,0:T(8,128)(2,1)S(1)}, bf16[2,320,128]{2,1,0:T(8,128)(2,1)S(1)}, u32[]{:S(2)}, u32[]{:S(2)}) collective-permute-start(bf16[2,320,128]{2,1,0:T(8,128)(2,1)S(1)} %get-tuple-element.17), channel_id=1, source_target_pairs={{0,0},{1,8},{2,2},{3,10},{4,4},{5,12},{6,6},{7,14},{8,1},{9,9},{10... | collective-permute-start | bytes 491528 | tf_op jit(solution)/shard_map/ppermute | solution.py:96
  16.1 7.5 %collective-permute-start.6 = (bf16[336,1280]{1,0:T(8,128)(2,1)S(1)}, bf16[336,1280]{1,0:T(8,128)(2,1)}, u32[]{:S(2)}, u32[]{:S(2)}) collective-permute-start(bf16[336,1280]{1,0:T(8,128)(2,1)S(1)} %get-tuple-element.18.refs_5_), channel_id=1, source_target_pairs={{0,8},{1,9},{2,10},{3,11},{4,12},{5,13},{6,14},{7,15},{8,0},{9,1},... | collective-permute-start | bytes 2580488 | tf_op jit(solution)/shard_map/ppermute | solution.py:96
  22.0 4.0 %collective-permute-start.7 = (bf16[336,1280]{1,0:T(8,128)(2,1)S(1)}, bf16[336,1280]{1,0:T(8,128)(2,1)S(1)}, u32[]{:S(2)}, u32[]{:S(2)}) collective-permute-start(bf16[336,1280]{1,0:T(8,128)(2,1)S(1)} %collective-permute-done.4.refs_7_), channel_id=1, source_target_pairs={{0,8},{1,9},{2,10},{3,11},{4,12},{5,13},{6,14},{7,15},{8,0},{9,1},... | collective-permute-start | bytes 2580488 | tf_op jit(solution)/shard_map/ppermute | solution.py:96
  23.6 2.5 %collective-permute-start.5 = (bf16[4,320,128]{2,1,0:T(8,128)(2,1)S(1)}, bf16[4,320,128]{2,1,0:T(8,128)(2,1)S(1)}, u32[]{:S(2)}, u32[]{:S(2)}) collective-permute-start(bf16[4,320,128]{2,1,0:T(8,128)(2,1)S(1)} %pick.1), channel_id=1, source_target_pairs={{0,8},{1,9},{2,10},{3,11},{4,12},{5,13},{6,14},{7,15},{8,0},{9,1},... | collective-permute-start | bytes 983048 | tf_op jit(solution)/shard_map/ppermute | solution.py:96
  32.6 1.7 %collective-permute-start.8 = (bf16[4,320,128]{2,1,0:T(8,128)(2,1)S(1)}, bf16[4,320,128]{2,1,0:T(8,128)(2,1)S(1)}, u32[]{:S(2)}, u32[]{:S(2)}) collective-permute-start(bf16[4,320,128]{2,1,0:T(8,128)(2,1)S(1)} %get-tuple-element.22), channel_id=1, source_target_pairs={{0,8},{1,9},{2,10},{3,11},{4,12},{5,13},{6,14},{7,15},{8,0},{9,1},... | collective-permute-start | bytes 983048 | tf_op jit(solution)/shard_map/ppermute | solution.py:96
  32.9 9.7 %collective-permute-start.14 = (bf16[1,320,128]{2,1,0:T(8,128)(2,1)S(1)}, bf16[1,320,128]{2,1,0:T(8,128)(2,1)S(1)}, u32[]{:S(2)}, u32[]{:S(2)}) collective-permute-start(bf16[1,320,128]{2,1,0:T(8,128)(2,1)S(1)} %get-tuple-element.23), channel_id=1, source_target_pairs={{0,4},{1,12},{2,6},{3,14},{4,0},{5,8},{6,2},{7,10},{8,5},{9,13},{1... | collective-permute-start | bytes 245768 | tf_op jit(solution)/shard_map/ppermute | solution.py:96
  34.4 16.9 %collective-permute-start.9 = (bf16[2,320,128]{2,1,0:T(8,128)(2,1)S(1)}, bf16[2,320,128]{2,1,0:T(8,128)(2,1)S(1)}, u32[]{:S(2)}, u32[]{:S(2)}) collective-permute-start(bf16[2,320,128]{2,1,0:T(8,128)(2,1)S(1)} %pad_maximum_fusion), channel_id=1, source_target_pairs={{0,0},{1,8},{2,2},{3,10},{4,4},{5,12},{6,6},{7,14},{8,1},{9,9},{10... | collective-permute-start | bytes 491528 | tf_op jit(solution)/shard_map/ppermute | solution.py:96
  37.6 13.7 %collective-permute-start.10 = (bf16[2,320,128]{2,1,0:T(8,128)(2,1)S(1)}, bf16[2,320,128]{2,1,0:T(8,128)(2,1)S(1)}, u32[]{:S(2)}, u32[]{:S(2)}) collective-permute-start(bf16[2,320,128]{2,1,0:T(8,128)(2,1)S(1)} %pad_maximum_fusion.1), channel_id=1, source_target_pairs={{0,2},{1,10},{2,0},{3,8},{4,6},{5,14},{6,4},{7,12},{8,3},{9,11},{1... | collective-permute-start | bytes 491528 | tf_op jit(solution)/shard_map/ppermute | solution.py:96
  39.1 9.3 %collective-permute-start.13 = (bf16[1,320,128]{2,1,0:T(8,128)(2,1)S(1)}, bf16[1,320,128]{2,1,0:T(8,128)(2,1)S(1)}, u32[]{:S(2)}, u32[]{:S(2)}) collective-permute-start(bf16[1,320,128]{2,1,0:T(8,128)(2,1)S(1)} %get-tuple-element.24), channel_id=1, source_target_pairs={{0,6},{1,14},{2,4},{3,12},{4,2},{5,10},{6,0},{7,8},{8,7},{9,15},{1... | collective-permute-start | bytes 245768 | tf_op jit(solution)/shard_map/ppermute | solution.py:96
  40.3 8.7 %collective-permute-start.12 = (bf16[1,320,128]{2,1,0:T(8,128)(2,1)S(1)}, bf16[1,320,128]{2,1,0:T(8,128)(2,1)S(1)}, u32[]{:S(2)}, u32[]{:S(2)}) collective-permute-start(bf16[1,320,128]{2,1,0:T(8,128)(2,1)S(1)} %get-tuple-element.27), channel_id=1, source_target_pairs={{0,4},{1,12},{2,6},{3,14},{4,0},{5,8},{6,2},{7,10},{8,5},{9,13},{1... | collective-permute-start | bytes 245768 | tf_op jit(solution)/shard_map/ppermute | solution.py:96
  42.6 8.7 %collective-permute-start.11 = (bf16[1,320,128]{2,1,0:T(8,128)(2,1)S(1)}, bf16[1,320,128]{2,1,0:T(8,128)(2,1)S(1)}, u32[]{:S(2)}, u32[]{:S(2)}) collective-permute-start(bf16[1,320,128]{2,1,0:T(8,128)(2,1)S(1)} %get-tuple-element.28), channel_id=1, source_target_pairs={{0,6},{1,14},{2,4},{3,12},{4,2},{5,10},{6,0},{7,8},{8,7},{9,15},{1... | collective-permute-start | bytes 245768 | tf_op jit(solution)/shard_map/ppermute | solution.py:96
